TPU v7x, 32 devices: a whole 2x2x4 slice. The times are simulated.
32 devices in a mesh: gx: 8 (over z, x), gy: 4 (over y, core).
Axes of the slice: x: 2, y: 2, z: 4, core: 2. Of those that a mesh axis runs over, the one named last changes fastest.
Arguments:
- velocity_guess: float32 [8, 2, 256, 1024], P(None, None, 'gx', 'gy'), may hold values from -6 to 6
- friction: bfloat16 [8, 256, 1024], P(None, 'gx', 'gy'), may hold values from 0.5 to 4
- thickness: float32 [256, 1024], P('gx', 'gy'), may hold values from 0.5 to 4.5
- surface: float32 [256, 1024], P('gx', 'gy'), may hold values from -4 to 324
- ice_mask: int32 [256, 1024], P('gx', 'gy'), may hold values 0 or 1
- grounded_mask: int32 [256, 1024], P('gx', 'gy'), may hold values 0 or 1
Outputs:
- velocity: float32 [8, 2, 256, 1024], P(None, None, 'gx', 'gy')
All inputs are finite; a program needn't handle non-finite values. No bound on the sum of `ice_mask` or of `grounded_mask` on one device may be relied on, other than what follows from the above.
Results may differ from a plain program's by a relative error of at most 0.0003.
Values sent between devices are 32-bit elements; how exact they have to be, the bound alone decides.
No kernel may reach another device: no remote copies, remote signals or barrier semaphores. Data moves between devices by JAX's collectives and lax.ppermute only.
A program may use at most 64 MiB of HBM per device.

v0:
```python
import jax
import jax.numpy as jnp
from jax import lax
from jax.sharding import PartitionSpec as P

strain_floor = 0.1
water_drag = 0.25
flow_power = 1.0 / 3.0


def padded_2(cells, sides, width):
    for axis, dim in sides:
        count = lax.axis_size(axis)
        ends = count - 1
        head = lax.slice_in_dim(cells, 0, width, axis=dim)
        tail = lax.slice_in_dim(cells, cells.shape[dim] - width, cells.shape[dim], axis=dim)
        cells = jnp.concatenate(
            [
                lax.ppermute(tail, axis, [(i, (i + 1) % count) for i in range(ends)]),
                cells,
                lax.ppermute(head, axis, [((i + 1) % count, i) for i in range(ends)]),
            ],
            axis=dim,
        )
    return cells


def centre_rows(padded):
    return 0.5 * (padded[..., 2:, 1:-1] - padded[..., :-2, 1:-1])


def centre_cols(padded):
    return 0.5 * (padded[..., 1:-1, 2:] - padded[..., 1:-1, :-2])


def strains(padded):
    field_u = padded[:, 0]
    field_v = padded[:, 1]
    return (centre_rows(field_u), centre_cols(field_v), centre_cols(field_u) + centre_rows(field_v))


def stresses(visc, padded):
    ka, kb, kc = strains(padded)
    return (visc * (4.0 * ka + 2.0 * kb), visc * (2.0 * ka + 4.0 * kb), visc * kc)


def divergence(sxx, syy, sxy, field, drag, icef):
    out_u = icef * (drag * field[:, 0] - centre_rows(sxx) - centre_cols(sxy))
    out_v = icef * (drag * field[:, 1] - centre_cols(syy) - centre_rows(sxy))
    return jnp.stack([out_u, out_v], 1)


def extend(field):
    flat = field.reshape((-1,) + field.shape[2:])
    grown = padded_2(flat, (("gx", 1), ("gy", 2)), 1)
    return grown.reshape(field.shape[:2] + grown.shape[1:])


def member_dot(left, right):
    return lax.psum(jnp.sum(left * right, axis=(1, 2, 3)), ("gx", "gy"))


def column(values):
    return values[:, None, None, None]


def per_device(velocity_guess, friction, thickness, surface, ice_mask, grounded_mask):
    members = velocity_guess.shape[0]
    icef = ice_mask.astype(jnp.float32)
    groundf = grounded_mask.astype(jnp.float32)
    drag = icef * (groundf * friction.astype(jnp.float32) + water_drag)
    start = icef * velocity_guess
    stacked = jnp.concatenate([start.reshape((-1,) + start.shape[2:]), surface[None]], 0)
    grown = padded_2(stacked, (("gx", 1), ("gy", 2)), 1)
    start_ext = grown[: 2 * members].reshape((members, 2) + grown.shape[1:])
    start_one = grown[: 2 * members].reshape((members, 2) + grown.shape[1:])
    surf_one = grown[2 * members]
    sa, sb, sc = strains(start_one)
    visc = (
        icef
        * 0.5
        * thickness
        * jnp.power(sa * sa + sb * sb + sa * sb + 0.25 * (sc * sc) + strain_floor, -flow_power)
    )
    visc_ext = padded_2(visc, (("gx", 1), ("gy", 2)), 1)
    near_rows = visc_ext[:, 2:, 1:-1] + visc_ext[:, :-2, 1:-1]
    near_cols = visc_ext[:, 1:-1, 2:] + visc_ext[:, 1:-1, :-2]
    precond = jnp.stack(
        [
            icef * (near_rows + 0.25 * near_cols + drag) + (1.0 - icef),
            icef * (near_cols + 0.25 * near_rows + drag) + (1.0 - icef),
        ],
        1,
    )
    force = jnp.stack(
        [icef * -(thickness * centre_rows(surf_one)), icef * -(thickness * centre_cols(surf_one))],
        0,
    )

    def operate(padded):
        sxx, syy, sxy = stresses(visc, padded)
        joined = jnp.concatenate([sxx, syy, sxy], 0)
        wider = padded_2(joined, (("gx", 1), ("gy", 2)), 1)
        field = padded[:, :, 1:-1, 1:-1]
        return divergence(
            wider[:members], wider[members : 2 * members], wider[2 * members :], field, drag, icef
        )

    velocity = start
    resid = force[None] - operate(start_ext)
    scaled = resid / precond
    direction = scaled
    norm_now = member_dot(resid, scaled)
    for step in range(2):
        image = operate(extend(direction))
        alpha = norm_now / member_dot(direction, image)
        velocity = velocity + column(alpha) * direction
        resid = resid - column(alpha) * image
        if step == 0:
            scaled = resid / precond
            norm_next = member_dot(resid, scaled)
            direction = scaled + column(norm_next / norm_now) * direction
            norm_now = norm_next
    return velocity


def solution(mesh):
    placed = (
        P(None, None, "gx", "gy"),
        P(None, "gx", "gy"),
        P("gx", "gy"),
        P("gx", "gy"),
        P("gx", "gy"),
        P("gx", "gy"),
    )
    return jax.shard_map(
        per_device, mesh=mesh, in_specs=placed, out_specs=P(None, None, "gx", "gy"), check_vma=False
    )
```

profile of v0, /device:TPU:0, one launch (start us, length us, event | category | flops | bytes accessed | tf_op | source)
XLA Modules:
  0.0 279.2 jit_solution(14531693554155521967)
XLA Ops:
  1.9 4.8 %collective-permute-start = (f32[17,1,256]{2,1,0:T(1,128)S(1)}, f32[17,1,256]{2,1,0:T(1,128)S(1)}, u32[]{:S(2)}, u32[]{:S(2)}) collective-permute-start(f32[17,1,256]{2,1,0:T(1,128)S(1)} %get-tuple-element.45), channel_id=1, source_target_pairs={{0,4},{4,8},{8,12},{12,16},{16,20},{20,24},{24,28},{1,5},{5,9},{9,... | collective-permute-start | bytes 52232 | tf_op jit(solution)/shard_map/ppermute | solution.py:19
  8.2 4.2 %collective-permute-done.1 = f32[17,1,256]{2,1,0:T(1,128)S(1)} collective-permute-done((f32[17,1,256]{2,1,0:T(1,128)S(1)}, f32[17,1,256]{2,1,0:T(1,128)S(1)}, u32[]{:S(2)}, u32[]{:S(2)}) %collective-permute-start.1) | collective-permute-done | bytes 17440 | tf_op jit(solution)/shard_map/ppermute | solution.py:21
  15.3 3.9 %collective-permute-done.3 = f32[17,34,1]{2,1,0:T(8,128)S(1)} collective-permute-done((f32[17,34,1]{2,1,0:T(8,128)S(1)}, f32[17,34,1]{2,1,0:T(8,128)S(1)}, u32[]{:S(2)}, u32[]{:S(2)}) %collective-permute-start.3) | collective-permute-done | bytes 2344 | tf_op jit(solution)/shard_map/ppermute | solution.py:21
  23.1 5.0 %collective-permute-start.9 = (f32[8,1,256]{2,1,0:T(1,128)S(1)}, f32[8,1,256]{2,1,0:T(1,128)S(1)}, u32[]{:S(2)}, u32[]{:S(2)}) collective-permute-start(f32[8,1,256]{2,1,0:T(1,128)S(1)} %get-tuple-element.57), channel_id=1, source_target_pairs={{0,4},{4,8},{8,12},{12,16},{16,20},{20,24},{24,28},{1,5},{5,9},{9,... | collective-permute-start | bytes 24584 | tf_op jit(solution)/shard_map/ppermute | solution.py:19
  29.5 5.5 %collective-permute-start.5 = (f32[24,1,256]{2,1,0:T(1,128)S(1)}, f32[24,1,256]{2,1,0:T(1,128)S(1)}, u32[]{:S(2)}, u32[]{:S(2)}) collective-permute-start(f32[24,1,256]{2,1,0:T(1,128)S(1)} %get-tuple-element.38), channel_id=1, source_target_pairs={{0,4},{4,8},{8,12},{12,16},{16,20},{20,24},{24,28},{1,5},{5,9},{9,... | collective-permute-start | bytes 73736 | tf_op jit(solution)/shard_map/ppermute | solution.py:19
  36.6 7.3 %collective-permute-start.11 = (f32[8,34,1]{2,1,0:T(8,128)S(1)}, f32[8,34,1]{2,1,0:T(8,128)S(1)}, u32[]{:S(2)}, u32[]{:S(2)}) collective-permute-start(f32[8,34,1]{2,1,0:T(8,128)S(1)} %get-tuple-element.53), channel_id=1, source_target_pairs={{0,1},{1,2},{2,3},{4,5},{5,6},{6,7},{8,9},{9,10},{10,11},{12,13},{... | collective-permute-start | bytes 3272 | tf_op jit(solution)/shard_map/ppermute | solution.py:19
  47.1 5.5 %collective-permute-start.7 = (f32[24,34,1]{2,1,0:T(8,128)S(1)}, f32[24,34,1]{2,1,0:T(8,128)S(1)}, u32[]{:S(2)}, u32[]{:S(2)}) collective-permute-start(f32[24,34,1]{2,1,0:T(8,128)S(1)} %get-tuple-element.30), channel_id=1, source_target_pairs={{0,1},{1,2},{2,3},{4,5},{5,6},{6,7},{8,9},{9,10},{10,11},{12,13},{... | collective-permute-start | bytes 9800 | tf_op jit(solution)/shard_map/ppermute | solution.py:19
  55.1 4.5 %collective-permute-start.12 = (f32[16,1,256]{2,1,0:T(1,128)S(1)}, f32[16,1,256]{2,1,0:T(1,128)S(1)}, u32[]{:S(2)}, u32[]{:S(2)}) collective-permute-start(f32[16,1,256]{2,1,0:T(1,128)S(1)} %get-tuple-element.50), channel_id=1, source_target_pairs={{0,4},{4,8},{8,12},{12,16},{16,20},{20,24},{24,28},{1,5},{5,9},{9,... | collective-permute-start | bytes 49160 | tf_op jit(solution)/shard_map/ppermute | solution.py:19
  61.1 4.2 %collective-permute-done.13 = f32[16,1,256]{2,1,0:T(1,128)S(1)} collective-permute-done((f32[16,1,256]{2,1,0:T(1,128)S(1)}, f32[16,1,256]{2,1,0:T(1,128)S(1)}, u32[]{:S(2)}, u32[]{:S(2)}) %collective-permute-start.13) | collective-permute-done | bytes 16416 | tf_op jit(solution)/shard_map/ppermute | solution.py:21
  65.5 7.3 %collective-permute-start.14 = (f32[16,34,1]{2,1,0:T(8,128)S(1)}, f32[16,34,1]{2,1,0:T(8,128)S(1)}, u32[]{:S(2)}, u32[]{:S(2)}) collective-permute-start(f32[16,34,1]{2,1,0:T(8,128)S(1)} %get-tuple-element.43), channel_id=1, source_target_pairs={{0,1},{1,2},{2,3},{4,5},{5,6},{6,7},{8,9},{9,10},{10,11},{12,13},{... | collective-permute-start | bytes 6536 | tf_op jit(solution)/shard_map/ppermute | solution.py:19
  74.1 5.6 %collective-permute-done.15 = f32[16,34,1]{2,1,0:T(8,128)S(1)} collective-permute-done((f32[16,34,1]{2,1,0:T(8,128)S(1)}, f32[16,34,1]{2,1,0:T(8,128)S(1)}, u32[]{:S(2)}, u32[]{:S(2)}) %collective-permute-start.15) | collective-permute-done | bytes 2208 | tf_op jit(solution)/shard_map/ppermute | solution.py:21
  82.1 4.5 %collective-permute-start.17 = (f32[24,1,256]{2,1,0:T(1,128)S(1)}, f32[24,1,256]{2,1,0:T(1,128)S(1)}, u32[]{:S(2)}, u32[]{:S(2)}) collective-permute-start(f32[24,1,256]{2,1,0:T(1,128)S(1)} %get-tuple-element.36), channel_id=1, source_target_pairs={{0,4},{4,8},{8,12},{12,16},{16,20},{20,24},{24,28},{1,5},{5,9},{9,... | collective-permute-start | bytes 73736 | tf_op jit(solution)/shard_map/ppermute | solution.py:19
  86.7 1.5 collective-permute-done.17
  89.8 6.8 %collective-permute-start.19 = (f32[24,34,1]{2,1,0:T(8,128)S(1)}, f32[24,34,1]{2,1,0:T(8,128)S(1)}, u32[]{:S(2)}, u32[]{:S(2)}) collective-permute-start(f32[24,34,1]{2,1,0:T(8,128)S(1)} %get-tuple-element.26), channel_id=1, source_target_pairs={{0,1},{1,2},{2,3},{4,5},{5,6},{6,7},{8,9},{9,10},{10,11},{12,13},{... | collective-permute-start | bytes 9800 | tf_op jit(solution)/shard_map/ppermute | solution.py:19
  99.9 48.0 %all-reduce = (f32[8]{0:T(128)S(1)}, f32[8]{0:T(128)S(1)}) all-reduce(f32[8]{0:T(128)S(1)} %get-tuple-element.6, f32[8]{0:T(128)S(1)} %get-tuple-element.5), channel_id=1, replica_groups=mesh['gx'=8,'gy'=4] {'gx','gy'}, use_global_device_ids=true, to_apply=%region_1.0 | all-reduce | flops 16 | bytes 128 | tf_op jit(solution)/shard_map/psum | solution.py:60
  147.9 2.2 fusion.63
  150.2 41.4 %psum.30 = f32[8]{0:T(128)S(1)} all-reduce(f32[8]{0:T(128)S(1)} %get-tuple-element.13), channel_id=1, replica_groups=mesh['gx'=8,'gy'=4] {'gx','gy'}, use_global_device_ids=true, to_apply=%region_5.0 | all-reduce | flops 8 | bytes 64 | tf_op jit(solution)/shard_map/psum | solution.py:60
  193.7 4.2 %collective-permute-start.20 = (f32[16,1,256]{2,1,0:T(1,128)S(1)}, f32[16,1,256]{2,1,0:T(1,128)S(1)}, u32[]{:S(2)}, u32[]{:S(2)}) collective-permute-start(f32[16,1,256]{2,1,0:T(1,128)S(1)} %get-tuple-element.48), channel_id=1, source_target_pairs={{0,4},{4,8},{8,12},{12,16},{16,20},{20,24},{24,28},{1,5},{5,9},{9,... | collective-permute-start | bytes 49160 | tf_op jit(solution)/shard_map/ppermute | solution.py:19
  199.3 4.2 %collective-permute-done.21 = f32[16,1,256]{2,1,0:T(1,128)S(1)} collective-permute-done((f32[16,1,256]{2,1,0:T(1,128)S(1)}, f32[16,1,256]{2,1,0:T(1,128)S(1)}, u32[]{:S(2)}, u32[]{:S(2)}) %collective-permute-start.21) | collective-permute-done | bytes 16416 | tf_op jit(solution)/shard_map/ppermute | solution.py:21
  206.5 2.3 collective-permute-done.23
  211.3 5.4 %collective-permute-start.25 = (f32[24,1,256]{2,1,0:T(1,128)S(1)}, f32[24,1,256]{2,1,0:T(1,128)S(1)}, u32[]{:S(2)}, u32[]{:S(2)}) collective-permute-start(f32[24,1,256]{2,1,0:T(1,128)S(1)} %get-tuple-element.34), channel_id=1, source_target_pairs={{0,4},{4,8},{8,12},{12,16},{16,20},{20,24},{24,28},{1,5},{5,9},{9,... | collective-permute-start | bytes 73736 | tf_op jit(solution)/shard_map/ppermute | solution.py:19
  216.7 1.5 collective-permute-done.25
  219.9 7.1 %collective-permute-start.27 = (f32[24,34,1]{2,1,0:T(8,128)S(1)}, f32[24,34,1]{2,1,0:T(8,128)S(1)}, u32[]{:S(2)}, u32[]{:S(2)}) collective-permute-start(f32[24,34,1]{2,1,0:T(8,128)S(1)} %get-tuple-element.22), channel_id=1, source_target_pairs={{0,1},{1,2},{2,3},{4,5},{5,6},{6,7},{8,9},{9,10},{10,11},{12,13},{... | collective-permute-start | bytes 9800 | tf_op jit(solution)/shard_map/ppermute | solution.py:19
  229.9 48.3 %psum.31 = f32[8]{0:T(128)S(1)} all-reduce(f32[8]{0:T(128)S(1)} %fusion), channel_id=1, replica_groups=mesh['gx'=8,'gy'=4] {'gx','gy'}, use_global_device_ids=true, to_apply=%region_7.0 | all-reduce | flops 8 | bytes 64 | tf_op jit(solution)/shard_map/psum | solution.py:60
  (132 shorter events, 43.3 us)
Async XLA Ops:
  1.9 6.3 %collective-permute-start = (f32[17,1,256]{2,1,0:T(1,128)S(1)}, f32[17,1,256]{2,1,0:T(1,128)S(1)}, u32[]{:S(2)}, u32[]{:S(2)}) collective-permute-start(f32[17,1,256]{2,1,0:T(1,128)S(1)} %get-tuple-element.45), channel_id=1, source_target_pairs={{0,4},{4,8},{8,12},{12,16},{16,20},{20,24},{24,28},{1,5},{5,9},{9,... | collective-permute-start | bytes 52232 | tf_op jit(solution)/shard_map/ppermute | solution.py:19
  6.8 5.6 %collective-permute-start.1 = (f32[17,1,256]{2,1,0:T(1,128)S(1)}, f32[17,1,256]{2,1,0:T(1,128)S(1)}, u32[]{:S(2)}, u32[]{:S(2)}) collective-permute-start(f32[17,1,256]{2,1,0:T(1,128)S(1)} %get-tuple-element.46), channel_id=1, source_target_pairs={{4,0},{8,4},{12,8},{16,12},{20,16},{24,20},{28,24},{5,1},{9,5},{13... | collective-permute-start | bytes 52232 | tf_op jit(solution)/shard_map/ppermute | solution.py:21
  21.8 13.1 %collective-permute-start.8 = (f32[8,1,256]{2,1,0:T(1,128)S(1)}, f32[8,1,256]{2,1,0:T(1,128)S(1)}, u32[]{:S(2)}, u32[]{:S(2)}) collective-permute-start(f32[8,1,256]{2,1,0:T(1,128)S(1)} %get-tuple-element.56), channel_id=1, source_target_pairs={{4,0},{8,4},{12,8},{16,12},{20,16},{24,20},{28,24},{5,1},{9,5},{13... | collective-permute-start | bytes 24584 | tf_op jit(solution)/shard_map/ppermute | solution.py:21
  23.1 11.8 %collective-permute-start.9 = (f32[8,1,256]{2,1,0:T(1,128)S(1)}, f32[8,1,256]{2,1,0:T(1,128)S(1)}, u32[]{:S(2)}, u32[]{:S(2)}) collective-permute-start(f32[8,1,256]{2,1,0:T(1,128)S(1)} %get-tuple-element.57), channel_id=1, source_target_pairs={{0,4},{4,8},{8,12},{12,16},{16,20},{20,24},{24,28},{1,5},{5,9},{9,... | collective-permute-start | bytes 24584 | tf_op jit(solution)/shard_map/ppermute | solution.py:19
  28.2 17.3 %collective-permute-start.4 = (f32[24,1,256]{2,1,0:T(1,128)S(1)}, f32[24,1,256]{2,1,0:T(1,128)S(1)}, u32[]{:S(2)}, u32[]{:S(2)}) collective-permute-start(f32[24,1,256]{2,1,0:T(1,128)S(1)} %get-tuple-element.37), channel_id=1, source_target_pairs={{4,0},{8,4},{12,8},{16,12},{20,16},{24,20},{28,24},{5,1},{9,5},{13... | collective-permute-start | bytes 73736 | tf_op jit(solution)/shard_map/ppermute | solution.py:21
  29.5 16.0 %collective-permute-start.5 = (f32[24,1,256]{2,1,0:T(1,128)S(1)}, f32[24,1,256]{2,1,0:T(1,128)S(1)}, u32[]{:S(2)}, u32[]{:S(2)}) collective-permute-start(f32[24,1,256]{2,1,0:T(1,128)S(1)} %get-tuple-element.38), channel_id=1, source_target_pairs={{0,4},{4,8},{8,12},{12,16},{16,20},{20,24},{24,28},{1,5},{5,9},{9,... | collective-permute-start | bytes 73736 | tf_op jit(solution)/shard_map/ppermute | solution.py:19
  35.1 8.7 %collective-permute-start.10 = (f32[8,34,1]{2,1,0:T(8,128)S(1)}, f32[8,34,1]{2,1,0:T(8,128)S(1)}, u32[]{:S(2)}, u32[]{:S(2)}) collective-permute-start(f32[8,34,1]{2,1,0:T(8,128)S(1)} %get-tuple-element.52), channel_id=1, source_target_pairs={{1,0},{2,1},{3,2},{5,4},{6,5},{7,6},{9,8},{10,9},{11,10},{13,12},{... | collective-permute-start | bytes 3272 | tf_op jit(solution)/shard_map/ppermute | solution.py:21
  36.6 8.3 %collective-permute-start.11 = (f32[8,34,1]{2,1,0:T(8,128)S(1)}, f32[8,34,1]{2,1,0:T(8,128)S(1)}, u32[]{:S(2)}, u32[]{:S(2)}) collective-permute-start(f32[8,34,1]{2,1,0:T(8,128)S(1)} %get-tuple-element.53), channel_id=1, source_target_pairs={{0,1},{1,2},{2,3},{4,5},{5,6},{6,7},{8,9},{9,10},{10,11},{12,13},{... | collective-permute-start | bytes 3272 | tf_op jit(solution)/shard_map/ppermute | solution.py:19
  45.8 6.9 %collective-permute-start.6 = (f32[24,34,1]{2,1,0:T(8,128)S(1)}, f32[24,34,1]{2,1,0:T(8,128)S(1)}, u32[]{:S(2)}, u32[]{:S(2)}) collective-permute-start(f32[24,34,1]{2,1,0:T(8,128)S(1)} %get-tuple-element.29), channel_id=1, source_target_pairs={{1,0},{2,1},{3,2},{5,4},{6,5},{7,6},{9,8},{10,9},{11,10},{13,12},{... | collective-permute-start | bytes 9800 | tf_op jit(solution)/shard_map/ppermute | solution.py:21
  47.1 7.0 %collective-permute-start.7 = (f32[24,34,1]{2,1,0:T(8,128)S(1)}, f32[24,34,1]{2,1,0:T(8,128)S(1)}, u32[]{:S(2)}, u32[]{:S(2)}) collective-permute-start(f32[24,34,1]{2,1,0:T(8,128)S(1)} %get-tuple-element.30), channel_id=1, source_target_pairs={{0,1},{1,2},{2,3},{4,5},{5,6},{6,7},{8,9},{9,10},{10,11},{12,13},{... | collective-permute-start | bytes 9800 | tf_op jit(solution)/shard_map/ppermute | solution.py:19
  55.1 6.0 %collective-permute-start.12 = (f32[16,1,256]{2,1,0:T(1,128)S(1)}, f32[16,1,256]{2,1,0:T(1,128)S(1)}, u32[]{:S(2)}, u32[]{:S(2)}) collective-permute-start(f32[16,1,256]{2,1,0:T(1,128)S(1)} %get-tuple-element.50), channel_id=1, source_target_pairs={{0,4},{4,8},{8,12},{12,16},{16,20},{20,24},{24,28},{1,5},{5,9},{9,... | collective-permute-start | bytes 49160 | tf_op jit(solution)/shard_map/ppermute | solution.py:19
  59.6 5.6 %collective-permute-start.13 = (f32[16,1,256]{2,1,0:T(1,128)S(1)}, f32[16,1,256]{2,1,0:T(1,128)S(1)}, u32[]{:S(2)}, u32[]{:S(2)}) collective-permute-start(f32[16,1,256]{2,1,0:T(1,128)S(1)} %get-tuple-element.51), channel_id=1, source_target_pairs={{4,0},{8,4},{12,8},{16,12},{20,16},{24,20},{28,24},{5,1},{9,5},{13... | collective-permute-start | bytes 49160 | tf_op jit(solution)/shard_map/ppermute | solution.py:21
  65.5 8.6 %collective-permute-start.14 = (f32[16,34,1]{2,1,0:T(8,128)S(1)}, f32[16,34,1]{2,1,0:T(8,128)S(1)}, u32[]{:S(2)}, u32[]{:S(2)}) collective-permute-start(f32[16,34,1]{2,1,0:T(8,128)S(1)} %get-tuple-element.43), channel_id=1, source_target_pairs={{0,1},{1,2},{2,3},{4,5},{5,6},{6,7},{8,9},{9,10},{10,11},{12,13},{... | collective-permute-start | bytes 6536 | tf_op jit(solution)/shard_map/ppermute | solution.py:19
  72.8 6.9 %collective-permute-start.15 = (f32[16,34,1]{2,1,0:T(8,128)S(1)}, f32[16,34,1]{2,1,0:T(8,128)S(1)}, u32[]{:S(2)}, u32[]{:S(2)}) collective-permute-start(f32[16,34,1]{2,1,0:T(8,128)S(1)} %get-tuple-element.44), channel_id=1, source_target_pairs={{1,0},{2,1},{3,2},{5,4},{6,5},{7,6},{9,8},{10,9},{11,10},{13,12},{... | collective-permute-start | bytes 6536 | tf_op jit(solution)/shard_map/ppermute | solution.py:21
  80.8 5.9 %collective-permute-start.16 = (f32[24,1,256]{2,1,0:T(1,128)S(1)}, f32[24,1,256]{2,1,0:T(1,128)S(1)}, u32[]{:S(2)}, u32[]{:S(2)}) collective-permute-start(f32[24,1,256]{2,1,0:T(1,128)S(1)} %get-tuple-element.35), channel_id=1, source_target_pairs={{4,0},{8,4},{12,8},{16,12},{20,16},{24,20},{28,24},{5,1},{9,5},{13... | collective-permute-start | bytes 73736 | tf_op jit(solution)/shard_map/ppermute | solution.py:21
  82.1 6.1 %collective-permute-start.17 = (f32[24,1,256]{2,1,0:T(1,128)S(1)}, f32[24,1,256]{2,1,0:T(1,128)S(1)}, u32[]{:S(2)}, u32[]{:S(2)}) collective-permute-start(f32[24,1,256]{2,1,0:T(1,128)S(1)} %get-tuple-element.36), channel_id=1, source_target_pairs={{0,4},{4,8},{8,12},{12,16},{16,20},{20,24},{24,28},{1,5},{5,9},{9,... | collective-permute-start | bytes 73736 | tf_op jit(solution)/shard_map/ppermute | solution.py:19
  88.5 8.1 %collective-permute-start.18 = (f32[24,34,1]{2,1,0:T(8,128)S(1)}, f32[24,34,1]{2,1,0:T(8,128)S(1)}, u32[]{:S(2)}, u32[]{:S(2)}) collective-permute-start(f32[24,34,1]{2,1,0:T(8,128)S(1)} %get-tuple-element.25), channel_id=1, source_target_pairs={{1,0},{2,1},{3,2},{5,4},{6,5},{7,6},{9,8},{10,9},{11,10},{13,12},{... | collective-permute-start | bytes 9800 | tf_op jit(solution)/shard_map/ppermute | solution.py:21
  89.8 8.2 %collective-permute-start.19 = (f32[24,34,1]{2,1,0:T(8,128)S(1)}, f32[24,34,1]{2,1,0:T(8,128)S(1)}, u32[]{:S(2)}, u32[]{:S(2)}) collective-permute-start(f32[24,34,1]{2,1,0:T(8,128)S(1)} %get-tuple-element.26), channel_id=1, source_target_pairs={{0,1},{1,2},{2,3},{4,5},{5,6},{6,7},{8,9},{9,10},{10,11},{12,13},{... | collective-permute-start | bytes 9800 | tf_op jit(solution)/shard_map/ppermute | solution.py:19
  193.7 5.6 %collective-permute-start.20 = (f32[16,1,256]{2,1,0:T(1,128)S(1)}, f32[16,1,256]{2,1,0:T(1,128)S(1)}, u32[]{:S(2)}, u32[]{:S(2)}) collective-permute-start(f32[16,1,256]{2,1,0:T(1,128)S(1)} %get-tuple-element.48), channel_id=1, source_target_pairs={{0,4},{4,8},{8,12},{12,16},{16,20},{20,24},{24,28},{1,5},{5,9},{9,... | collective-permute-start | bytes 49160 | tf_op jit(solution)/shard_map/ppermute | solution.py:19
  197.9 5.6 %collective-permute-start.21 = (f32[16,1,256]{2,1,0:T(1,128)S(1)}, f32[16,1,256]{2,1,0:T(1,128)S(1)}, u32[]{:S(2)}, u32[]{:S(2)}) collective-permute-start(f32[16,1,256]{2,1,0:T(1,128)S(1)} %get-tuple-element.49), channel_id=1, source_target_pairs={{4,0},{8,4},{12,8},{16,12},{20,16},{24,20},{28,24},{5,1},{9,5},{13... | collective-permute-start | bytes 49160 | tf_op jit(solution)/shard_map/ppermute | solution.py:21
  210.0 6.7 %collective-permute-start.24 = (f32[24,1,256]{2,1,0:T(1,128)S(1)}, f32[24,1,256]{2,1,0:T(1,128)S(1)}, u32[]{:S(2)}, u32[]{:S(2)}) collective-permute-start(f32[24,1,256]{2,1,0:T(1,128)S(1)} %get-tuple-element.33), channel_id=1, source_target_pairs={{4,0},{8,4},{12,8},{16,12},{20,16},{24,20},{28,24},{5,1},{9,5},{13... | collective-permute-start | bytes 73736 | tf_op jit(solution)/shard_map/ppermute | solution.py:21
  211.3 6.9 %collective-permute-start.25 = (f32[24,1,256]{2,1,0:T(1,128)S(1)}, f32[24,1,256]{2,1,0:T(1,128)S(1)}, u32[]{:S(2)}, u32[]{:S(2)}) collective-permute-start(f32[24,1,256]{2,1,0:T(1,128)S(1)} %get-tuple-element.34), channel_id=1, source_target_pairs={{0,4},{4,8},{8,12},{12,16},{16,20},{20,24},{24,28},{1,5},{5,9},{9,... | collective-permute-start | bytes 73736 | tf_op jit(solution)/shard_map/ppermute | solution.py:19
  218.6 8.4 %collective-permute-start.26 = (f32[24,34,1]{2,1,0:T(8,128)S(1)}, f32[24,34,1]{2,1,0:T(8,128)S(1)}, u32[]{:S(2)}, u32[]{:S(2)}) collective-permute-start(f32[24,34,1]{2,1,0:T(8,128)S(1)} %get-tuple-element.21), channel_id=1, source_target_pairs={{1,0},{2,1},{3,2},{5,4},{6,5},{7,6},{9,8},{10,9},{11,10},{13,12},{... | collective-permute-start | bytes 9800 | tf_op jit(solution)/shard_map/ppermute | solution.py:21
  219.9 8.5 %collective-permute-start.27 = (f32[24,34,1]{2,1,0:T(8,128)S(1)}, f32[24,34,1]{2,1,0:T(8,128)S(1)}, u32[]{:S(2)}, u32[]{:S(2)}) collective-permute-start(f32[24,34,1]{2,1,0:T(8,128)S(1)} %get-tuple-element.22), channel_id=1, source_target_pairs={{0,1},{1,2},{2,3},{4,5},{5,6},{6,7},{8,9},{9,10},{10,11},{12,13},{... | collective-permute-start | bytes 9800 | tf_op jit(solution)/shard_map/ppermute | solution.py:19
  (21 other events, 433.9 us)
where the time goes:
time: 281 us; the launch traced here: 279 us
  blocking collectives  138 us (49%)
  starting transfers between devices  88.9 us (32%)
  waiting for transfers between devices  33.1 us (12%)
  other arithmetic  13.5 us (5%)
  local copies, waits for them, and re-layouts  5.37 us (2%)
    psum x3, blocking collectives, member_dot(): return lax.psum(jnp.sum(left * right, axis=(1, 2, 3)), ('gx', 'gy'))  138 us
    ppermute x14, starting transfers between devices, padded_2(): lax.ppermute(tail, axis, [(i, (i + 1) % count) for i in range(ends)])  70.5 us
    ppermute x14, waiting for transfers between devices, padded_2(): lax.ppermute(head, axis, [((i + 1) % count, i) for i in range(ends)])  24.5 us
    ppermute x14, starting transfers between devices, padded_2(): lax.ppermute(head, axis, [((i + 1) % count, i) for i in range(ends)])  18.4 us
    ppermute x14, waiting for transfers between devices, padded_2(): lax.ppermute(tail, axis, [(i, (i + 1) % count) for i in range(ends)])  8.54 us
  transfers between devices with their start and end apart: 28, of which 15 were waited for; matrix products, arithmetic and copies ran while one was open for 0% of the time, Pallas kernels for 0%

commit v1 on v0

v1 whole, which is shorter than its diff:
```python
import functools

import jax
import jax.numpy as jnp
from jax import lax
from jax.experimental import pallas as pl
from jax.experimental.pallas import tpu as pltpu
from jax.sharding import PartitionSpec as P

strain_floor = 0.1
water_drag = 0.25
flow_power = 1.0 / 3.0

F32 = jnp.float32
DEPTH = 5
SIDE = 8
LANES = 128
PLANES = 4
GROUPS = LANES // SIDE
ROWS_PER_STRIP = GROUPS // PLANES


def vmem(shape):
    return pltpu.VMEM(shape, F32)


def call(kernel, outs, ins, scratch=(), flops=0):
    specs = [pl.BlockSpec(memory_space=pltpu.HBM if space == "hbm" else pltpu.VMEM) for space in ins]
    out_specs = [
        pl.BlockSpec(memory_space=pltpu.HBM if isinstance(o, jax.ShapeDtypeStruct) else pltpu.VMEM) for o in outs
    ]
    return pl.pallas_call(
        kernel,
        out_shape=outs,
        in_specs=specs,
        out_specs=out_specs,
        scratch_shapes=scratch,
        cost_estimate=pl.CostEstimate(flops=flops, bytes_accessed=flops // 8, transcendentals=0),
        compiler_params=pltpu.CompilerParams(vmem_limit_bytes=48 * 1024 * 1024),
    )


def lane_iota(shape):
    return lax.broadcasted_iota(jnp.int32, shape, len(shape) - 1)


def sublane_iota(shape):
    return lax.broadcasted_iota(jnp.int32, shape, len(shape) - 2)


def pack_kernel(
    vel, fric, thick, surf, ice, ground, own, to_left, to_right,
    vel_in, fric_in, thick_in, surf_in, ice_in, ground_in, friction32, sems,
):
    members, rows, cols = fric.shape
    tiles = cols // LANES
    copies = [
        pltpu.make_async_copy(source, target, sems.at[k])
        for k, (source, target) in enumerate(
            [(fric, fric_in), (thick, thick_in), (surf, surf_in), (ice, ice_in), (ground, ground_in)]
            + [(vel.at[:, pl.ds(t * LANES, LANES)], vel_in.at[t]) for t in range(tiles)]
        )
    ]
    for copy in copies:
        copy.start()
    for copy in copies:
        copy.wait()
    for t in range(tiles):
        friction32[t] = fric_in[:, :, t * LANES : (t + 1) * LANES].astype(F32).reshape(members * rows, LANES)
    group = lane_iota((members, LANES)) // SIDE
    sub = sublane_iota((members, LANES))

    def strip(block, carry):
        base = pl.multiple_of(block * 8, 8)
        near = []
        for t in range(tiles):
            part = slice(t * LANES, (t + 1) * LANES)
            icef = ice_in[pl.ds(base, 8), part].astype(F32)
            near.append(
                (
                    icef,
                    icef * ground_in[pl.ds(base, 8), part].astype(F32),
                    icef * thick_in[pl.ds(base, 8), part],
                    surf_in[pl.ds(base, 8), part],
                )
            )
        for half in range(8 // ROWS_PER_STRIP):
            heads = jnp.zeros((members, LANES), F32)
            tails = jnp.zeros((members, LANES), F32)
            for step in range(ROWS_PER_STRIP):
                at = half * ROWS_PER_STRIP + step
                row = base + at
                for t in range(tiles):
                    part = slice(t * LANES, (t + 1) * LANES)
                    icef, grounded, thin, top = (value[at : at + 1, :] for value in near[t])
                    field_u = vel_in[t, pl.ds(row, members, stride=2 * rows), :] * icef
                    field_v = vel_in[t, pl.ds(rows + row, members, stride=2 * rows), :] * icef
                    rough = friction32[t, pl.ds(row, members, stride=rows), :]
                    drag = grounded * rough + water_drag * icef
                    shared = jnp.where(sub == 0, thin, jnp.where(sub == 1, top, jnp.where(sub == 2, icef, 0.0)))
                    for plane, value in enumerate((field_u, field_v, drag, shared)):
                        own[row, plane, :, part] = value
                        place = step * PLANES + plane
                        if t == 0:
                            head = pltpu.roll(value, place * SIDE, 1) if place else value
                            heads = jnp.where(group == place, head, heads)
                        if t == tiles - 1:
                            tail = pltpu.roll(value, (place + 1) * SIDE, 1) if place != GROUPS - 1 else value
                            tails = jnp.where(group == place, tail, tails)
            to_left[block * (8 // ROWS_PER_STRIP) + half] = heads
            to_right[block * (8 // ROWS_PER_STRIP) + half] = tails
        return carry

    lax.fori_loop(0, rows // 8, strip, 0)


def side_tile(from_left, from_right, row, plane, lane):
    block, step = row // ROWS_PER_STRIP, row % ROWS_PER_STRIP
    place = step * PLANES + plane
    right = from_right[block]
    left = from_left[block]
    if place:
        right = pltpu.roll(right, LANES - place * SIDE, 1)
    if place != GROUPS - 1:
        left = pltpu.roll(left, LANES - (place + 1) * SIDE, 1)
    return jnp.where(lane < SIDE, right, jnp.where(lane >= LANES - SIDE, left, 0.0))


def edge_kernel(own, from_left, from_right, to_up, to_down):
    rows, _, members, cols = own.shape
    lane = lane_iota((members, LANES))
    for step in range(DEPTH):
        for target, row in ((to_up, step), (to_down, rows - DEPTH + step)):
            for plane in range(PLANES):
                target[step, plane, :, :cols] = own[row, plane]
                target[step, plane, :, cols:] = side_tile(from_left, from_right, row, plane, lane)


def loop(low, high, block, body, carry=0):
    count = high - low
    whole = count // block

    def step(index, carry):
        return body(low + index * block, block, carry)

    carry = lax.fori_loop(0, whole, step, carry)
    if count % block:
        carry = body(low + whole * block, count % block, carry)
    return carry


def compute_kernel(
    own, from_left, from_right, from_up, from_down, sums, along, across,
    field, visc, sx, sy, sz, rest, inverse,
):
    rows, _, members, cols = own.shape
    wide = cols + LANES
    lane = lane_iota((members, LANES))

    for step in range(DEPTH):
        field[step] = from_up[step]
        field[DEPTH + rows + step] = from_down[step]

    def place(block, carry):
        base = block * ROWS_PER_STRIP
        for step in range(ROWS_PER_STRIP):
            for plane in range(PLANES):
                item = step * PLANES + plane
                right = from_right[block]
                left = from_left[block]
                if item:
                    right = pltpu.roll(right, LANES - item * SIDE, 1)
                if item != GROUPS - 1:
                    left = pltpu.roll(left, LANES - (item + 1) * SIDE, 1)
                field[DEPTH + base + step, plane, :, :cols] = own[base + step, plane]
                field[DEPTH + base + step, plane, :, cols:] = jnp.where(
                    lane < SIDE, right, jnp.where(lane >= LANES - SIDE, left, 0.0)
                )
        return carry

    lax.fori_loop(0, rows // ROWS_PER_STRIP, place, 0)

    def spread(row, sub):
        return jnp.broadcast_to(field[row, 3, pl.ds(sub, 1), :], (members, wide))

    def after(value):
        return pltpu.roll(value, wide - 1, 1)

    def before(value):
        return pltpu.roll(value, 1, 1)

    def stress(row, strain_u, strain_v, strain_c, nu):
        half = 0.5 * nu
        sx[row] = half * (2.0 * strain_u + strain_v)
        sy[row] = half * (strain_u + 2.0 * strain_v)
        sz[row] = half * (0.5 * strain_c)

    def strains(ref_u, ref_v, first, count):
        us = [ref_u(first - 1 + k) for k in range(count + 2)]
        vs = [ref_v(first - 1 + k) for k in range(count + 2)]
        for k in range(count):
            yield (
                first + k,
                us[k + 2] - us[k],
                after(vs[k + 1]) - before(vs[k + 1]),
                (after(us[k + 1]) - before(us[k + 1])) + (vs[k + 2] - vs[k]),
            )

    last = rows + 2 * DEPTH

    def viscosity(first, count, carry):
        for row, su, sv, sc in strains(lambda r: field[r, 0], lambda r: field[r, 1], first, count):
            square = 0.25 * (su * su + sv * sv + su * sv + 0.25 * (sc * sc)) + strain_floor
            nu = (0.5 * spread(row, 0)) * jnp.exp(-flow_power * jnp.log(square))
            visc[row] = nu
            stress(row, su, sv, sc, nu)
        return carry

    loop(1, last - 1, 2, viscosity)

    def divergences(first, count):
        for row in range(count):
            row = first + row
            z = sz[row]
            y = sy[row]
            yield (
                row,
                (sx[row + 1] - sx[row - 1]) + (after(z) - before(z)),
                (after(y) - before(y)) + (sz[row + 1] - sz[row - 1]),
            )

    def residual(first, count, carry):
        for row, div_u, div_v in divergences(first, count):
            drag = field[row, 2]
            thin = spread(row, 0)
            icef = spread(row, 2)
            top = spread(row, 1)
            half = 0.5 * thin
            force_u = half * (spread(row - 1, 1) - spread(row + 1, 1))
            force_v = half * (before(top) - after(top))
            res_u = force_u - (drag * field[row, 0] - icef * div_u)
            res_v = force_v - (drag * field[row, 1] - icef * div_v)
            nu = visc[row]
            near_rows = visc[row + 1] + visc[row - 1]
            near_cols = after(nu) + before(nu)
            diag_u = near_rows + 0.25 * near_cols + drag
            diag_v = near_cols + 0.25 * near_rows + drag
            on = icef > 0.0
            inv_u = 1.0 / jnp.where(on, diag_u, 1.0)
            inv_v = 1.0 / jnp.where(on, diag_v, 1.0)
            rest[row, 0] = res_u
            rest[row, 1] = res_v
            inverse[row, 0] = inv_u
            inverse[row, 1] = inv_v
            along[row, 0] = res_u * inv_u
            along[row, 1] = res_v * inv_v
        return carry

    loop(2, last - 2, 2, residual)

    def direction(first, count, carry):
        for row, su, sv, sc in strains(lambda r: along[r, 0], lambda r: along[r, 1], first, count):
            stress(row, su, sv, sc, visc[row])
        return carry

    loop(3, last - 3, 2, direction)

    def image(first, count, carry):
        for row, div_u, div_v in divergences(first, count):
            drag = field[row, 2]
            icef = spread(row, 2)
            dir_u = along[row, 0]
            dir_v = along[row, 1]
            off_u = drag * dir_u - icef * div_u - rest[row, 0]
            off_v = drag * dir_v - icef * div_v - rest[row, 1]
            across[row, 0] = off_u * inverse[row, 0]
            across[row, 1] = off_v * inverse[row, 1]
        return carry

    loop(4, last - 4, 2, image)

    def energy(first, count, carry):
        norm, cross, square, power = carry
        for row, su, sv, sc in strains(lambda r: across[r, 0], lambda r: across[r, 1], first, count):
            su, sv, sc = su[:, :cols], sv[:, :cols], sc[:, :cols]
            drag = field[row, 2, :, :cols]
            nu = visc[row, :, :cols]
            res_u, res_v = rest[row, 0, :, :cols], rest[row, 1, :, :cols]
            dir_u, dir_v = along[row, 0, :, :cols], along[row, 1, :, :cols]
            off_u, off_v = across[row, 0, :, :cols], across[row, 1, :, :cols]
            norm = norm + (res_u * dir_u + res_v * dir_v)
            cross = cross + (res_u * off_u + res_v * off_v)
            square = square + (off_u * off_u / inverse[row, 0, :, :cols] + off_v * off_v / inverse[row, 1, :, :cols])
            power = power + (
                drag * (off_u * off_u + off_v * off_v)
                + nu * (su * su + su * sv + sv * sv + 0.25 * (sc * sc))
            )
        return norm, cross, square, power

    zero = jnp.zeros((members, cols), F32)
    totals = loop(DEPTH, DEPTH + rows, 2, energy, (zero,) * 4)
    sub = sublane_iota((members, LANES))
    row = jnp.zeros((members, LANES), F32)
    for k, total in enumerate(totals):
        row = row + jnp.where(lane == sub + members * k, jnp.sum(total, axis=1, keepdims=True), 0.0)
    row = jnp.sum(row, axis=0, keepdims=True)
    sums[...] = jnp.broadcast_to(row[None], sums.shape)


def final_kernel(parts, own, along, across, out, out_tiles, sems):
    rows, _, members, cols = own.shape
    total = jnp.sum(parts[...], axis=0)
    spread = jnp.broadcast_to(total, (members, LANES))
    lane = lane_iota((members, LANES))
    sub = sublane_iota((members, LANES))
    norm, cross, square, power = (
        jnp.sum(jnp.where(lane == sub + members * k, spread, 0.0), axis=1, keepdims=True) for k in range(4)
    )
    k1, k2, k3 = cross / norm, square / norm, power / norm
    scale = 1.0 + k1
    first = 1.0 / scale
    beta = (k2 - k1 * k1) * first * first
    curve = (k1 * k1 * scale - 2.0 * k1 * (k1 + k2) + k3) * first * first - beta * beta * scale
    second = jnp.where(curve > 0.0, beta / jnp.where(curve > 0.0, curve, 1.0), 0.0)
    on_along = jnp.broadcast_to(first + second * (k1 * first + beta), (members, LANES))
    on_across = jnp.broadcast_to(second * first, (members, LANES))
    tiles = cols // LANES

    def body(block, carry):
        for step in range(4):
            row = block * 4 + step
            for part in range(2):
                for t in range(tiles):
                    place = slice(t * LANES, (t + 1) * LANES)
                    out_tiles[t, pl.ds(part * rows + row, members, stride=2 * rows), :] = (
                        own[row, part, :, place]
                        + on_along * along[DEPTH + row, part, :, place]
                        - on_across * across[DEPTH + row, part, :, place]
                    )
        return carry

    lax.fori_loop(0, rows // 4, body, 0)
    copies = [
        pltpu.make_async_copy(out_tiles.at[t], out.at[:, pl.ds(t * LANES, LANES)], sems.at[t])
        for t in range(tiles)
    ]
    for copy in copies:
        copy.start()
    for copy in copies:
        copy.wait()


def shifted(axis, array, up):
    count = lax.axis_size(axis)
    pairs = [(i, i + 1) if up else (i + 1, i) for i in range(count - 1)]
    return lax.ppermute(array, axis, pairs)


def per_device(velocity_guess, friction, thickness, surface, ice_mask, grounded_mask):
    members, parts, rows, cols = velocity_guess.shape
    devices = lax.axis_size(("gx", "gy"))
    wide = cols + LANES
    high = rows + 2 * DEPTH
    strips = rows // ROWS_PER_STRIP
    tiles = cols // LANES
    flat = members * parts * rows
    own, to_left, to_right = call(
        pack_kernel,
        [
            vmem((rows, PLANES, members, cols)),
            vmem((strips, members, LANES)),
            vmem((strips, members, LANES)),
        ],
        ["hbm"] * 6,
        [
            pltpu.VMEM((tiles, flat, LANES), F32),
            pltpu.VMEM((members, rows, cols), friction.dtype),
            pltpu.VMEM((rows, cols), F32),
            pltpu.VMEM((rows, cols), F32),
            pltpu.VMEM((rows, cols), jnp.int32),
            pltpu.VMEM((rows, cols), jnp.int32),
            pltpu.VMEM((tiles, members * rows, LANES), F32),
            pltpu.SemaphoreType.DMA((5 + tiles,)),
        ],
    )(velocity_guess.reshape(flat, cols), friction, thickness, surface, ice_mask, grounded_mask)
    from_left = shifted("gy", to_right, True)
    from_right = shifted("gy", to_left, False)
    edge = vmem((DEPTH, PLANES, members, wide))
    to_up, to_down = call(edge_kernel, [edge, edge], ["vmem"] * 3)(own, from_left, from_right)
    from_up = shifted("gx", to_down, True)
    from_down = shifted("gx", to_up, False)
    two = (high, 2, members, wide)
    one = (high, members, wide)
    sums, along, across = call(
        compute_kernel,
        [vmem((devices, 1, LANES)), vmem(two), vmem(two)],
        ["vmem"] * 5,
        [vmem((high, PLANES, members, wide))] + [vmem(one)] * 4 + [vmem(two)] * 2,
    )(own, from_left, from_right, from_up, from_down)
    shares = lax.all_to_all(sums, ("gx", "gy"), 0, 0, tiled=True)
    (out,) = call(
        final_kernel,
        [jax.ShapeDtypeStruct((flat, cols), F32)],
        ["vmem"] * 4,
        [pltpu.VMEM((tiles, flat, LANES), F32), pltpu.SemaphoreType.DMA((tiles,))],
    )(shares, own, along, across)
    return out.reshape(members, parts, rows, cols)


def solution(mesh):
    placed = (
        P(None, None, "gx", "gy"),
        P(None, "gx", "gy"),
        P("gx", "gy"),
        P("gx", "gy"),
        P("gx", "gy"),
        P("gx", "gy"),
    )
    return jax.shard_map(
        per_device, mesh=mesh, in_specs=placed, out_specs=P(None, None, "gx", "gy"), check_vma=False
    )
```

time: 281 us -> 54.6 us (0.19)
  blocking collectives: 138 us -> 15 us
  starting transfers between devices: 88.9 us -> 8.35 us
  waiting for transfers between devices: 33.1 us -> 11.9 us
  Pallas kernels: 0 us -> 13.7 us
  other arithmetic: 13.5 us -> 0 us
    psum x3 -> x0, blocking collectives: 138 us -> none  [member_dot(): return lax.psum(jnp.sum(left * right, axis=(1, 2, 3)), ('gx', 'gy'))]
    ppermute x28 -> x4, starting transfers between devices: 88.9 us -> 8.35 us  [shifted(): return lax.ppermute(array, axis, pairs)]
    ppermute x28 -> x4, waiting for transfers between devices: 33.1 us -> 11.9 us  [shifted(): return lax.ppermute(array, axis, pairs)]
    all_to_all x0 -> x1, blocking collectives: none -> 15 us  [per_device(): shares = lax.all_to_all(sums, ('gx', 'gy'), 0, 0, tiled=True)]
    pallas_call x0 -> x4, Pallas kernels: none -> 13.7 us  [the longest x1 10.8 us: per_device(): call(compute_kernel, [vmem((devices, 1, LANES)), vmem(two), vmem(two)], [...]
    mul x5 -> x0, other arithmetic: 3.12 us -> none  [the longest x3 1.71 us: stresses(): visc * (4.0 * ka + 2.0 * kb)]
    another operation x11 -> x0, other arithmetic: 3 us -> none  [the longest x6 2.25 us: divergence(): return jnp.stack([out_u, out_v], 1)]
  transfers between devices with their start and end apart: 28 -> 4, of which waited for: 15 -> 3; matrix products, arithmetic and copies ran while one was open for 0% -> 0% of each run, Pallas kernels for 0% -> 0%
where the time goes in v1:
time: 54.6 us; the launch traced here: 54 us
  blocking collectives  15 us (27%)
  Pallas kernels  13.7 us (25%)
  waiting for transfers between devices  11.9 us (22%)
  starting transfers between devices  8.35 us (15%)
  local copies, waits for them, and re-layouts  4.97 us (9%)
    all_to_all x1, blocking collectives, per_device(): shares = lax.all_to_all(sums, ('gx', 'gy'), 0, 0, tiled=True)  15 us
    ppermute x4, waiting for transfers between devices, shifted(): return lax.ppermute(array, axis, pairs)  11.9 us
    pallas_call x1, Pallas kernels, per_device(): call(compute_kernel, [vmem((devices, 1, LANES)), vmem(two), vmem(two)], [...  10.8 us
    ppermute x4, starting transfers between devices, shifted(): return lax.ppermute(array, axis, pairs)  8.35 us
    unnamed x12, local copies, waits for them, and re-layouts  4.97 us
    pallas_call x1, Pallas kernels, per_device(): call(final_kernel, [jax.ShapeDtypeStruct((flat, cols), F32)], ['vmem'] *...  1.47 us
    pallas_call x1, Pallas kernels, per_device(): call(pack_kernel, [vmem((rows, PLANES, members, cols)), vmem((strips, mem...  1.24 us
  transfers between devices with their start and end apart: 4, of which 3 were waited for; matrix products, arithmetic and copies ran while one was open for 0% of the time, Pallas kernels for 0%

profile of v1, /device:TPU:0, one launch (start us, length us, event | category | flops | bytes accessed | tf_op | source)
XLA Modules:
  0.0 54.0 jit_solution(9208334309750238534)
XLA Ops:
  0.0 0.0 copy-start
  0.0 1.0 %copy-done = f32[8,2,32,256]{3,2,1,0:T(8,128)S(1)} copy-done((f32[8,2,32,256]{3,2,1,0:T(8,128)S(1)}, f32[8,2,32,256]{3,2,1,0:T(8,128)}, u32[]{:S(2)}) %copy-start) | copy-done | bytes 524312
  1.0 0.0 copy-start.1
  1.0 0.9 %copy-done.1 = bf16[8,32,256]{2,1,0:T(8,128)(2,1)S(1)} copy-done((bf16[8,32,256]{2,1,0:T(8,128)(2,1)S(1)}, bf16[8,32,256]{2,1,0:T(8,128)(2,1)}, u32[]{:S(2)}) %copy-start.1) | copy-done | bytes 131096
  1.9 0.0 copy-start.2
  1.9 0.8 %copy-done.2 = f32[32,256]{1,0:T(8,128)S(1)} copy-done((f32[32,256]{1,0:T(8,128)S(1)}, f32[32,256]{1,0:T(8,128)}, u32[]{:S(2)}) %copy-start.2) | copy-done | bytes 32792
  2.7 0.0 copy-start.3
  2.7 0.8 %copy-done.3 = f32[32,256]{1,0:T(8,128)S(1)} copy-done((f32[32,256]{1,0:T(8,128)S(1)}, f32[32,256]{1,0:T(8,128)}, u32[]{:S(2)}) %copy-start.3) | copy-done | bytes 32792
  3.5 0.0 copy-start.4
  3.5 0.8 %copy-done.4 = s32[32,256]{1,0:T(8,128)S(1)} copy-done((s32[32,256]{1,0:T(8,128)S(1)}, s32[32,256]{1,0:T(8,128)}, u32[]{:S(2)}) %copy-start.4) | copy-done | bytes 32792
  4.2 0.8 %copy-done.5 = s32[32,256]{1,0:T(8,128)S(1)} copy-done((s32[32,256]{1,0:T(8,128)S(1)}, s32[32,256]{1,0:T(8,128)}, u32[]{:S(2)}) %copy-start.5) | copy-done | bytes 32792
  5.0 1.2 %shard_map.64 = (f32[32,4,8,256]{3,2,1,0:T(8,128)S(1)}, f32[8,8,128]{2,1,0:T(8,128)S(1)}, f32[8,8,128]{2,1,0:T(8,128)S(1)}) custom-call(f32[512,256]{1,0:T(8,128)S(1)} %bitcast.2, bf16[8,32,256]{2,1,0:T(8,128)(2,1)S(1)} %copy-done.1, f32[32,256]{1,0:T(8,128)S(1)} %copy-done.2, f32[32,256]{1,0:T(8,128)S(1)} %copy-done.3, s32[32,256]{1,0:T(8,128)S(1)} %copy-done.4, ...), custom_call_target="tpu_custom_call" | custom-call | tf_op jit(solution)/shard_map/pallas_call | solution.py:367
  6.2 2.4 %collective-permute-start = (f32[8,8,128]{2,1,0:T(8,128)S(1)}, f32[8,8,128]{2,1,0:T(8,128)S(1)}, u32[]{:S(2)}, u32[]{:S(2)}) collective-permute-start(f32[8,8,128]{2,1,0:T(8,128)S(1)} %get-tuple-element.14), channel_id=1, source_target_pairs={{0,1},{1,2},{2,3},{4,5},{5,6},{6,7},{8,9},{9,10},{10,11},{12,13},{... | collective-permute-start | bytes 98312 | tf_op jit(solution)/shard_map/ppermute | solution.py:356
  8.6 1.3 %collective-permute-start.1 = (f32[8,8,128]{2,1,0:T(8,128)S(1)}, f32[8,8,128]{2,1,0:T(8,128)S(1)}, u32[]{:S(2)}, u32[]{:S(2)}) collective-permute-start(f32[8,8,128]{2,1,0:T(8,128)S(1)} %get-tuple-element.15), channel_id=1, source_target_pairs={{1,0},{2,1},{3,2},{5,4},{6,5},{7,6},{9,8},{10,9},{11,10},{13,12},{... | collective-permute-start | bytes 98312 | tf_op jit(solution)/shard_map/ppermute | solution.py:356
  9.9 0.0 collective-permute-done.from_left
  9.9 3.9 %collective-permute-done.1.from_right = f32[8,8,128]{2,1,0:T(8,128)S(1)} collective-permute-done((f32[8,8,128]{2,1,0:T(8,128)S(1)}, f32[8,8,128]{2,1,0:T(8,128)S(1)}, u32[]{:S(2)}, u32[]{:S(2)}) %collective-permute-start.1) | collective-permute-done | bytes 32800 | tf_op jit(solution)/shard_map/ppermute | solution.py:356
  13.8 0.1 shard_map.65
  14.0 3.4 %collective-permute-start.2 = (f32[5,4,8,384]{3,2,1,0:T(8,128)S(1)}, f32[5,4,8,384]{3,2,1,0:T(8,128)S(1)}, u32[]{:S(2)}, u32[]{:S(2)}) collective-permute-start(f32[5,4,8,384]{3,2,1,0:T(8,128)S(1)} %get-tuple-element.16), channel_id=1, source_target_pairs={{0,4},{4,8},{8,12},{12,16},{16,20},{20,24},{24,28},{1,5},{5,9},{9,... | collective-permute-start | bytes 737288 | tf_op jit(solution)/shard_map/ppermute | solution.py:356
  17.4 1.3 %collective-permute-start.3 = (f32[5,4,8,384]{3,2,1,0:T(8,128)S(1)}, f32[5,4,8,384]{3,2,1,0:T(8,128)S(1)}, u32[]{:S(2)}, u32[]{:S(2)}) collective-permute-start(f32[5,4,8,384]{3,2,1,0:T(8,128)S(1)} %get-tuple-element.17), channel_id=1, source_target_pairs={{4,0},{8,4},{12,8},{16,12},{20,16},{24,20},{28,24},{5,1},{9,5},{13... | collective-permute-start | bytes 737288 | tf_op jit(solution)/shard_map/ppermute | solution.py:356
  18.7 3.3 %collective-permute-done.2.from_up = f32[5,4,8,384]{3,2,1,0:T(8,128)S(1)} collective-permute-done((f32[5,4,8,384]{3,2,1,0:T(8,128)S(1)}, f32[5,4,8,384]{3,2,1,0:T(8,128)S(1)}, u32[]{:S(2)}, u32[]{:S(2)}) %collective-permute-start.2) | collective-permute-done | bytes 245792 | tf_op jit(solution)/shard_map/ppermute | solution.py:356
  22.0 4.7 %collective-permute-done.3.from_down = f32[5,4,8,384]{3,2,1,0:T(8,128)S(1)} collective-permute-done((f32[5,4,8,384]{3,2,1,0:T(8,128)S(1)}, f32[5,4,8,384]{3,2,1,0:T(8,128)S(1)}, u32[]{:S(2)}, u32[]{:S(2)}) %collective-permute-start.3) | collective-permute-done | bytes 245792 | tf_op jit(solution)/shard_map/ppermute | solution.py:356
  26.7 10.8 %shard_map.66 = (f32[32,1,128]{2,1,0:T(1,128)S(1)}, f32[42,2,8,384]{3,2,1,0:T(8,128)S(1)}, f32[42,2,8,384]{3,2,1,0:T(8,128)S(1)}) custom-call(f32[32,4,8,256]{3,2,1,0:T(8,128)S(1)} %get-tuple-element.13.own, f32[8,8,128]{2,1,0:T(8,128)S(1)} %collective-permute-done.from_left, f32[8,8,128]{2,1,0:T(8,128)S(1)} %collective-permute-done.1.from_right, ...), custom_call_target="tpu_custom_call" | custom-call | tf_op jit(solution)/shard_map/pallas_call | solution.py:394
  37.6 15.0 %all_to_all.5.parts = f32[32,1,128]{2,1,0:T(1,128)S(1)} all-to-all(f32[32,1,128]{2,1,0:T(1,128)S(1)} %get-tuple-element.18), channel_id=1, replica_groups=mesh['gx'=8,'gy'=4] {'gx','gy'}, dimensions={0} | all-to-all | bytes 32768 | tf_op jit(solution)/shard_map/all_to_all | solution.py:400
  52.6 1.5 %shard_map.67 = f32[512,256]{1,0:T(8,128)} custom-call(f32[32,1,128]{2,1,0:T(1,128)S(1)} %all_to_all.5.parts, f32[32,4,8,256]{3,2,1,0:T(8,128)S(1)} %get-tuple-element.13.own, f32[42,2,8,384]{3,2,1,0:T(8,128)S(1)} %get-tuple-element.19.along, f32[42,2,8,384]{3,2,1,0:T(8,128)S(1)} %get-tuple-element.20.across), custom_call_target="tpu_custom_call" | custom-call | tf_op jit(solution)/shard_map/pallas_call | solution.py:401
  (1 shorter events, 0.0 us)
Async XLA Ops:
  0.0 1.0 %copy-start = (f32[8,2,32,256]{3,2,1,0:T(8,128)S(1)}, f32[8,2,32,256]{3,2,1,0:T(8,128)}, u32[]{:S(2)}) copy-start(f32[8,2,32,256]{3,2,1,0:T(8,128)} %param.6) | copy-start | bytes 1572868
  1.0 0.9 %copy-start.1 = (bf16[8,32,256]{2,1,0:T(8,128)(2,1)S(1)}, bf16[8,32,256]{2,1,0:T(8,128)(2,1)}, u32[]{:S(2)}) copy-start(bf16[8,32,256]{2,1,0:T(8,128)(2,1)} %fric.1) | copy-start | bytes 393220
  1.9 0.8 %copy-start.2 = (f32[32,256]{1,0:T(8,128)S(1)}, f32[32,256]{1,0:T(8,128)}, u32[]{:S(2)}) copy-start(f32[32,256]{1,0:T(8,128)} %thick.1) | copy-start | bytes 98308
  2.7 0.8 %copy-start.3 = (f32[32,256]{1,0:T(8,128)S(1)}, f32[32,256]{1,0:T(8,128)}, u32[]{:S(2)}) copy-start(f32[32,256]{1,0:T(8,128)} %surf.1) | copy-start | bytes 98308
  3.5 0.8 %copy-start.4 = (s32[32,256]{1,0:T(8,128)S(1)}, s32[32,256]{1,0:T(8,128)}, u32[]{:S(2)}) copy-start(s32[32,256]{1,0:T(8,128)} %ice.1) | copy-start | bytes 98308
  4.2 0.8 %copy-start.5 = (s32[32,256]{1,0:T(8,128)S(1)}, s32[32,256]{1,0:T(8,128)}, u32[]{:S(2)}) copy-start(s32[32,256]{1,0:T(8,128)} %ground.1) | copy-start | bytes 98308
  6.2 3.7 %collective-permute-start = (f32[8,8,128]{2,1,0:T(8,128)S(1)}, f32[8,8,128]{2,1,0:T(8,128)S(1)}, u32[]{:S(2)}, u32[]{:S(2)}) collective-permute-start(f32[8,8,128]{2,1,0:T(8,128)S(1)} %get-tuple-element.14), channel_id=1, source_target_pairs={{0,1},{1,2},{2,3},{4,5},{5,6},{6,7},{8,9},{9,10},{10,11},{12,13},{... | collective-permute-start | bytes 98312 | tf_op jit(solution)/shard_map/ppermute | solution.py:356
  8.6 5.2 %collective-permute-start.1 = (f32[8,8,128]{2,1,0:T(8,128)S(1)}, f32[8,8,128]{2,1,0:T(8,128)S(1)}, u32[]{:S(2)}, u32[]{:S(2)}) collective-permute-start(f32[8,8,128]{2,1,0:T(8,128)S(1)} %get-tuple-element.15), channel_id=1, source_target_pairs={{1,0},{2,1},{3,2},{5,4},{6,5},{7,6},{9,8},{10,9},{11,10},{13,12},{... | collective-permute-start | bytes 98312 | tf_op jit(solution)/shard_map/ppermute | solution.py:356
  14.0 8.0 %collective-permute-start.2 = (f32[5,4,8,384]{3,2,1,0:T(8,128)S(1)}, f32[5,4,8,384]{3,2,1,0:T(8,128)S(1)}, u32[]{:S(2)}, u32[]{:S(2)}) collective-permute-start(f32[5,4,8,384]{3,2,1,0:T(8,128)S(1)} %get-tuple-element.16), channel_id=1, source_target_pairs={{0,4},{4,8},{8,12},{12,16},{16,20},{20,24},{24,28},{1,5},{5,9},{9,... | collective-permute-start | bytes 737288 | tf_op jit(solution)/shard_map/ppermute | solution.py:356
  17.4 9.3 %collective-permute-start.3 = (f32[5,4,8,384]{3,2,1,0:T(8,128)S(1)}, f32[5,4,8,384]{3,2,1,0:T(8,128)S(1)}, u32[]{:S(2)}, u32[]{:S(2)}) collective-permute-start(f32[5,4,8,384]{3,2,1,0:T(8,128)S(1)} %get-tuple-element.17), channel_id=1, source_target_pairs={{4,0},{8,4},{12,8},{16,12},{20,16},{24,20},{28,24},{5,1},{9,5},{13... | collective-permute-start | bytes 737288 | tf_op jit(solution)/shard_map/ppermute | solution.py:356

commit v2 on v0

v2 whole, which is shorter than its diff:
```python
import functools

import jax
import jax.numpy as jnp
from jax import lax
from jax.experimental import pallas as pl
from jax.experimental.pallas import tpu as pltpu
from jax.sharding import PartitionSpec as P

strain_floor = 0.1
water_drag = 0.25
flow_power = 1.0 / 3.0

F32 = jnp.float32
DEPTH = 5
SIDE = 8
LANES = 128
PLANES = 4
GROUPS = LANES // SIDE
ROWS_PER_STRIP = GROUPS // PLANES
MOVING = DEPTH
DRAGGED = DEPTH - 2
SHARED = DEPTH - 1
TOTALS = 4


def vmem(shape):
    return pltpu.VMEM(shape, F32)


def call(kernel, outs, ins, scratch=(), flops=0, limit=24, aliases=None):
    specs = [pl.BlockSpec(memory_space=pltpu.HBM if space == "hbm" else pltpu.VMEM) for space in ins]
    out_specs = [
        pl.BlockSpec(memory_space=pltpu.HBM if isinstance(o, jax.ShapeDtypeStruct) else pltpu.VMEM) for o in outs
    ]
    return pl.pallas_call(
        kernel,
        out_shape=outs,
        in_specs=specs,
        out_specs=out_specs,
        scratch_shapes=scratch,
        input_output_aliases=aliases or {},
        cost_estimate=pl.CostEstimate(flops=flops, bytes_accessed=flops // 8, transcendentals=0),
        compiler_params=pltpu.CompilerParams(vmem_limit_bytes=limit * 1024 * 1024),
    )


def lane_iota(shape):
    return lax.broadcasted_iota(jnp.int32, shape, len(shape) - 1)


def sublane_iota(shape):
    return lax.broadcasted_iota(jnp.int32, shape, len(shape) - 2)


def swaps(axis):
    count = lax.axis_size(axis)
    inner = [(i, i ^ 1) if i ^ 1 < count else (i, i) for i in range(count)]
    if count % 2:
        outer = [(i, i + 1) if i % 2 else (i, i - 1) if i else (i, i) for i in range(count)]
    else:
        outer = [(i, (i + 1) % count) if i % 2 else (i, (i - 1) % count) for i in range(count)]
    return inner, outer


def neighbours(axis):
    index, count = lax.axis_index(axis), lax.axis_size(axis)
    lower = lax.rem(index, 2) == 0
    inner = jnp.logical_or(jnp.logical_not(lower), index + 1 < count)
    outer = jnp.where(lower, index > 0, index + 1 < count)
    return lower, inner, outer


def either(flag, first, second):
    return jnp.where(flag, first, second)


def pack_kernel(
    vel, fric, thick, surf, ice, ground, own, to_inner, to_outer,
    vel_in, fric_in, thick_in, surf_in, ice_in, ground_in, friction32, sems,
):
    members, rows, cols = fric.shape
    tiles = cols // LANES
    copies = [
        pltpu.make_async_copy(source, target, sems.at[k])
        for k, (source, target) in enumerate(
            [(fric, fric_in), (ice, ice_in), (ground, ground_in), (thick, thick_in), (surf, surf_in)]
            + [(vel.at[:, pl.ds(t * LANES, LANES)], vel_in.at[t]) for t in range(tiles)]
        )
    ]
    for copy in copies:
        copy.start()
    lower, _, _ = neighbours("gy")
    group = lane_iota((members, LANES)) // SIDE
    sub = sublane_iota((members, LANES))
    for copy in copies[:5]:
        copy.wait()
    for t in range(tiles):
        friction32[t] = fric_in[:, :, t * LANES : (t + 1) * LANES].astype(F32).reshape(members * rows, LANES)
    for copy in copies[5:]:
        copy.wait()
    near = {}
    for base in range(0, rows, 8):
        for t in range(tiles):
            part = slice(t * LANES, (t + 1) * LANES)
            icef = ice_in[base : base + 8, part].astype(F32)
            near[base, t] = (
                icef,
                icef * ground_in[base : base + 8, part].astype(F32),
                icef * thick_in[base : base + 8, part],
                surf_in[base : base + 8, part],
            )
    for strip in range(rows // ROWS_PER_STRIP):
        heads = jnp.zeros((members, LANES), F32)
        tails = jnp.zeros((members, LANES), F32)
        for step in range(ROWS_PER_STRIP):
            row = strip * ROWS_PER_STRIP + step
            at = row % 8
            for t in range(tiles):
                part = slice(t * LANES, (t + 1) * LANES)
                icef, grounded, thin, top = (value[at : at + 1, :] for value in near[row - at, t])
                field_u = vel_in[t, pl.ds(row, members, stride=2 * rows), :] * icef
                field_v = vel_in[t, pl.ds(rows + row, members, stride=2 * rows), :] * icef
                rough = friction32[t, pl.ds(row, members, stride=rows), :]
                drag = grounded * rough + water_drag * icef
                shared = jnp.where(sub == 0, thin, jnp.where(sub == 1, top, jnp.where(sub == 2, icef, 0.0)))
                for plane, value in enumerate((field_u, field_v, drag, shared)):
                    own[row, plane, :, part] = value
                    place = step * PLANES + plane
                    if t == 0:
                        head = pltpu.roll(value, place * SIDE, 1) if place else value
                        heads = jnp.where(group == place, head, heads)
                    if t == tiles - 1:
                        tail = pltpu.roll(value, (place + 1) * SIDE, 1) if place != GROUPS - 1 else value
                        tails = jnp.where(group == place, tail, tails)
        to_inner[strip] = either(lower, tails, heads)
        to_outer[strip] = either(lower, heads, tails)


def side_strips(from_inner, from_outer):
    lower, has_inner, has_outer = neighbours("gy")

    def strips(strip):
        inner = jnp.where(has_inner, from_inner[strip], 0.0)
        outer = jnp.where(has_outer, from_outer[strip], 0.0)
        return either(lower, outer, inner), either(lower, inner, outer)

    return strips


def unpacked(left, right, place, lane):
    if place:
        right = pltpu.roll(right, LANES - place * SIDE, 1)
    if place != GROUPS - 1:
        left = pltpu.roll(left, LANES - (place + 1) * SIDE, 1)
    return jnp.where(lane < SIDE, right, jnp.where(lane >= LANES - SIDE, left, 0.0))


def edge_items():
    moving = [(plane, k) for k in range(MOVING) for plane in (0, 1)]
    return moving + [(2, k) for k in range(DRAGGED)] + [(3, k) for k in range(0, SHARED, 2)]


def edge_tiles(cols):
    items = len(edge_items())
    per_tile = GROUPS // 2
    return items * (cols // LANES) + -(-items // per_tile)


def edge_kernel(own, from_inner, from_outer, to_inner, to_outer, field):
    rows, _, members, cols = own.shape
    tiles = cols // LANES
    lane = lane_iota((members, LANES))
    sub = sublane_iota((members, LANES))
    strips = side_strips(from_inner, from_outer)
    lower, _, _ = neighbours("gx")
    items = edge_items()
    per_tile = GROUPS // 2

    for first in (0, rows - 2 * ROWS_PER_STRIP):
        for strip in (first // ROWS_PER_STRIP, first // ROWS_PER_STRIP + 1):
            left, right = strips(strip)
            for step in range(ROWS_PER_STRIP):
                for plane in range(PLANES):
                    field[strip * ROWS_PER_STRIP + step, plane] = unpacked(
                        left, right, step * PLANES + plane, lane
                    )

    def tile_of(up, plane, k, t):
        depth = (MOVING, MOVING, DRAGGED, SHARED)[plane]
        row = k if up else rows - depth + k

        def one(row):
            return own[row, plane, :, t * LANES : (t + 1) * LANES] if t < tiles else field[row, plane]

        if plane < 3:
            return one(row)
        return jnp.where(sub < 4, one(row), pltpu.roll(one(row + 1), 4, 0))

    for target, up in ((to_inner, False), (to_outer, True)):
        at = 0
        sides = None
        for j, (plane, k) in enumerate(items):
            for t in range(tiles):
                target[at] = either(lower, tile_of(up, plane, k, t), tile_of(not up, plane, k, t))
                at += 1
            side = either(lower, tile_of(up, plane, k, tiles), tile_of(not up, plane, k, tiles))
            side = pltpu.roll(side, (SIDE + 2 * SIDE * (j % per_tile)) % LANES, 1)
            if j % per_tile == 0:
                sides = side
            else:
                sides = jnp.where(lane // (2 * SIDE) == j % per_tile, side, sides)
            if j % per_tile == per_tile - 1 or j == len(items) - 1:
                target[len(items) * tiles + j // per_tile] = sides


def stages(field, store, rows, members, cols):
    visc, sx, sy, sz, tx, ty, tz, rest, inverse, along, across = store
    wide = cols + LANES

    def spread(row, sub):
        return jnp.broadcast_to(field[row + DEPTH, 3, sub : sub + 1, :], (members, wide))

    def after(value):
        return pltpu.roll(value, wide - 1, 1)

    def before(value):
        return pltpu.roll(value, 1, 1)

    def strains(ref, row):
        row = row + DEPTH
        u, v = ref[row, 0], ref[row, 1]
        return (
            ref[row + 1, 0] - ref[row - 1, 0],
            after(v) - before(v),
            (after(u) - before(u)) + (ref[row + 1, 1] - ref[row - 1, 1]),
        )

    def stress(x, y, z, row, strain_u, strain_v, strain_c, nu):
        half = 0.5 * nu
        x[row + DEPTH] = half * (2.0 * strain_u + strain_v)
        y[row + DEPTH] = half * (strain_u + 2.0 * strain_v)
        z[row + DEPTH] = half * (0.5 * strain_c)

    def divergence(x, y, z, row):
        row = row + DEPTH
        shear, normal = z[row], y[row]
        return (
            (x[row + 1] - x[row - 1]) + (after(shear) - before(shear)),
            (after(normal) - before(normal)) + (z[row + 1] - z[row - 1]),
        )

    def viscosity(row):
        su, sv, sc = strains(field, row)
        square = 0.25 * (su * su + sv * sv + su * sv + 0.25 * (sc * sc)) + strain_floor
        nu = (0.5 * spread(row, 0)) * jnp.exp(-flow_power * jnp.log(square))
        visc[row + DEPTH] = nu
        stress(sx, sy, sz, row, su, sv, sc, nu)

    def reciprocal(value):
        guess = pltpu.reciprocal(value, approx=True)
        return guess * (2.0 - value * guess)

    def residual(row):
        div_u, div_v = divergence(sx, sy, sz, row)
        at = row + DEPTH
        drag = field[at, 2]
        icef = spread(row, 2)
        top = spread(row, 1)
        half = 0.5 * spread(row, 0)
        force_u = half * (spread(row - 1, 1) - spread(row + 1, 1))
        force_v = half * (before(top) - after(top))
        res_u = force_u - (drag * field[at, 0] - icef * div_u)
        res_v = force_v - (drag * field[at, 1] - icef * div_v)
        nu = visc[at]
        near_rows = visc[at + 1] + visc[at - 1]
        near_cols = after(nu) + before(nu)
        on = icef > 0.0
        inv_u = reciprocal(jnp.where(on, near_rows + 0.25 * near_cols + drag, 1.0))
        inv_v = reciprocal(jnp.where(on, near_cols + 0.25 * near_rows + drag, 1.0))
        rest[at, 0] = res_u
        rest[at, 1] = res_v
        inverse[at, 0] = inv_u
        inverse[at, 1] = inv_v
        along[at, 0] = res_u * inv_u
        along[at, 1] = res_v * inv_v

    def direction(row):
        su, sv, sc = strains(along, row)
        stress(tx, ty, tz, row, su, sv, sc, visc[row + DEPTH])

    def image(row, totals):
        div_u, div_v = divergence(tx, ty, tz, row)
        at = row + DEPTH
        drag = field[at, 2]
        icef = spread(row, 2)
        dir_u, dir_v = along[at, 0], along[at, 1]
        res_u, res_v = rest[at, 0], rest[at, 1]
        off_u = drag * dir_u - icef * div_u - res_u
        off_v = drag * dir_v - icef * div_v - res_v
        new_u = off_u * inverse[at, 0]
        new_v = off_v * inverse[at, 1]
        across[at, 0] = new_u
        across[at, 1] = new_v
        if 0 <= row < rows:
            totals[0] += (res_u * dir_u + res_v * dir_v)[:, :cols]
            totals[1] += (res_u * new_u + res_v * new_v)[:, :cols]
            totals[2] += (off_u * new_u + off_v * new_v)[:, :cols]

    def energy(row, totals):
        su, sv, sc = strains(across, row)
        at = row + DEPTH
        u, v = across[at, 0], across[at, 1]
        power = field[at, 2] * (u * u + v * v) + visc[at] * (su * su + su * sv + sv * sv + 0.25 * (sc * sc))
        totals[3] += power[:, :cols]

    return viscosity, residual, direction, image, energy


def run(steps, totals, ranges):
    viscosity, residual, direction, image, energy = steps
    for step, over in zip((viscosity, residual, direction), ranges[:3], strict=True):
        for row in over:
            step(row)
    for step, over in zip((image, energy), ranges[3:], strict=True):
        for row in over:
            step(row, totals)


def inner_ranges(rows):
    return [range(k, rows - k) for k in range(1, 6)]


def inner_kernel(own, from_inner, from_outer, field, *rest):
    store, totals_ref = rest[:11], rest[11]
    rows, _, members, cols = own.shape
    lane = lane_iota((members, LANES))
    strips = side_strips(from_inner, from_outer)
    for strip in range(rows // ROWS_PER_STRIP):
        left, right = strips(strip)
        for step in range(ROWS_PER_STRIP):
            row = strip * ROWS_PER_STRIP + step
            for plane in range(PLANES):
                field[row + DEPTH, plane, :, :cols] = own[row, plane]
                field[row + DEPTH, plane, :, cols:] = unpacked(left, right, step * PLANES + plane, lane)
    totals = [jnp.zeros((members, cols), F32) for _ in range(TOTALS)]
    run(stages(field, store, rows, members, cols), totals, inner_ranges(rows))
    for k, total in enumerate(totals):
        totals_ref[k] = total


def outer_kernel(from_inner, from_outer, totals_ref, *refs):
    sums, field, store = refs[12], refs[13], refs[14:25]
    high, _, members, wide = field.shape
    rows, cols = high - 2 * DEPTH, wide - LANES
    tiles = cols // LANES
    lane = lane_iota((members, LANES))
    items = edge_items()
    per_tile = GROUPS // 2
    lower, has_inner, has_outer = neighbours("gx")

    def both(k):
        inner = jnp.where(has_inner, from_inner[k], 0.0)
        outer = jnp.where(has_outer, from_outer[k], 0.0)
        return either(lower, outer, inner), either(lower, inner, outer)

    sides = [both(len(items) * tiles + k) for k in range(-(-len(items) // per_tile))]
    for j, (plane, k) in enumerate(items):
        depth = (MOVING, MOVING, DRAGGED, SHARED)[plane]
        ups = [DEPTH - depth + k]
        downs = [DEPTH + rows + k]
        if plane == 3:
            ups, downs = [ups[0], ups[0] + 1], [downs[0], downs[0] + 1]
        values = [both(j * tiles + t) for t in range(tiles)]
        shift = (LANES - (SIDE + 2 * SIDE * (j % per_tile))) % LANES
        ends = []
        for side in sides[j // per_tile]:
            side = pltpu.roll(side, shift, 1) if shift else side
            ends.append(jnp.where((lane < SIDE) | (lane >= LANES - SIDE), side, 0.0))
        values.append(tuple(ends))
        for t, pair in enumerate(values):
            for value, places in zip(pair, (ups, downs), strict=True):
                for n, place in enumerate(places):
                    field[place, plane, :, t * LANES : (t + 1) * LANES] = (
                        pltpu.roll(value, 4, 0) if n else value
                    )
    inner = inner_ranges(rows)
    ranges = [
        [row for row in range(k, rows - k) if row not in inner[k + 4]] for k in range(-4, 1)
    ]
    totals = [totals_ref[k] for k in range(TOTALS)]
    run(stages(field, store, rows, members, cols), totals, ranges)
    sub = sublane_iota((members, LANES))
    row = jnp.zeros((members, LANES), F32)
    for k, total in enumerate(totals):
        row = row + jnp.where(lane == sub + members * k, jnp.sum(total, axis=1, keepdims=True), 0.0)
    row = jnp.sum(row, axis=0, keepdims=True)
    sums[...] = jnp.broadcast_to(row[None], sums.shape)


def final_kernel(parts, field, along, across, out, out_tiles, sems):
    high, _, members, wide = field.shape
    rows, cols = high - 2 * DEPTH, wide - LANES
    total = jnp.sum(parts[...], axis=0)
    spread = jnp.broadcast_to(total, (members, LANES))
    lane = lane_iota((members, LANES))
    sub = sublane_iota((members, LANES))
    norm, cross, square, power = (
        jnp.sum(jnp.where(lane == sub + members * k, spread, 0.0), axis=1, keepdims=True)
        for k in range(TOTALS)
    )
    k1, k2, k3 = cross / norm, square / norm, power / norm
    scale = 1.0 + k1
    first = 1.0 / scale
    beta = (k2 - k1 * k1) * first * first
    curve = (k1 * k1 * scale - 2.0 * k1 * (k1 + k2) + k3) * first * first - beta * beta * scale
    second = jnp.where(curve > 0.0, beta / jnp.where(curve > 0.0, curve, 1.0), 0.0)
    on_along = jnp.broadcast_to(first + second * (k1 * first + beta), (members, LANES))
    on_across = jnp.broadcast_to(second * first, (members, LANES))
    copies = []
    for t in range(cols // LANES):
        place = slice(t * LANES, (t + 1) * LANES)
        for row in range(rows):
            for part in range(2):
                out_tiles[t, pl.ds(part * rows + row, members, stride=2 * rows), :] = (
                    field[DEPTH + row, part, :, place]
                    + on_along * along[DEPTH + row, part, :, place]
                    - on_across * across[DEPTH + row, part, :, place]
                )
        copies.append(
            pltpu.make_async_copy(out_tiles.at[t], out.at[:, pl.ds(t * LANES, LANES)], sems.at[t])
        )
        copies[-1].start()
    for copy in copies:
        copy.wait()


def per_device(velocity_guess, friction, thickness, surface, ice_mask, grounded_mask):
    members, parts, rows, cols = velocity_guess.shape
    devices = lax.axis_size(("gx", "gy"))
    wide = cols + LANES
    high = rows + 2 * DEPTH
    tiles = cols // LANES
    flat = members * parts * rows
    strip = vmem((rows // ROWS_PER_STRIP, members, LANES))
    own, side_inner, side_outer = call(
        pack_kernel,
        [vmem((rows, PLANES, members, cols)), strip, strip],
        ["hbm"] * 6,
        [
            pltpu.VMEM((tiles, flat, LANES), F32),
            pltpu.VMEM((members, rows, cols), friction.dtype),
            pltpu.VMEM((rows, cols), F32),
            pltpu.VMEM((rows, cols), F32),
            pltpu.VMEM((rows, cols), jnp.int32),
            pltpu.VMEM((rows, cols), jnp.int32),
            pltpu.VMEM((tiles, members * rows, LANES), F32),
            pltpu.SemaphoreType.DMA((5 + tiles,)),
        ],
        limit=60,
    )(velocity_guess.reshape(flat, cols), friction, thickness, surface, ice_mask, grounded_mask)
    inner, outer = swaps("gy")
    side_inner = lax.ppermute(side_inner, "gy", inner)
    side_outer = lax.ppermute(side_outer, "gy", outer)

    edge = vmem((edge_tiles(cols), members, LANES))
    edge_inner, edge_outer = call(
        edge_kernel, [edge, edge], ["vmem"] * 3, [pltpu.VMEM((rows, PLANES, members, LANES), F32)]
    )(own, side_inner, side_outer)
    inner, outer = swaps("gx")
    edge_outer = lax.ppermute(edge_outer, "gx", outer)
    edge_inner = lax.ppermute(edge_inner, "gx", inner)

    one, two = vmem((high, members, wide)), vmem((high, 2, members, wide))
    held = [vmem((high, PLANES, members, wide))] + [one] * 7 + [two] * 4
    *held_now, totals = call(
        inner_kernel,
        held + [vmem((TOTALS, members, cols))],
        ["vmem"] * 3,
        flops=rows * members * wide * 300,
    )(own, side_inner, side_outer)
    sums, *held_now = call(
        outer_kernel,
        [vmem((devices, 1, LANES))] + held,
        ["vmem"] * 15,
        aliases={3 + k: 1 + k for k in range(12)},
    )(edge_inner, edge_outer, totals, *held_now)
    shares = lax.all_to_all(sums, ("gx", "gy"), 0, 0, tiled=True)
    (out,) = call(
        final_kernel,
        [jax.ShapeDtypeStruct((flat, cols), F32)],
        ["vmem"] * 4,
        [pltpu.VMEM((tiles, flat, LANES), F32), pltpu.SemaphoreType.DMA((tiles,))],
    )(shares, held_now[0], held_now[-2], held_now[-1])
    return out.reshape(members, parts, rows, cols)


def solution(mesh):
    placed = (
        P(None, None, "gx", "gy"),
        P(None, "gx", "gy"),
        P("gx", "gy"),
        P("gx", "gy"),
        P("gx", "gy"),
        P("gx", "gy"),
    )
    return jax.shard_map(
        per_device, mesh=mesh, in_specs=placed, out_specs=P(None, None, "gx", "gy"), check_vma=False
    )
```

time: 281 us -> 31.2 us (0.11)
  blocking collectives: 138 us -> 11.9 us
  starting transfers between devices: 88.9 us -> 8.39 us
  waiting for transfers between devices: 33.1 us -> 3.86 us
  other arithmetic: 13.5 us -> 0 us
  Pallas kernels: 0 us -> 6.97 us
  local copies, waits for them, and re-layouts: 5.37 us -> 0 us
    psum x3 -> x0, blocking collectives: 138 us -> none  [member_dot(): return lax.psum(jnp.sum(left * right, axis=(1, 2, 3)), ('gx', 'gy'))]
    ppermute x28 -> x4, starting transfers between devices: 88.9 us -> 8.39 us  [the longest x1 3.57 us: per_device(): edge_outer = lax.ppermute(edge_outer, 'gx', outer)]
    ppermute x28 -> x4, waiting for transfers between devices: 33.1 us -> 3.86 us  [the longest x1 2.09 us: per_device(): edge_outer = lax.ppermute(edge_outer, 'gx', outer)]
    all_to_all x0 -> x1, blocking collectives: none -> 11.9 us  [per_device(): shares = lax.all_to_all(sums, ('gx', 'gy'), 0, 0, tiled=True)]
    pallas_call x0 -> x5, Pallas kernels: none -> 6.97 us  [the longest x1 2.5 us: per_device(): call(inner_kernel, held + [vmem((TOTALS, members, cols))], ['vmem'] * 3,...]
    mul x5 -> x0, other arithmetic: 3.12 us -> none  [the longest x3 1.71 us: stresses(): visc * (4.0 * ka + 2.0 * kb)]
    another operation x11 -> x0, other arithmetic: 3 us -> none  [the longest x6 2.25 us: divergence(): return jnp.stack([out_u, out_v], 1)]
  transfers between devices with their start and end apart: 28 -> 4, of which waited for: 15 -> 3; matrix products, arithmetic and copies ran while one was open for 0% -> 0% of each run, Pallas kernels for 0% -> 8%
where the time goes in v2:
time: 31.2 us; the launch traced here: 31.1 us
  blocking collectives  11.9 us (38%)
  starting transfers between devices  8.39 us (27%)
  Pallas kernels  6.97 us (22%)
  waiting for transfers between devices  3.86 us (12%)
    all_to_all x1, blocking collectives, per_device(): shares = lax.all_to_all(sums, ('gx', 'gy'), 0, 0, tiled=True)  11.9 us
    ppermute x1, starting transfers between devices, per_device(): edge_outer = lax.ppermute(edge_outer, 'gx', outer)  3.57 us
    ppermute x1, starting transfers between devices, per_device(): side_outer = lax.ppermute(side_outer, 'gy', outer)  2.64 us
    pallas_call x1, Pallas kernels, per_device(): call(inner_kernel, held + [vmem((TOTALS, members, cols))], ['vmem'] * 3,...  2.5 us
    ppermute x1, waiting for transfers between devices, per_device(): edge_outer = lax.ppermute(edge_outer, 'gx', outer)  2.09 us
    pallas_call x1, Pallas kernels, per_device(): call(pack_kernel, [vmem((rows, PLANES, members, cols)), strip, strip], ['...  1.89 us
    ppermute x1, waiting for transfers between devices, per_device(): side_outer = lax.ppermute(side_outer, 'gy', outer)  1.67 us
    ppermute x1, starting transfers between devices, per_device(): edge_inner = lax.ppermute(edge_inner, 'gx', inner)  1.66 us
  transfers between devices with their start and end apart: 4, of which 3 were waited for; matrix products, arithmetic and copies ran while one was open for 0% of the time, Pallas kernels for 8%

profile of v2, /device:TPU:0, one launch (start us, length us, event | category | flops | bytes accessed | tf_op | source)
XLA Modules:
  0.0 31.1 jit_solution(7095787498250095718)
XLA Ops:
  0.0 1.9 %shard_map.64 = (f32[32,4,8,256]{3,2,1,0:T(8,128)S(1)}, f32[8,8,128]{2,1,0:T(8,128)S(1)}, f32[8,8,128]{2,1,0:T(8,128)S(1)}) custom-call(f32[512,256]{1,0:T(8,128)} %bitcast.2, bf16[8,32,256]{2,1,0:T(8,128)(2,1)} %fric.1, f32[32,256]{1,0:T(8,128)} %thick.1, f32[32,256]{1,0:T(8,128)} %surf.1, s32[32,256]{1,0:T(8,128)} %ice.1, s32[32,256]{1,0:T(8,128)} %ground.1), custom_call_target="tpu_custom_call" | custom-call | tf_op jit(solution)/shard_map/pallas_call | solution.py:446
  1.9 0.5 %collective-permute-start = (f32[8,8,128]{2,1,0:T(8,128)S(1)}, f32[8,8,128]{2,1,0:T(8,128)S(1)}, u32[]{:S(2)}, u32[]{:S(2)}) collective-permute-start(f32[8,8,128]{2,1,0:T(8,128)S(1)} %get-tuple-element.28), channel_id=1, source_target_pairs={{0,1},{1,0},{2,3},{3,2},{4,5},{5,4},{6,7},{7,6},{8,9},{9,8},{10,11... | collective-permute-start | bytes 98312 | tf_op jit(solution)/shard_map/ppermute | solution.py:463
  2.4 2.6 %collective-permute-start.1 = (f32[8,8,128]{2,1,0:T(8,128)S(1)}, f32[8,8,128]{2,1,0:T(8,128)S(1)}, u32[]{:S(2)}, u32[]{:S(2)}) collective-permute-start(f32[8,8,128]{2,1,0:T(8,128)S(1)} %get-tuple-element.29), channel_id=1, source_target_pairs={{0,3},{1,2},{2,1},{3,0},{4,7},{5,6},{6,5},{7,4},{8,11},{9,10},{10,... | collective-permute-start | bytes 98312 | tf_op jit(solution)/shard_map/ppermute | solution.py:464
  5.1 0.0 collective-permute-done.from_inner
  5.1 1.7 %collective-permute-done.1.from_outer = f32[8,8,128]{2,1,0:T(8,128)S(1)} collective-permute-done((f32[8,8,128]{2,1,0:T(8,128)S(1)}, f32[8,8,128]{2,1,0:T(8,128)S(1)}, u32[]{:S(2)}, u32[]{:S(2)}) %collective-permute-start.1) | collective-permute-done | bytes 32800 | tf_op jit(solution)/shard_map/ppermute | solution.py:464
  6.7 0.2 shard_map.65
  6.9 1.7 %collective-permute-start.2 = (f32[32,8,128]{2,1,0:T(8,128)S(1)}, f32[32,8,128]{2,1,0:T(8,128)S(1)}, u32[]{:S(2)}, u32[]{:S(2)}) collective-permute-start(f32[32,8,128]{2,1,0:T(8,128)S(1)} %get-tuple-element.30), channel_id=1, source_target_pairs={{0,4},{4,0},{8,12},{12,8},{16,20},{20,16},{24,28},{28,24},{1,5},{5... | collective-permute-start | bytes 393224 | tf_op jit(solution)/shard_map/ppermute | solution.py:472
  8.6 3.6 %collective-permute-start.3 = (f32[32,8,128]{2,1,0:T(8,128)S(1)}, f32[32,8,128]{2,1,0:T(8,128)S(1)}, u32[]{:S(2)}, u32[]{:S(2)}) collective-permute-start(f32[32,8,128]{2,1,0:T(8,128)S(1)} %get-tuple-element.31), channel_id=1, source_target_pairs={{0,28},{4,8},{8,4},{12,16},{16,12},{20,24},{24,20},{28,0},{1,29},{... | collective-permute-start | bytes 393224 | tf_op jit(solution)/shard_map/ppermute | solution.py:471
  12.2 2.5 %shard_map.66 = (f32[42,4,8,384]{3,2,1,0:T(8,128)S(1)}, f32[42,8,384]{2,1,0:T(8,128)S(1)}, f32[42,8,384]{2,1,0:T(8,128)S(1)}, f32[42,8,384]{2,1,0:T(8,128)S(1)},...) custom-call(f32[32,4,8,256]{3,2,1,0:T(8,128)S(1)} %get-tuple-element, ...), custom_call_target="tpu_custom_call" | custom-call | flops 29491200 | bytes 3686400 | tf_op jit(solution)/shard_map/pallas_call | solution.py:476
  14.7 0.1 collective-permute-done.2.from_inner
  14.8 2.1 %collective-permute-done.3.from_outer = f32[32,8,128]{2,1,0:T(8,128)S(1)} collective-permute-done((f32[32,8,128]{2,1,0:T(8,128)S(1)}, f32[32,8,128]{2,1,0:T(8,128)S(1)}, u32[]{:S(2)}, u32[]{:S(2)}) %collective-permute-start.3) | collective-permute-done | bytes 131104 | tf_op jit(solution)/shard_map/ppermute | solution.py:471
  16.9 1.0 %shard_map.67 = (f32[32,1,128]{2,1,0:T(1,128)S(1)}, f32[42,4,8,384]{3,2,1,0:T(8,128)S(1)}, f32[42,8,384]{2,1,0:T(8,128)S(1)}, f32[42,8,384]{2,1,0:T(8,128)S(1)},...) custom-call(f32[32,8,128]{2,1,0:T(8,128)S(1)} %collective-permute-do, ...), custom_call_target="tpu_custom_call", output_to_operand_aliasing={{1}: (3, {}), {2}: (4, {}), {3}: (5, {}), {4}: (6, {}), {5}... | custom-call | tf_op jit(solution)/shard_map/pallas_call | solution.py:482
  17.9 11.9 %all_to_all.5.parts = f32[32,1,128]{2,1,0:T(1,128)S(1)} all-to-all(f32[32,1,128]{2,1,0:T(1,128)S(1)} %get-tuple-element.45), channel_id=1, replica_groups=mesh['gx'=8,'gy'=4] {'gx','gy'}, dimensions={0} | all-to-all | bytes 32768 | tf_op jit(solution)/shard_map/all_to_all | solution.py:488
  29.8 1.3 %shard_map.68 = f32[512,256]{1,0:T(8,128)} custom-call(f32[32,1,128]{2,1,0:T(1,128)S(1)} %all_to_all.5.parts, f32[42,4,8,384]{3,2,1,0:T(8,128)S(1)} %get-tuple-element.46.field, f32[42,2,8,384]{3,2,1,0:T(8,128)S(1)} %get-tuple-element.47.along, f32[42,2,8,384]{3,2,1,0:T(8,128)S(1)} %get-tuple-element.48.across), custom_call_target="tpu_custom_call" | custom-call | tf_op jit(solution)/shard_map/pallas_call | solution.py:489
Async XLA Ops:
  1.9 3.2 %collective-permute-start = (f32[8,8,128]{2,1,0:T(8,128)S(1)}, f32[8,8,128]{2,1,0:T(8,128)S(1)}, u32[]{:S(2)}, u32[]{:S(2)}) collective-permute-start(f32[8,8,128]{2,1,0:T(8,128)S(1)} %get-tuple-element.28), channel_id=1, source_target_pairs={{0,1},{1,0},{2,3},{3,2},{4,5},{5,4},{6,7},{7,6},{8,9},{9,8},{10,11... | collective-permute-start | bytes 98312 | tf_op jit(solution)/shard_map/ppermute | solution.py:463
  2.4 4.3 %collective-permute-start.1 = (f32[8,8,128]{2,1,0:T(8,128)S(1)}, f32[8,8,128]{2,1,0:T(8,128)S(1)}, u32[]{:S(2)}, u32[]{:S(2)}) collective-permute-start(f32[8,8,128]{2,1,0:T(8,128)S(1)} %get-tuple-element.29), channel_id=1, source_target_pairs={{0,3},{1,2},{2,1},{3,0},{4,7},{5,6},{6,5},{7,4},{8,11},{9,10},{10,... | collective-permute-start | bytes 98312 | tf_op jit(solution)/shard_map/ppermute | solution.py:464
  6.9 7.8 %collective-permute-start.2 = (f32[32,8,128]{2,1,0:T(8,128)S(1)}, f32[32,8,128]{2,1,0:T(8,128)S(1)}, u32[]{:S(2)}, u32[]{:S(2)}) collective-permute-start(f32[32,8,128]{2,1,0:T(8,128)S(1)} %get-tuple-element.30), channel_id=1, source_target_pairs={{0,4},{4,0},{8,12},{12,8},{16,20},{20,16},{24,28},{28,24},{1,5},{5... | collective-permute-start | bytes 393224 | tf_op jit(solution)/shard_map/ppermute | solution.py:472
  8.6 8.3 %collective-permute-start.3 = (f32[32,8,128]{2,1,0:T(8,128)S(1)}, f32[32,8,128]{2,1,0:T(8,128)S(1)}, u32[]{:S(2)}, u32[]{:S(2)}) collective-permute-start(f32[32,8,128]{2,1,0:T(8,128)S(1)} %get-tuple-element.31), channel_id=1, source_target_pairs={{0,28},{4,8},{8,4},{12,16},{16,12},{20,24},{24,20},{28,0},{1,29},{... | collective-permute-start | bytes 393224 | tf_op jit(solution)/shard_map/ppermute | solution.py:471

commit v3 on v2

v3 whole, which is shorter than its diff:
```python
import functools

import jax
import jax.numpy as jnp
from jax import lax
from jax.experimental import pallas as pl
from jax.experimental.pallas import tpu as pltpu
from jax.sharding import PartitionSpec as P

strain_floor = 0.1
water_drag = 0.25
flow_power = 1.0 / 3.0

F32 = jnp.float32
DEPTH = 5
SIDE = 8
CORNER = 4
BLOCK = 8
LANES = 128
PLANES = 4
GROUPS = LANES // SIDE
ROWS_PER_STRIP = GROUPS // PLANES
MOVING = DEPTH
DRAGGED = DEPTH - 2
SHARED = DEPTH - 1
TOTALS = 4


def vmem(shape):
    return pltpu.VMEM(shape, F32)


def call(kernel, outs, ins, scratch=(), flops=0, limit=24, aliases=None):
    specs = [pl.BlockSpec(memory_space=pltpu.HBM if space == "hbm" else pltpu.VMEM) for space in ins]
    out_specs = [
        pl.BlockSpec(memory_space=pltpu.HBM if isinstance(o, jax.ShapeDtypeStruct) else pltpu.VMEM) for o in outs
    ]
    return pl.pallas_call(
        kernel,
        out_shape=outs,
        in_specs=specs,
        out_specs=out_specs,
        scratch_shapes=scratch,
        input_output_aliases=aliases or {},
        cost_estimate=pl.CostEstimate(flops=flops, bytes_accessed=flops // 8, transcendentals=0),
        compiler_params=pltpu.CompilerParams(vmem_limit_bytes=limit * 1024 * 1024),
    )


def lane_iota(shape):
    return lax.broadcasted_iota(jnp.int32, shape, len(shape) - 1)


def sublane_iota(shape):
    return lax.broadcasted_iota(jnp.int32, shape, len(shape) - 2)


def swaps(axis):
    count = lax.axis_size(axis)
    inner = [(i, i ^ 1) if i ^ 1 < count else (i, i) for i in range(count)]
    if count % 2:
        outer = [(i, i + 1) if i % 2 else (i, i - 1) if i else (i, i) for i in range(count)]
    else:
        outer = [(i, (i + 1) % count) if i % 2 else (i, (i - 1) % count) for i in range(count)]
    return inner, outer


def row_swaps():
    side = lax.axis_size("gy")
    inner, outer = swaps("gx")
    beside = dict(swaps("gy")[0])
    inner = [(i * side + k, j * side + k) for i, j in inner for k in range(side)]
    outer = [
        (i * side + k, j * side + k) if abs(i - j) == 1 else (i * side + k, i * side + beside[k])
        for i, j in outer
        for k in range(side)
    ]
    return inner, outer


def neighbours(axis):
    index, count = lax.axis_index(axis), lax.axis_size(axis)
    lower = lax.rem(index, 2) == 0
    inner = jnp.logical_or(jnp.logical_not(lower), index + 1 < count)
    outer = jnp.where(lower, index > 0, index + 1 < count)
    return lower, inner, outer


def either(flag, first, second):
    return jnp.where(flag, first, second)


def edge_items():
    moving = [(plane, k) for k in range(MOVING) for plane in (0, 1)]
    return moving + [(2, k) for k in range(DRAGGED)] + [(3, 0)]


def edge_row(plane, k, rows, up):
    return k if up else rows - (MOVING, MOVING, DRAGGED, SHARED)[plane] + k


def pack_kernel(
    vel, fric, thick, surf, ice, ground, own, to_inner, to_outer, edge_inner, edge_outer,
    vel_in, fric_in, thick_in, surf_in, ice_in, ground_in, friction32, sems,
):
    members, rows, cols = fric.shape
    tiles, blocks = cols // LANES, rows // BLOCK
    small = [
        pltpu.make_async_copy(source, target, sems.at[k])
        for k, (source, target) in enumerate(
            [(fric, fric_in), (ice, ice_in), (ground, ground_in), (thick, thick_in), (surf, surf_in)]
        )
    ]
    large = [
        [
            pltpu.make_async_copy(
                vel.at[:, pl.ds(b * BLOCK, BLOCK), pl.ds(t * LANES, LANES)],
                vel_in.at[t, b].reshape(2 * members, BLOCK, LANES),
                sems.at[len(small) + b * tiles + t],
            )
            for t in range(tiles)
        ]
        for b in range(blocks)
    ]
    for copy in small + large[0] + large[-1] + sum(large[1:-1], []):
        copy.start()
    lower, _, _ = neighbours("gy")
    first, _, _ = neighbours("gx")
    group = lane_iota((members, LANES)) // SIDE
    sub = sublane_iota((members, LANES))
    for copy in small:
        copy.wait()
    for t in range(tiles):
        friction32[t] = fric_in[:, :, t * LANES : (t + 1) * LANES].astype(F32).reshape(members * rows, LANES)
    for b in [0, blocks - 1] + list(range(1, blocks - 1)):
        for copy in large[b]:
            copy.wait()
        base = b * BLOCK
        near = []
        for t in range(tiles):
            part = slice(t * LANES, (t + 1) * LANES)
            icef = ice_in[base : base + BLOCK, part].astype(F32)
            near.append(
                (
                    icef,
                    icef * ground_in[base : base + BLOCK, part].astype(F32),
                    icef * thick_in[base : base + BLOCK, part],
                    surf_in[base : base + BLOCK, part],
                )
            )
        for strip in range(base // ROWS_PER_STRIP, (base + BLOCK) // ROWS_PER_STRIP):
            heads = jnp.zeros((members, LANES), F32)
            tails = jnp.zeros((members, LANES), F32)
            for step in range(ROWS_PER_STRIP):
                row = strip * ROWS_PER_STRIP + step
                at = row - base
                for t in range(tiles):
                    part = slice(t * LANES, (t + 1) * LANES)
                    icef, grounded, thin, top = (value[at : at + 1, :] for value in near[t])
                    field_u = vel_in[t, b, pl.ds(at, members, stride=2 * BLOCK), :] * icef
                    field_v = vel_in[t, b, pl.ds(BLOCK + at, members, stride=2 * BLOCK), :] * icef
                    rough = friction32[t, pl.ds(row, members, stride=rows), :]
                    drag = grounded * rough + water_drag * icef
                    shared = jnp.where(sub == 0, thin, jnp.where(sub == 1, top, 0.0))
                    for plane, value in enumerate((field_u, field_v, drag, shared)):
                        own[row, plane, :, part] = value
                        place = step * PLANES + plane
                        if t == 0:
                            head = pltpu.roll(value, place * SIDE, 1) if place else value
                            heads = jnp.where(group == place, head, heads)
                        if t == tiles - 1:
                            tail = pltpu.roll(value, (place + 1) * SIDE, 1) if place != GROUPS - 1 else value
                            tails = jnp.where(group == place, tail, tails)
            to_inner[strip] = either(lower, tails, heads)
            to_outer[strip] = either(lower, heads, tails)

    def tile(up, plane, k, part):
        row = edge_row(plane, k, rows, up)
        if plane < 3:
            return own[row, plane, :, part]
        value = own[row, 3, :, part]
        for n in range(1, SHARED):
            value = value + pltpu.roll(own[row + n, 3, :, part], 2 * n, 0)
        return value

    for j, (plane, k) in enumerate(edge_items()):
        for t in range(tiles):
            part = slice(t * LANES, (t + 1) * LANES)
            top, bottom = tile(True, plane, k, part), tile(False, plane, k, part)
            edge_inner[j * tiles + t] = either(first, bottom, top)
            edge_outer[j * tiles + t] = either(first, top, bottom)


def side_strips(from_inner, from_outer):
    lower, has_inner, has_outer = neighbours("gy")

    def strips(strip):
        inner = jnp.where(has_inner, from_inner[strip], 0.0)
        outer = jnp.where(has_outer, from_outer[strip], 0.0)
        return either(lower, outer, inner), either(lower, inner, outer)

    return strips


def unpacked(left, right, place, lane):
    if place:
        right = pltpu.roll(right, LANES - place * SIDE, 1)
    if place != GROUPS - 1:
        left = pltpu.roll(left, LANES - (place + 1) * SIDE, 1)
    return jnp.where(lane < SIDE, right, jnp.where(lane >= LANES - SIDE, left, 0.0))


def corner_kernel(from_inner, from_outer, to_outer, to_inner):
    strip_count, members, _ = from_inner.shape
    rows = strip_count * ROWS_PER_STRIP
    lane = lane_iota((members, LANES))
    strips = side_strips(from_inner, from_outer)
    first, _, _ = neighbours("gx")
    known = {}

    def tile(row, plane):
        if row not in known:
            left, right = strips(row // ROWS_PER_STRIP)
            step = row % ROWS_PER_STRIP
            known[row] = [unpacked(left, right, step * PLANES + p, lane) for p in range(PLANES)]
        return known[row][plane]

    def item(up, plane, k):
        row = edge_row(plane, k, rows, up)
        value = tile(row, plane)
        if plane == 3:
            for n in range(1, SHARED):
                value = value + pltpu.roll(tile(row + n, plane), 2 * n, 0)
        return value

    top = jnp.zeros((members, LANES), F32)
    bottom = jnp.zeros((members, LANES), F32)
    for j, (plane, k) in enumerate(edge_items()):
        here = lane // (2 * CORNER) == j
        shift = CORNER + 2 * CORNER * j
        top = jnp.where(here, pltpu.roll(item(True, plane, k), shift, 1), top)
        bottom = jnp.where(here, pltpu.roll(item(False, plane, k), shift, 1), bottom)
    to_inner[...] = either(first, bottom, top)
    to_outer[...] = either(first, top, bottom)


def stages(field, store, rows, members, cols):
    visc, sx, sy, sz, tx, ty, tz, rest, inverse, along, across = store
    wide = cols + LANES

    def spread(row, sub):
        return jnp.broadcast_to(field[row + DEPTH, 3, sub : sub + 1, :], (members, wide))

    def after(value):
        return pltpu.roll(value, wide - 1, 1)

    def before(value):
        return pltpu.roll(value, 1, 1)

    def strains(ref, row):
        row = row + DEPTH
        u, v = ref[row, 0], ref[row, 1]
        return (
            ref[row + 1, 0] - ref[row - 1, 0],
            after(v) - before(v),
            (after(u) - before(u)) + (ref[row + 1, 1] - ref[row - 1, 1]),
        )

    def stress(x, y, z, row, strain_u, strain_v, strain_c, nu):
        half = 0.5 * nu
        x[row + DEPTH] = half * (2.0 * strain_u + strain_v)
        y[row + DEPTH] = half * (strain_u + 2.0 * strain_v)
        z[row + DEPTH] = half * (0.5 * strain_c)

    def divergence(x, y, z, row):
        row = row + DEPTH
        shear, normal = z[row], y[row]
        return (
            (x[row + 1] - x[row - 1]) + (after(shear) - before(shear)),
            (after(normal) - before(normal)) + (z[row + 1] - z[row - 1]),
        )

    def viscosity(row):
        su, sv, sc = strains(field, row)
        square = 0.25 * (su * su + sv * sv + su * sv + 0.25 * (sc * sc)) + strain_floor
        nu = (0.5 * spread(row, 0)) * jnp.exp(-flow_power * jnp.log(square))
        visc[row + DEPTH] = nu
        stress(sx, sy, sz, row, su, sv, sc, nu)

    def reciprocal(value):
        guess = pltpu.reciprocal(value, approx=True)
        return guess * (2.0 - value * guess)

    def residual(row):
        div_u, div_v = divergence(sx, sy, sz, row)
        at = row + DEPTH
        drag = field[at, 2]
        on = drag > 0.0
        top = spread(row, 1)
        half = 0.5 * spread(row, 0)
        force_u = half * (spread(row - 1, 1) - spread(row + 1, 1))
        force_v = half * (before(top) - after(top))
        res_u = force_u - (drag * field[at, 0] - jnp.where(on, div_u, 0.0))
        res_v = force_v - (drag * field[at, 1] - jnp.where(on, div_v, 0.0))
        nu = visc[at]
        near_rows = visc[at + 1] + visc[at - 1]
        near_cols = after(nu) + before(nu)
        inv_u = reciprocal(jnp.where(on, near_rows + 0.25 * near_cols + drag, 1.0))
        inv_v = reciprocal(jnp.where(on, near_cols + 0.25 * near_rows + drag, 1.0))
        rest[at, 0] = res_u
        rest[at, 1] = res_v
        inverse[at, 0] = inv_u
        inverse[at, 1] = inv_v
        along[at, 0] = res_u * inv_u
        along[at, 1] = res_v * inv_v

    def direction(row):
        su, sv, sc = strains(along, row)
        stress(tx, ty, tz, row, su, sv, sc, visc[row + DEPTH])

    def image(row, totals):
        div_u, div_v = divergence(tx, ty, tz, row)
        at = row + DEPTH
        drag = field[at, 2]
        on = drag > 0.0
        dir_u, dir_v = along[at, 0], along[at, 1]
        res_u, res_v = rest[at, 0], rest[at, 1]
        off_u = drag * dir_u - jnp.where(on, div_u, 0.0) - res_u
        off_v = drag * dir_v - jnp.where(on, div_v, 0.0) - res_v
        new_u = off_u * inverse[at, 0]
        new_v = off_v * inverse[at, 1]
        across[at, 0] = new_u
        across[at, 1] = new_v
        if 0 <= row < rows:
            totals[0] += (res_u * dir_u + res_v * dir_v)[:, :cols]
            totals[1] += (res_u * new_u + res_v * new_v)[:, :cols]
            totals[2] += (off_u * new_u + off_v * new_v)[:, :cols]

    def energy(row, totals):
        su, sv, sc = strains(across, row)
        at = row + DEPTH
        u, v = across[at, 0], across[at, 1]
        power = field[at, 2] * (u * u + v * v) + visc[at] * (su * su + su * sv + sv * sv + 0.25 * (sc * sc))
        totals[3] += power[:, :cols]

    return viscosity, residual, direction, image, energy


def run(steps, totals, ranges):
    viscosity, residual, direction, image, energy = steps
    for step, over in zip((viscosity, residual, direction), ranges[:3], strict=True):
        for row in over:
            step(row)
    for step, over in zip((image, energy), ranges[3:], strict=True):
        for row in over:
            step(row, totals)


def inner_ranges(rows):
    return [range(k, rows - k) for k in range(1, 6)]


def inner_kernel(own, from_inner, from_outer, field, *rest):
    store, totals_ref = rest[:11], rest[11]
    rows, _, members, cols = own.shape
    lane = lane_iota((members, LANES))
    strips = side_strips(from_inner, from_outer)
    for strip in range(rows // ROWS_PER_STRIP):
        left, right = strips(strip)
        for step in range(ROWS_PER_STRIP):
            row = strip * ROWS_PER_STRIP + step
            for plane in range(PLANES):
                field[row + DEPTH, plane, :, :cols] = own[row, plane]
                field[row + DEPTH, plane, :, cols:] = unpacked(left, right, step * PLANES + plane, lane)
    totals = [jnp.zeros((members, cols), F32) for _ in range(TOTALS)]
    run(stages(field, store, rows, members, cols), totals, inner_ranges(rows))
    for k, total in enumerate(totals):
        totals_ref[k] = total


def outer_kernel(from_outer, from_inner, corner_outer, corner_inner, totals_ref, *refs):
    sums, field, store = refs[12], refs[13], refs[14:25]
    high, _, members, wide = field.shape
    rows, cols = high - 2 * DEPTH, wide - LANES
    tiles = cols // LANES
    lane = lane_iota((members, LANES))
    lower, has_inner, has_outer = neighbours("gx")

    def both(inner, outer):
        inner = jnp.where(has_inner, inner, 0.0)
        outer = jnp.where(has_outer, outer, 0.0)
        return either(lower, outer, inner), either(lower, inner, outer)

    corners = both(corner_inner[...], corner_outer[...])
    for j, (plane, k) in enumerate(edge_items()):
        above = DEPTH - rows + edge_row(plane, k, rows, False)
        below = DEPTH + rows + edge_row(plane, k, rows, True)
        values = [both(from_inner[j * tiles + t], from_outer[j * tiles + t]) for t in range(tiles)]
        values.append(
            tuple(
                jnp.where(
                    (lane < CORNER) | (lane >= LANES - CORNER),
                    pltpu.roll(corner, LANES - CORNER - 2 * CORNER * j, 1),
                    0.0,
                )
                for corner in corners
            )
        )
        for t, pair in enumerate(values):
            for value, row in zip(pair, (above, below), strict=True):
                for n in range(SHARED if plane == 3 else 1):
                    field[row + n, plane, :, t * LANES : (t + 1) * LANES] = (
                        pltpu.roll(value, members - 2 * n, 0) if n else value
                    )
    inner = inner_ranges(rows)
    ranges = [
        [row for row in range(k, rows - k) if row not in inner[k + 4]] for k in range(-4, 1)
    ]
    totals = [totals_ref[k] for k in range(TOTALS)]
    run(stages(field, store, rows, members, cols), totals, ranges)
    sub = sublane_iota((members, LANES))
    row = jnp.zeros((members, LANES), F32)
    for k, total in enumerate(totals):
        row = row + jnp.where(lane == sub + members * k, jnp.sum(total, axis=1, keepdims=True), 0.0)
    row = jnp.sum(row, axis=0, keepdims=True)
    sums[...] = jnp.broadcast_to(row[None], sums.shape)


def final_kernel(parts, field, along, across, out, out_tiles, sems):
    high, _, members, wide = field.shape
    rows, cols = high - 2 * DEPTH, wide - LANES
    total = jnp.sum(parts[...], axis=0)
    spread = jnp.broadcast_to(total, (members, LANES))
    lane = lane_iota((members, LANES))
    sub = sublane_iota((members, LANES))
    norm, cross, square, power = (
        jnp.sum(jnp.where(lane == sub + members * k, spread, 0.0), axis=1, keepdims=True)
        for k in range(TOTALS)
    )
    k1, k2, k3 = cross / norm, square / norm, power / norm
    scale = 1.0 + k1
    first = 1.0 / scale
    beta = (k2 - k1 * k1) * first * first
    curve = (k1 * k1 * scale - 2.0 * k1 * (k1 + k2) + k3) * first * first - beta * beta * scale
    second = jnp.where(curve > 0.0, beta / jnp.where(curve > 0.0, curve, 1.0), 0.0)
    on_along = jnp.broadcast_to(first + second * (k1 * first + beta), (members, LANES))
    on_across = jnp.broadcast_to(second * first, (members, LANES))
    tiles = cols // LANES
    copies = []
    for b in range(rows // BLOCK):
        for t in range(tiles):
            place = slice(t * LANES, (t + 1) * LANES)
            for step in range(BLOCK):
                row = DEPTH + b * BLOCK + step
                for part in range(2):
                    out_tiles[t, b, pl.ds(part * BLOCK + step, members, stride=2 * BLOCK), :] = (
                        field[row, part, :, place]
                        + on_along * along[row, part, :, place]
                        - on_across * across[row, part, :, place]
                    )
            copies.append(
                pltpu.make_async_copy(
                    out_tiles.at[t, b].reshape(2 * members, BLOCK, LANES),
                    out.at[:, pl.ds(b * BLOCK, BLOCK), pl.ds(t * LANES, LANES)],
                    sems.at[b * tiles + t],
                )
            )
            copies[-1].start()
    for copy in copies:
        copy.wait()


def per_device(velocity_guess, friction, thickness, surface, ice_mask, grounded_mask):
    members, parts, rows, cols = velocity_guess.shape
    devices = lax.axis_size(("gx", "gy"))
    wide = cols + LANES
    high = rows + 2 * DEPTH
    tiles, blocks = cols // LANES, rows // BLOCK
    tiled = pltpu.VMEM((tiles, blocks, members * parts * BLOCK, LANES), F32)
    strip = vmem((rows // ROWS_PER_STRIP, members, LANES))
    edge = vmem((len(edge_items()) * tiles, members, LANES))
    own, side_inner, side_outer, edge_inner, edge_outer = call(
        pack_kernel,
        [vmem((rows, PLANES, members, cols)), strip, strip, edge, edge],
        ["hbm"] * 6,
        [
            tiled,
            pltpu.VMEM((members, rows, cols), friction.dtype),
            pltpu.VMEM((rows, cols), F32),
            pltpu.VMEM((rows, cols), F32),
            pltpu.VMEM((rows, cols), jnp.int32),
            pltpu.VMEM((rows, cols), jnp.int32),
            pltpu.VMEM((tiles, members * rows, LANES), F32),
            pltpu.SemaphoreType.DMA((5 + tiles * blocks,)),
        ],
        limit=60,
    )(velocity_guess.reshape(members * parts, rows, cols), friction, thickness, surface, ice_mask, grounded_mask)
    inner, outer = swaps("gy")
    side_inner = lax.ppermute(side_inner, "gy", inner)
    side_outer = lax.ppermute(side_outer, "gy", outer)
    inner, outer = row_swaps()
    edge_outer = lax.ppermute(edge_outer, ("gx", "gy"), outer)
    edge_inner = lax.ppermute(edge_inner, ("gx", "gy"), inner)

    corner = vmem((members, LANES))
    corner_outer, corner_inner = call(corner_kernel, [corner, corner], ["vmem"] * 2)(side_inner, side_outer)
    corner_outer = lax.ppermute(corner_outer, ("gx", "gy"), outer)
    corner_inner = lax.ppermute(corner_inner, ("gx", "gy"), inner)

    one, two = vmem((high, members, wide)), vmem((high, 2, members, wide))
    held = [vmem((high, PLANES, members, wide))] + [one] * 7 + [two] * 4
    *held_now, totals = call(
        inner_kernel,
        held + [vmem((TOTALS, members, cols))],
        ["vmem"] * 3,
        flops=rows * members * wide * 300,
    )(own, side_inner, side_outer)
    sums, *held_now = call(
        outer_kernel,
        [vmem((devices, 1, LANES))] + held,
        ["vmem"] * 17,
        aliases={5 + k: 1 + k for k in range(12)},
    )(edge_outer, edge_inner, corner_outer, corner_inner, totals, *held_now)
    shares = lax.all_to_all(sums, ("gx", "gy"), 0, 0, tiled=True)
    (out,) = call(
        final_kernel,
        [jax.ShapeDtypeStruct((members * parts, rows, cols), F32)],
        ["vmem"] * 4,
        [tiled, pltpu.SemaphoreType.DMA((tiles * blocks,))],
    )(shares, held_now[0], held_now[-2], held_now[-1])
    return out.reshape(members, parts, rows, cols)


def solution(mesh):
    placed = (
        P(None, None, "gx", "gy"),
        P(None, "gx", "gy"),
        P("gx", "gy"),
        P("gx", "gy"),
        P("gx", "gy"),
        P("gx", "gy"),
    )
    return jax.shard_map(
        per_device, mesh=mesh, in_specs=placed, out_specs=P(None, None, "gx", "gy"), check_vma=False
    )
```

time: 31.2 us -> 28.4 us (0.910)
  waiting for transfers between devices: 3.86 us -> 1.72 us
  blocking collectives: 11.9 us -> 10.6 us
  starting transfers between devices: 8.39 us -> 9.29 us
  Pallas kernels: 6.97 us -> 6.59 us
    ppermute x2 -> x4, starting transfers between devices: 5.23 us -> 7.66 us  [the longest x1 4.03 us: per_device(): edge_inner = lax.ppermute(edge_inner, ('gx', 'gy'), inner)]
    ppermute x2 -> x4, waiting for transfers between devices: 2.19 us -> 0.01 us  [the longest x1 0.01 us: per_device(): corner_outer = lax.ppermute(corner_outer, ('gx', 'gy'), outer)]
    all_to_all x1, blocking collectives: 11.9 us -> 10.6 us  [per_device(): shares = lax.all_to_all(sums, ('gx', 'gy'), 0, 0, tiled=True)]
    ppermute x1, starting transfers between devices: 2.64 us -> 1.63 us  [per_device(): side_outer = lax.ppermute(side_outer, 'gy', outer)]
    ppermute x1, starting transfers between devices: 0.52 us -> 0.01 us  [per_device(): side_inner = lax.ppermute(side_inner, 'gy', inner)]
    pallas_call x4, Pallas kernels: 4.47 us -> 4.1 us  [the longest x1 1.81 us: per_device(): call(pack_kernel, [vmem((rows, PLANES, members, cols)), strip, strip, edg...]
  transfers between devices with their start and end apart: 4 -> 6, of which waited for: 3 -> 1; matrix products, arithmetic and copies ran while one was open for 0% -> 0% of each run, Pallas kernels for 8% -> 10%
where the time goes in v3:
time: 28.4 us; the launch traced here: 28.2 us
  blocking collectives  10.6 us (37%)
  starting transfers between devices  9.29 us (33%)
  Pallas kernels  6.59 us (23%)
  waiting for transfers between devices  1.72 us (6%)
    all_to_all x1, blocking collectives, per_device(): shares = lax.all_to_all(sums, ('gx', 'gy'), 0, 0, tiled=True)  10.6 us
    ppermute x1, starting transfers between devices, per_device(): edge_inner = lax.ppermute(edge_inner, ('gx', 'gy'), inner)  4.03 us
    ppermute x1, starting transfers between devices, per_device(): corner_inner = lax.ppermute(corner_inner, ('gx', 'gy'), inner)  2.53 us
    pallas_call x1, Pallas kernels, per_device(): call(inner_kernel, held + [vmem((TOTALS, members, cols))], ['vmem'] * 3,...  2.49 us
    pallas_call x1, Pallas kernels, per_device(): call(pack_kernel, [vmem((rows, PLANES, members, cols)), strip, strip, edg...  1.81 us
    ppermute x1, waiting for transfers between devices, per_device(): side_outer = lax.ppermute(side_outer, 'gy', outer)  1.7 us
    ppermute x1, starting transfers between devices, per_device(): side_outer = lax.ppermute(side_outer, 'gy', outer)  1.63 us
    pallas_call x1, Pallas kernels, per_device(): call(outer_kernel, [vmem((devices, 1, LANES))] + held, ['vmem'] * 17, ali...  1.07 us
  transfers between devices with their start and end apart: 6, of which 1 were waited for; matrix products, arithmetic and copies ran while one was open for 0% of the time, Pallas kernels for 10%

profile of v3, /device:TPU:0, one launch (start us, length us, event | category | flops | bytes accessed | tf_op | source)
XLA Modules:
  0.0 28.2 jit_solution(11852643912304028617)
XLA Ops:
  0.0 1.8 %shard_map.64 = (f32[32,4,8,256]{3,2,1,0:T(8,128)S(1)}, f32[8,8,128]{2,1,0:T(8,128)S(1)}, f32[8,8,128]{2,1,0:T(8,128)S(1)}, f32[28,8,128]{2,1,0:T(8,128)S(1)}, f32[28,8,128]{2,1,0:T(8,128)S(1)}) custom-call(f32[16,32,256]{2,1,0:T(8,128)} %bitcast.2, bf16[8,32,256]{2,1,0:T(8,128)(2,1)} %fric.1, f32[32,256]{1,0:T(8,128)} %thick.1, f32[32,256]{1,0:T(8,128)} %surf.1, ...), custom_call_target="tpu_custom_call" | custom-call | tf_op jit(solution)/shard_map/pallas_call | solution.py:482
  1.8 0.5 %collective-permute-start = (f32[28,8,128]{2,1,0:T(8,128)S(1)}, f32[28,8,128]{2,1,0:T(8,128)S(1)}, u32[]{:S(2)}, u32[]{:S(2)}) collective-permute-start(f32[28,8,128]{2,1,0:T(8,128)S(1)} %get-tuple-element.29), channel_id=1, source_target_pairs={{0,1},{1,0},{2,3},{3,2},{4,8},{5,9},{6,10},{7,11},{8,4},{9,5},{10,... | collective-permute-start | bytes 344072 | tf_op jit(solution)/shard_map/ppermute | solution.py:502
  2.3 4.0 %collective-permute-start.1 = (f32[28,8,128]{2,1,0:T(8,128)S(1)}, f32[28,8,128]{2,1,0:T(8,128)S(1)}, u32[]{:S(2)}, u32[]{:S(2)}) collective-permute-start(f32[28,8,128]{2,1,0:T(8,128)S(1)} %get-tuple-element.30), channel_id=1, source_target_pairs={{0,4},{1,5},{2,6},{3,7},{4,0},{5,1},{6,2},{7,3},{8,12},{9,13},{10,... | collective-permute-start | bytes 344072 | tf_op jit(solution)/shard_map/ppermute | solution.py:503
  6.4 0.0 collective-permute-start.2
  6.4 1.6 %collective-permute-start.3 = (f32[8,8,128]{2,1,0:T(8,128)S(1)}, f32[8,8,128]{2,1,0:T(8,128)S(1)}, u32[]{:S(2)}, u32[]{:S(2)}) collective-permute-start(f32[8,8,128]{2,1,0:T(8,128)S(1)} %get-tuple-element.32), channel_id=1, source_target_pairs={{0,3},{1,2},{2,1},{3,0},{4,7},{5,6},{6,5},{7,4},{8,11},{9,10},{10,... | collective-permute-start | bytes 98312 | tf_op jit(solution)/shard_map/ppermute | solution.py:500
  8.0 0.0 collective-permute-done.2.from_inner
  8.0 1.7 %collective-permute-done.3.from_outer = f32[8,8,128]{2,1,0:T(8,128)S(1)} collective-permute-done((f32[8,8,128]{2,1,0:T(8,128)S(1)}, f32[8,8,128]{2,1,0:T(8,128)S(1)}, u32[]{:S(2)}, u32[]{:S(2)}) %collective-permute-start.3) | collective-permute-done | bytes 32800 | tf_op jit(solution)/shard_map/ppermute | solution.py:500
  9.7 0.2 shard_map.65
  9.9 0.6 %collective-permute-start.4 = (f32[8,128]{1,0:T(8,128)S(1)}, f32[8,128]{1,0:T(8,128)S(1)}, u32[]{:S(2)}, u32[]{:S(2)}) collective-permute-start(f32[8,128]{1,0:T(8,128)S(1)} %get-tuple-element.33), channel_id=1, source_target_pairs={{0,1},{1,0},{2,3},{3,2},{4,8},{5,9},{6,10},{7,11},{8,4},{9,5},{10,... | collective-permute-start | bytes 12296 | tf_op jit(solution)/shard_map/ppermute | solution.py:507
  10.5 2.5 %collective-permute-start.5 = (f32[8,128]{1,0:T(8,128)S(1)}, f32[8,128]{1,0:T(8,128)S(1)}, u32[]{:S(2)}, u32[]{:S(2)}) collective-permute-start(f32[8,128]{1,0:T(8,128)S(1)} %get-tuple-element.34), channel_id=1, source_target_pairs={{0,4},{1,5},{2,6},{3,7},{4,0},{5,1},{6,2},{7,3},{8,12},{9,13},{10,... | collective-permute-start | bytes 12296 | tf_op jit(solution)/shard_map/ppermute | solution.py:508
  13.0 2.5 %shard_map.66 = (f32[42,4,8,384]{3,2,1,0:T(8,128)S(1)}, f32[42,8,384]{2,1,0:T(8,128)S(1)}, f32[42,8,384]{2,1,0:T(8,128)S(1)}, f32[42,8,384]{2,1,0:T(8,128)S(1)},...) custom-call(f32[32,4,8,256]{3,2,1,0:T(8,128)S(1)} %get-tuple-element, ...), custom_call_target="tpu_custom_call" | custom-call | flops 29491200 | bytes 3686400 | tf_op jit(solution)/shard_map/pallas_call | solution.py:512
  15.5 0.0 collective-permute-done.4.corner_outer
  15.5 0.0 collective-permute-done.5.corner_inner
  15.5 0.0 collective-permute-done.from_outer
  15.5 0.0 collective-permute-done.1.from_inner
  15.6 1.1 %shard_map.67 = (f32[32,1,128]{2,1,0:T(1,128)S(1)}, f32[42,4,8,384]{3,2,1,0:T(8,128)S(1)}, f32[42,8,384]{2,1,0:T(8,128)S(1)}, f32[42,8,384]{2,1,0:T(8,128)S(1)},...) custom-call(f32[28,8,128]{2,1,0:T(8,128)S(1)} %collective-permute-do, ...), custom_call_target="tpu_custom_call", output_to_operand_aliasing={{1}: (5, {}), {2}: (6, {}), {3}: (7, {}), {4}: (8, {}), {5}... | custom-call | tf_op jit(solution)/shard_map/pallas_call | solution.py:518
  16.6 10.6 %all_to_all.5.parts = f32[32,1,128]{2,1,0:T(1,128)S(1)} all-to-all(f32[32,1,128]{2,1,0:T(1,128)S(1)} %get-tuple-element.49), channel_id=1, replica_groups=mesh['gx'=8,'gy'=4] {'gx','gy'}, dimensions={0} | all-to-all | bytes 32768 | tf_op jit(solution)/shard_map/all_to_all | solution.py:524
  27.2 1.0 %shard_map.68 = f32[16,32,256]{2,1,0:T(8,128)} custom-call(f32[32,1,128]{2,1,0:T(1,128)S(1)} %all_to_all.5.parts, f32[42,4,8,384]{3,2,1,0:T(8,128)S(1)} %get-tuple-element.50.field, f32[42,2,8,384]{3,2,1,0:T(8,128)S(1)} %get-tuple-element.51.along, f32[42,2,8,384]{3,2,1,0:T(8,128)S(1)} %get-tuple-element.52.across), custom_call_target="tpu_custom_call" | custom-call | tf_op jit(solution)/shard_map/pallas_call | solution.py:525
Async XLA Ops:
  1.8 13.7 %collective-permute-start = (f32[28,8,128]{2,1,0:T(8,128)S(1)}, f32[28,8,128]{2,1,0:T(8,128)S(1)}, u32[]{:S(2)}, u32[]{:S(2)}) collective-permute-start(f32[28,8,128]{2,1,0:T(8,128)S(1)} %get-tuple-element.29), channel_id=1, source_target_pairs={{0,1},{1,0},{2,3},{3,2},{4,8},{5,9},{6,10},{7,11},{8,4},{9,5},{10,... | collective-permute-start | bytes 344072 | tf_op jit(solution)/shard_map/ppermute | solution.py:502
  2.3 13.2 %collective-permute-start.1 = (f32[28,8,128]{2,1,0:T(8,128)S(1)}, f32[28,8,128]{2,1,0:T(8,128)S(1)}, u32[]{:S(2)}, u32[]{:S(2)}) collective-permute-start(f32[28,8,128]{2,1,0:T(8,128)S(1)} %get-tuple-element.30), channel_id=1, source_target_pairs={{0,4},{1,5},{2,6},{3,7},{4,0},{5,1},{6,2},{7,3},{8,12},{9,13},{10,... | collective-permute-start | bytes 344072 | tf_op jit(solution)/shard_map/ppermute | solution.py:503
  6.4 1.6 %collective-permute-start.2 = (f32[8,8,128]{2,1,0:T(8,128)S(1)}, f32[8,8,128]{2,1,0:T(8,128)S(1)}, u32[]{:S(2)}, u32[]{:S(2)}) collective-permute-start(f32[8,8,128]{2,1,0:T(8,128)S(1)} %get-tuple-element.31), channel_id=1, source_target_pairs={{0,1},{1,0},{2,3},{3,2},{4,5},{5,4},{6,7},{7,6},{8,9},{9,8},{10,11... | collective-permute-start | bytes 98312 | tf_op jit(solution)/shard_map/ppermute | solution.py:499
  6.4 3.3 %collective-permute-start.3 = (f32[8,8,128]{2,1,0:T(8,128)S(1)}, f32[8,8,128]{2,1,0:T(8,128)S(1)}, u32[]{:S(2)}, u32[]{:S(2)}) collective-permute-start(f32[8,8,128]{2,1,0:T(8,128)S(1)} %get-tuple-element.32), channel_id=1, source_target_pairs={{0,3},{1,2},{2,1},{3,0},{4,7},{5,6},{6,5},{7,4},{8,11},{9,10},{10,... | collective-permute-start | bytes 98312 | tf_op jit(solution)/shard_map/ppermute | solution.py:500
  9.9 5.6 %collective-permute-start.4 = (f32[8,128]{1,0:T(8,128)S(1)}, f32[8,128]{1,0:T(8,128)S(1)}, u32[]{:S(2)}, u32[]{:S(2)}) collective-permute-start(f32[8,128]{1,0:T(8,128)S(1)} %get-tuple-element.33), channel_id=1, source_target_pairs={{0,1},{1,0},{2,3},{3,2},{4,8},{5,9},{6,10},{7,11},{8,4},{9,5},{10,... | collective-permute-start | bytes 12296 | tf_op jit(solution)/shard_map/ppermute | solution.py:507
  10.5 5.0 %collective-permute-start.5 = (f32[8,128]{1,0:T(8,128)S(1)}, f32[8,128]{1,0:T(8,128)S(1)}, u32[]{:S(2)}, u32[]{:S(2)}) collective-permute-start(f32[8,128]{1,0:T(8,128)S(1)} %get-tuple-element.34), channel_id=1, source_target_pairs={{0,4},{1,5},{2,6},{3,7},{4,0},{5,1},{6,2},{7,3},{8,12},{9,13},{10,... | collective-permute-start | bytes 12296 | tf_op jit(solution)/shard_map/ppermute | solution.py:508

commit v4 on v3

--- a/solution.py
+++ b/solution.py
@@ -100,7 +100,7 @@
 
 
 def pack_kernel(
-    vel, fric, thick, surf, ice, ground, own, to_inner, to_outer, edge_inner, edge_outer,
+    vel, fric, thick, surf, ice, ground, own, to_inner, to_outer,
     vel_in, fric_in, thick_in, surf_in, ice_in, ground_in, friction32, sems,
 ):
     members, rows, cols = fric.shape
@@ -125,7 +125,6 @@
     for copy in small + large[0] + large[-1] + sum(large[1:-1], []):
         copy.start()
     lower, _, _ = neighbours("gy")
-    first, _, _ = neighbours("gx")
     group = lane_iota((members, LANES)) // SIDE
     sub = sublane_iota((members, LANES))
     for copy in small:
@@ -174,6 +173,12 @@
             to_inner[strip] = either(lower, tails, heads)
             to_outer[strip] = either(lower, heads, tails)
 
+
+def edge_kernel(own, edge_outer, edge_inner):
+    rows, _, _, cols = own.shape
+    tiles = cols // LANES
+    first, _, _ = neighbours("gx")
+
     def tile(up, plane, k, part):
         row = edge_row(plane, k, rows, up)
         if plane < 3:
@@ -479,9 +484,9 @@
     tiled = pltpu.VMEM((tiles, blocks, members * parts * BLOCK, LANES), F32)
     strip = vmem((rows // ROWS_PER_STRIP, members, LANES))
     edge = vmem((len(edge_items()) * tiles, members, LANES))
-    own, side_inner, side_outer, edge_inner, edge_outer = call(
+    own, side_inner, side_outer = call(
         pack_kernel,
-        [vmem((rows, PLANES, members, cols)), strip, strip, edge, edge],
+        [vmem((rows, PLANES, members, cols)), strip, strip],
         ["hbm"] * 6,
         [
             tiled,
@@ -499,6 +504,7 @@
     side_inner = lax.ppermute(side_inner, "gy", inner)
     side_outer = lax.ppermute(side_outer, "gy", outer)
     inner, outer = row_swaps()
+    edge_outer, edge_inner = call(edge_kernel, [edge, edge], ["vmem"])(own)
     edge_outer = lax.ppermute(edge_outer, ("gx", "gy"), outer)
     edge_inner = lax.ppermute(edge_inner, ("gx", "gy"), inner)
 
@@ -513,7 +519,7 @@
         inner_kernel,
         held + [vmem((TOTALS, members, cols))],
         ["vmem"] * 3,
-        flops=rows * members * wide * 300,
+        flops=rows * members * wide * 30000,
     )(own, side_inner, side_outer)
     sums, *held_now = call(
         outer_kernel,

time: 28.4 us -> 26.9 us (0.947)
  waiting for transfers between devices: 1.72 us -> 0.02 us
    ppermute x1, waiting for transfers between devices: 1.7 us -> 0.01 us  [per_device(): side_outer = lax.ppermute(side_outer, 'gy', outer)]
    ppermute x1, starting transfers between devices: 4.03 us -> 2.97 us  [per_device(): edge_inner = lax.ppermute(edge_inner, ('gx', 'gy'), inner)]
    ppermute x1, starting transfers between devices: 1.63 us -> 2.64 us  [per_device(): side_outer = lax.ppermute(side_outer, 'gy', outer)]
    ppermute x1, starting transfers between devices: 0.01 us -> 0.52 us  [per_device(): side_inner = lax.ppermute(side_inner, 'gy', inner)]
    ppermute x1, starting transfers between devices: 0.57 us -> 0.07 us  [per_device(): corner_outer = lax.ppermute(corner_outer, ('gx', 'gy'), outer)]
    ppermute x1, starting transfers between devices: 2.53 us -> 3.03 us  [per_device(): corner_inner = lax.ppermute(corner_inner, ('gx', 'gy'), inner)]
    ppermute x1, starting transfers between devices: 0.52 us -> 0.13 us  [per_device(): edge_outer = lax.ppermute(edge_outer, ('gx', 'gy'), outer)]
    pallas_call x1 -> x2, Pallas kernels: 1.81 us -> 1.82 us  [the longest x1 1.79 us: per_device(): call(pack_kernel, [vmem((rows, PLANES, members, cols)), strip, strip], ['...]
  transfers between devices with their start and end apart: 6 -> 6, of which waited for: 1 -> 0; matrix products, arithmetic and copies ran while one was open for 0% -> 0% of each run, Pallas kernels for 10% -> 10%
where the time goes in v4:
time: 26.9 us; the launch traced here: 26.7 us
  blocking collectives  10.6 us (39%)
  starting transfers between devices  9.36 us (35%)
  Pallas kernels  6.6 us (25%)
    all_to_all x1, blocking collectives, per_device(): shares = lax.all_to_all(sums, ('gx', 'gy'), 0, 0, tiled=True)  10.6 us
    ppermute x1, starting transfers between devices, per_device(): corner_inner = lax.ppermute(corner_inner, ('gx', 'gy'), inner)  3.03 us
    ppermute x1, starting transfers between devices, per_device(): edge_inner = lax.ppermute(edge_inner, ('gx', 'gy'), inner)  2.97 us
    ppermute x1, starting transfers between devices, per_device(): side_outer = lax.ppermute(side_outer, 'gy', outer)  2.64 us
    pallas_call x1, Pallas kernels, per_device(): call(inner_kernel, held + [vmem((TOTALS, members, cols))], ['vmem'] * 3,...  2.49 us
    pallas_call x1, Pallas kernels, per_device(): call(pack_kernel, [vmem((rows, PLANES, members, cols)), strip, strip], ['...  1.79 us
    pallas_call x1, Pallas kernels, per_device(): call(outer_kernel, [vmem((devices, 1, LANES))] + held, ['vmem'] * 17, ali...  1.07 us
    pallas_call x1, Pallas kernels, per_device(): call(final_kernel, [jax.ShapeDtypeStruct((members * parts, rows, cols), F...  1.02 us
  transfers between devices with their start and end apart: 6, of which 0 were waited for; matrix products, arithmetic and copies ran while one was open for 0% of the time, Pallas kernels for 10%

profile of v4, /device:TPU:0, one launch (start us, length us, event | category | flops | bytes accessed | tf_op | source)
XLA Modules:
  0.0 26.7 jit_solution(3727121033111628228)
XLA Ops:
  0.0 1.8 %shard_map.64 = (f32[32,4,8,256]{3,2,1,0:T(8,128)S(1)}, f32[8,8,128]{2,1,0:T(8,128)S(1)}, f32[8,8,128]{2,1,0:T(8,128)S(1)}) custom-call(f32[16,32,256]{2,1,0:T(8,128)} %bitcast.2, bf16[8,32,256]{2,1,0:T(8,128)(2,1)} %fric.1, f32[32,256]{1,0:T(8,128)} %thick.1, f32[32,256]{1,0:T(8,128)} %surf.1, s32[32,256]{1,0:T(8,128)} %ice.1, s32[32,256]{1,0:T(8,128)} %ground.1), custom_call_target="tpu_custom_call" | custom-call | tf_op jit(solution)/shard_map/pallas_call | solution.py:487
  1.8 0.5 %collective-permute-start.2 = (f32[8,8,128]{2,1,0:T(8,128)S(1)}, f32[8,8,128]{2,1,0:T(8,128)S(1)}, u32[]{:S(2)}, u32[]{:S(2)}) collective-permute-start(f32[8,8,128]{2,1,0:T(8,128)S(1)} %get-tuple-element.32), channel_id=1, source_target_pairs={{0,1},{1,0},{2,3},{3,2},{4,5},{5,4},{6,7},{7,6},{8,9},{9,8},{10,11... | collective-permute-start | bytes 98312 | tf_op jit(solution)/shard_map/ppermute | solution.py:504
  2.3 2.6 %collective-permute-start.3 = (f32[8,8,128]{2,1,0:T(8,128)S(1)}, f32[8,8,128]{2,1,0:T(8,128)S(1)}, u32[]{:S(2)}, u32[]{:S(2)}) collective-permute-start(f32[8,8,128]{2,1,0:T(8,128)S(1)} %get-tuple-element.33), channel_id=1, source_target_pairs={{0,3},{1,2},{2,1},{3,0},{4,7},{5,6},{6,5},{7,4},{8,11},{9,10},{10,... | collective-permute-start | bytes 98312 | tf_op jit(solution)/shard_map/ppermute | solution.py:505
  5.0 0.1 collective-permute-start
  5.1 3.0 %collective-permute-start.1 = (f32[28,8,128]{2,1,0:T(8,128)S(1)}, f32[28,8,128]{2,1,0:T(8,128)S(1)}, u32[]{:S(2)}, u32[]{:S(2)}) collective-permute-start(f32[28,8,128]{2,1,0:T(8,128)S(1)} %get-tuple-element.31), channel_id=1, source_target_pairs={{0,4},{1,5},{2,6},{3,7},{4,0},{5,1},{6,2},{7,3},{8,12},{9,13},{10,... | collective-permute-start | bytes 344072 | tf_op jit(solution)/shard_map/ppermute | solution.py:509
  8.1 0.0 collective-permute-done.2.from_inner
  8.1 0.0 collective-permute-done.3.from_outer
  8.1 0.2 shard_map.66
  8.3 0.1 collective-permute-start.4
  8.4 3.0 %collective-permute-start.5 = (f32[8,128]{1,0:T(8,128)S(1)}, f32[8,128]{1,0:T(8,128)S(1)}, u32[]{:S(2)}, u32[]{:S(2)}) collective-permute-start(f32[8,128]{1,0:T(8,128)S(1)} %get-tuple-element.35), channel_id=1, source_target_pairs={{0,4},{1,5},{2,6},{3,7},{4,0},{5,1},{6,2},{7,3},{8,12},{9,13},{10,... | collective-permute-start | bytes 12296 | tf_op jit(solution)/shard_map/ppermute | solution.py:514
  11.4 2.5 %shard_map.67 = (f32[42,4,8,384]{3,2,1,0:T(8,128)S(1)}, f32[42,8,384]{2,1,0:T(8,128)S(1)}, f32[42,8,384]{2,1,0:T(8,128)S(1)}, f32[42,8,384]{2,1,0:T(8,128)S(1)},...) custom-call(f32[32,4,8,256]{3,2,1,0:T(8,128)S(1)} %get-tuple-element, ...), custom_call_target="tpu_custom_call" | custom-call | flops 2949120000 | bytes 368640000 | tf_op jit(solution)/shard_map/pallas_call | solution.py:518
  13.9 0.0 collective-permute-done.4.corner_outer
  13.9 0.0 collective-permute-done.5.corner_inner
  13.9 0.0 collective-permute-done.from_outer
  13.9 0.0 collective-permute-done.1.from_inner
  14.0 1.1 %shard_map.68 = (f32[32,1,128]{2,1,0:T(1,128)S(1)}, f32[42,4,8,384]{3,2,1,0:T(8,128)S(1)}, f32[42,8,384]{2,1,0:T(8,128)S(1)}, f32[42,8,384]{2,1,0:T(8,128)S(1)},...) custom-call(f32[28,8,128]{2,1,0:T(8,128)S(1)} %collective-permute-do, ...), custom_call_target="tpu_custom_call", output_to_operand_aliasing={{1}: (5, {}), {2}: (6, {}), {3}: (7, {}), {4}: (8, {}), {5}... | custom-call | tf_op jit(solution)/shard_map/pallas_call | solution.py:524
  15.0 10.6 %all_to_all.5.parts = f32[32,1,128]{2,1,0:T(1,128)S(1)} all-to-all(f32[32,1,128]{2,1,0:T(1,128)S(1)} %get-tuple-element.49), channel_id=1, replica_groups=mesh['gx'=8,'gy'=4] {'gx','gy'}, dimensions={0} | all-to-all | bytes 32768 | tf_op jit(solution)/shard_map/all_to_all | solution.py:530
  25.7 1.0 %shard_map.69 = f32[16,32,256]{2,1,0:T(8,128)} custom-call(f32[32,1,128]{2,1,0:T(1,128)S(1)} %all_to_all.5.parts, f32[42,4,8,384]{3,2,1,0:T(8,128)S(1)} %get-tuple-element.50.field, f32[42,2,8,384]{3,2,1,0:T(8,128)S(1)} %get-tuple-element.51.along, f32[42,2,8,384]{3,2,1,0:T(8,128)S(1)} %get-tuple-element.52.across), custom_call_target="tpu_custom_call" | custom-call | tf_op jit(solution)/shard_map/pallas_call | solution.py:531
  (1 shorter events, 0.0 us)
Async XLA Ops:
  1.8 6.3 %collective-permute-start.2 = (f32[8,8,128]{2,1,0:T(8,128)S(1)}, f32[8,8,128]{2,1,0:T(8,128)S(1)}, u32[]{:S(2)}, u32[]{:S(2)}) collective-permute-start(f32[8,8,128]{2,1,0:T(8,128)S(1)} %get-tuple-element.32), channel_id=1, source_target_pairs={{0,1},{1,0},{2,3},{3,2},{4,5},{5,4},{6,7},{7,6},{8,9},{9,8},{10,11... | collective-permute-start | bytes 98312 | tf_op jit(solution)/shard_map/ppermute | solution.py:504
  2.3 5.8 %collective-permute-start.3 = (f32[8,8,128]{2,1,0:T(8,128)S(1)}, f32[8,8,128]{2,1,0:T(8,128)S(1)}, u32[]{:S(2)}, u32[]{:S(2)}) collective-permute-start(f32[8,8,128]{2,1,0:T(8,128)S(1)} %get-tuple-element.33), channel_id=1, source_target_pairs={{0,3},{1,2},{2,1},{3,0},{4,7},{5,6},{6,5},{7,4},{8,11},{9,10},{10,... | collective-permute-start | bytes 98312 | tf_op jit(solution)/shard_map/ppermute | solution.py:505
  5.0 8.9 %collective-permute-start = (f32[28,8,128]{2,1,0:T(8,128)S(1)}, f32[28,8,128]{2,1,0:T(8,128)S(1)}, u32[]{:S(2)}, u32[]{:S(2)}) collective-permute-start(f32[28,8,128]{2,1,0:T(8,128)S(1)} %get-tuple-element.30), channel_id=1, source_target_pairs={{0,1},{1,0},{2,3},{3,2},{4,8},{5,9},{6,10},{7,11},{8,4},{9,5},{10,... | collective-permute-start | bytes 344072 | tf_op jit(solution)/shard_map/ppermute | solution.py:508
  5.1 8.8 %collective-permute-start.1 = (f32[28,8,128]{2,1,0:T(8,128)S(1)}, f32[28,8,128]{2,1,0:T(8,128)S(1)}, u32[]{:S(2)}, u32[]{:S(2)}) collective-permute-start(f32[28,8,128]{2,1,0:T(8,128)S(1)} %get-tuple-element.31), channel_id=1, source_target_pairs={{0,4},{1,5},{2,6},{3,7},{4,0},{5,1},{6,2},{7,3},{8,12},{9,13},{10,... | collective-permute-start | bytes 344072 | tf_op jit(solution)/shard_map/ppermute | solution.py:509
  8.3 5.6 %collective-permute-start.4 = (f32[8,128]{1,0:T(8,128)S(1)}, f32[8,128]{1,0:T(8,128)S(1)}, u32[]{:S(2)}, u32[]{:S(2)}) collective-permute-start(f32[8,128]{1,0:T(8,128)S(1)} %get-tuple-element.34), channel_id=1, source_target_pairs={{0,1},{1,0},{2,3},{3,2},{4,8},{5,9},{6,10},{7,11},{8,4},{9,5},{10,... | collective-permute-start | bytes 12296 | tf_op jit(solution)/shard_map/ppermute | solution.py:513
  8.4 5.5 %collective-permute-start.5 = (f32[8,128]{1,0:T(8,128)S(1)}, f32[8,128]{1,0:T(8,128)S(1)}, u32[]{:S(2)}, u32[]{:S(2)}) collective-permute-start(f32[8,128]{1,0:T(8,128)S(1)} %get-tuple-element.35), channel_id=1, source_target_pairs={{0,4},{1,5},{2,6},{3,7},{4,0},{5,1},{6,2},{7,3},{8,12},{9,13},{10,... | collective-permute-start | bytes 12296 | tf_op jit(solution)/shard_map/ppermute | solution.py:514

commit v5 on v4

--- a/solution.py
+++ b/solution.py
@@ -17,12 +17,12 @@
 CORNER = 4
 BLOCK = 8
 LANES = 128
-PLANES = 4
+PLANES = 3
 GROUPS = LANES // SIDE
-ROWS_PER_STRIP = GROUPS // PLANES
+QUAD = 4
+ITEMS = QUAD * PLANES + 1
 MOVING = DEPTH
 DRAGGED = DEPTH - 2
-SHARED = DEPTH - 1
 TOTALS = 4
 
 
@@ -92,15 +92,15 @@
 
 def edge_items():
     moving = [(plane, k) for k in range(MOVING) for plane in (0, 1)]
-    return moving + [(2, k) for k in range(DRAGGED)] + [(3, 0)]
+    return moving + [(2, k) for k in range(DRAGGED)] + [(PLANES, 0)]
 
 
 def edge_row(plane, k, rows, up):
-    return k if up else rows - (MOVING, MOVING, DRAGGED, SHARED)[plane] + k
+    return k if up else rows - (MOVING, MOVING, DRAGGED, QUAD)[plane] + k
 
 
 def pack_kernel(
-    vel, fric, thick, surf, ice, ground, own, to_inner, to_outer,
+    vel, fric, thick, surf, ice, ground, own, own_shared, to_inner, to_outer,
     vel_in, fric_in, thick_in, surf_in, ice_in, ground_in, friction32, sems,
 ):
     members, rows, cols = fric.shape
@@ -122,7 +122,7 @@
         ]
         for b in range(blocks)
     ]
-    for copy in small + large[0] + large[-1] + sum(large[1:-1], []):
+    for copy in small + sum(large, []):
         copy.start()
     lower, _, _ = neighbours("gy")
     group = lane_iota((members, LANES)) // SIDE
@@ -131,62 +131,65 @@
         copy.wait()
     for t in range(tiles):
         friction32[t] = fric_in[:, :, t * LANES : (t + 1) * LANES].astype(F32).reshape(members * rows, LANES)
-    for b in [0, blocks - 1] + list(range(1, blocks - 1)):
-        for copy in large[b]:
-            copy.wait()
-        base = b * BLOCK
-        near = []
+    near = {}
+    for b in range(blocks):
+        for t in range(tiles):
+            at = (slice(b * BLOCK, (b + 1) * BLOCK), slice(t * LANES, (t + 1) * LANES))
+            icef = ice_in[at].astype(F32)
+            near[b, t] = (icef, icef * ground_in[at].astype(F32), icef * thick_in[at], surf_in[at])
+    strips = [[jnp.zeros((members, LANES), F32)] * 2 for _ in range(rows // QUAD)]
+
+    def place(strip, item, t, value):
+        if t == 0:
+            head = pltpu.roll(value, item * SIDE, 1) if item else value
+            strips[strip][0] = jnp.where(group == item, head, strips[strip][0])
+        if t == tiles - 1:
+            tail = pltpu.roll(value, (item + 1) * SIDE % LANES, 1)
+            strips[strip][1] = jnp.where(group == item, tail, strips[strip][1])
+
+    for strip in range(rows // QUAD):
+        b, first = divmod(strip * QUAD, BLOCK)
         for t in range(tiles):
             part = slice(t * LANES, (t + 1) * LANES)
-            icef = ice_in[base : base + BLOCK, part].astype(F32)
-            near.append(
-                (
-                    icef,
-                    icef * ground_in[base : base + BLOCK, part].astype(F32),
-                    icef * thick_in[base : base + BLOCK, part],
-                    surf_in[base : base + BLOCK, part],
-                )
-            )
-        for strip in range(base // ROWS_PER_STRIP, (base + BLOCK) // ROWS_PER_STRIP):
-            heads = jnp.zeros((members, LANES), F32)
-            tails = jnp.zeros((members, LANES), F32)
-            for step in range(ROWS_PER_STRIP):
-                row = strip * ROWS_PER_STRIP + step
-                at = row - base
-                for t in range(tiles):
-                    part = slice(t * LANES, (t + 1) * LANES)
-                    icef, grounded, thin, top = (value[at : at + 1, :] for value in near[t])
-                    field_u = vel_in[t, b, pl.ds(at, members, stride=2 * BLOCK), :] * icef
-                    field_v = vel_in[t, b, pl.ds(BLOCK + at, members, stride=2 * BLOCK), :] * icef
-                    rough = friction32[t, pl.ds(row, members, stride=rows), :]
-                    drag = grounded * rough + water_drag * icef
-                    shared = jnp.where(sub == 0, thin, jnp.where(sub == 1, top, 0.0))
-                    for plane, value in enumerate((field_u, field_v, drag, shared)):
-                        own[row, plane, :, part] = value
-                        place = step * PLANES + plane
-                        if t == 0:
-                            head = pltpu.roll(value, place * SIDE, 1) if place else value
-                            heads = jnp.where(group == place, head, heads)
-                        if t == tiles - 1:
-                            tail = pltpu.roll(value, (place + 1) * SIDE, 1) if place != GROUPS - 1 else value
-                            tails = jnp.where(group == place, tail, tails)
-            to_inner[strip] = either(lower, tails, heads)
-            to_outer[strip] = either(lower, heads, tails)
-
-
-def edge_kernel(own, edge_outer, edge_inner):
+            icef, grounded, thin, top = near[b, t]
+            shared = jnp.zeros((members, LANES), F32)
+            for step in range(QUAD):
+                row = strip * QUAD + step
+                at = slice(first + step, first + step + 1)
+                shared = jnp.where(sub == 2 * step, thin[at], jnp.where(sub == 2 * step + 1, top[at], shared))
+                rough = friction32[t, pl.ds(row, members, stride=rows), :]
+                drag = grounded[at] * rough + water_drag * icef[at]
+                own[row, 2, :, part] = drag
+                place(strip, step * PLANES + 2, t, drag)
+            own_shared[strip, :, part] = shared
+            place(strip, ITEMS - 1, t, shared)
+    for copy in sum(large, []):
+        copy.wait()
+    for b in range(blocks):
+        for row in range(b * BLOCK, (b + 1) * BLOCK):
+            strip, step = divmod(row, QUAD)
+            at = row - b * BLOCK
+            for t in range(tiles):
+                icef = near[b, t][0][at : at + 1, :]
+                for plane in range(2):
+                    value = vel_in[t, b, pl.ds(plane * BLOCK + at, members, stride=2 * BLOCK), :] * icef
+                    own[row, plane, :, t * LANES : (t + 1) * LANES] = value
+                    place(strip, step * PLANES + plane, t, value)
+            if step == QUAD - 1:
+                heads, tails = strips[strip]
+                to_inner[strip] = either(lower, tails, heads)
+                to_outer[strip] = either(lower, heads, tails)
+
+
+def edge_kernel(own, own_shared, edge_outer, edge_inner):
     rows, _, _, cols = own.shape
     tiles = cols // LANES
     first, _, _ = neighbours("gx")
 
     def tile(up, plane, k, part):
-        row = edge_row(plane, k, rows, up)
-        if plane < 3:
-            return own[row, plane, :, part]
-        value = own[row, 3, :, part]
-        for n in range(1, SHARED):
-            value = value + pltpu.roll(own[row + n, 3, :, part], 2 * n, 0)
-        return value
+        if plane == PLANES:
+            return own_shared[0 if up else rows // QUAD - 1, :, part]
+        return own[edge_row(plane, k, rows, up), plane, :, part]
 
     for j, (plane, k) in enumerate(edge_items()):
         for t in range(tiles):
@@ -217,26 +220,15 @@
 
 def corner_kernel(from_inner, from_outer, to_outer, to_inner):
     strip_count, members, _ = from_inner.shape
-    rows = strip_count * ROWS_PER_STRIP
+    rows = strip_count * QUAD
     lane = lane_iota((members, LANES))
     strips = side_strips(from_inner, from_outer)
     first, _, _ = neighbours("gx")
-    known = {}
-
-    def tile(row, plane):
-        if row not in known:
-            left, right = strips(row // ROWS_PER_STRIP)
-            step = row % ROWS_PER_STRIP
-            known[row] = [unpacked(left, right, step * PLANES + p, lane) for p in range(PLANES)]
-        return known[row][plane]
 
     def item(up, plane, k):
-        row = edge_row(plane, k, rows, up)
-        value = tile(row, plane)
-        if plane == 3:
-            for n in range(1, SHARED):
-                value = value + pltpu.roll(tile(row + n, plane), 2 * n, 0)
-        return value
+        strip, step = divmod(edge_row(plane, k, rows, up), QUAD)
+        left, right = strips(strip)
+        return unpacked(left, right, ITEMS - 1 if plane == PLANES else step * PLANES + plane, lane)
 
     top = jnp.zeros((members, LANES), F32)
     bottom = jnp.zeros((members, LANES), F32)
@@ -249,18 +241,44 @@
     to_outer[...] = either(first, top, bottom)
 
 
-def stages(field, store, rows, members, cols):
+def stages(field, shared, slope, store, rows, members, cols):
     visc, sx, sy, sz, tx, ty, tz, rest, inverse, along, across = store
     wide = cols + LANES
 
-    def spread(row, sub):
-        return jnp.broadcast_to(field[row + DEPTH, 3, sub : sub + 1, :], (members, wide))
+    def spread(ref, row, sub):
+        strip, step = divmod(row + QUAD, QUAD)
+        at = 2 * step + sub
+        return jnp.broadcast_to(ref[strip, at : at + 1, :], (members, wide))
+
+    lane = lane_iota((members, LANES))
+    count = wide // LANES
+
+    def split(value):
+        return [value[:, t * LANES : (t + 1) * LANES] for t in range(count)]
 
     def after(value):
-        return pltpu.roll(value, wide - 1, 1)
+        parts = split(value)
+        return jnp.concatenate(
+            [
+                pltpu.roll(jnp.where(lane == 0, parts[(t + 1) % count], parts[t]), LANES - 1, 1)
+                for t in range(count)
+            ],
+            axis=1,
+        )
 
     def before(value):
-        return pltpu.roll(value, 1, 1)
+        parts = split(value)
+        return jnp.concatenate(
+            [
+                pltpu.roll(jnp.where(lane == LANES - 1, parts[t - 1], parts[t]), 1, 1)
+                for t in range(count)
+            ],
+            axis=1,
+        )
+
+    def incline(strip):
+        value = shared[strip]
+        slope[strip] = before(value) - after(value)
 
     def strains(ref, row):
         row = row + DEPTH
@@ -288,7 +306,7 @@
     def viscosity(row):
         su, sv, sc = strains(field, row)
         square = 0.25 * (su * su + sv * sv + su * sv + 0.25 * (sc * sc)) + strain_floor
-        nu = (0.5 * spread(row, 0)) * jnp.exp(-flow_power * jnp.log(square))
+        nu = (0.5 * spread(shared, row, 0)) * jnp.exp(-flow_power * jnp.log(square))
         visc[row + DEPTH] = nu
         stress(sx, sy, sz, row, su, sv, sc, nu)
 
@@ -301,10 +319,9 @@
         at = row + DEPTH
         drag = field[at, 2]
         on = drag > 0.0
-        top = spread(row, 1)
-        half = 0.5 * spread(row, 0)
-        force_u = half * (spread(row - 1, 1) - spread(row + 1, 1))
-        force_v = half * (before(top) - after(top))
+        half = 0.5 * spread(shared, row, 0)
+        force_u = half * (spread(shared, row - 1, 1) - spread(shared, row + 1, 1))
+        force_v = half * spread(slope, row, 1)
         res_u = force_u - (drag * field[at, 0] - jnp.where(on, div_u, 0.0))
         res_v = force_v - (drag * field[at, 1] - jnp.where(on, div_v, 0.0))
         nu = visc[at]
@@ -348,11 +365,13 @@
         power = field[at, 2] * (u * u + v * v) + visc[at] * (su * su + su * sv + sv * sv + 0.25 * (sc * sc))
         totals[3] += power[:, :cols]
 
-    return viscosity, residual, direction, image, energy
-
-
-def run(steps, totals, ranges):
-    viscosity, residual, direction, image, energy = steps
+    return incline, viscosity, residual, direction, image, energy
+
+
+def run(steps, totals, strips, ranges):
+    incline, viscosity, residual, direction, image, energy = steps
+    for strip in strips:
+        incline(strip)
     for step, over in zip((viscosity, residual, direction), ranges[:3], strict=True):
         for row in over:
             step(row)
@@ -365,26 +384,29 @@
     return [range(k, rows - k) for k in range(1, 6)]
 
 
-def inner_kernel(own, from_inner, from_outer, field, *rest):
+def inner_kernel(own, own_shared, from_inner, from_outer, field, shared, slope, *rest):
     store, totals_ref = rest[:11], rest[11]
     rows, _, members, cols = own.shape
     lane = lane_iota((members, LANES))
     strips = side_strips(from_inner, from_outer)
-    for strip in range(rows // ROWS_PER_STRIP):
+    for strip in range(rows // QUAD):
         left, right = strips(strip)
-        for step in range(ROWS_PER_STRIP):
-            row = strip * ROWS_PER_STRIP + step
+        shared[strip + 1, :, :cols] = own_shared[strip]
+        shared[strip + 1, :, cols:] = unpacked(left, right, ITEMS - 1, lane)
+        for step in range(QUAD):
+            row = strip * QUAD + step
             for plane in range(PLANES):
                 field[row + DEPTH, plane, :, :cols] = own[row, plane]
                 field[row + DEPTH, plane, :, cols:] = unpacked(left, right, step * PLANES + plane, lane)
     totals = [jnp.zeros((members, cols), F32) for _ in range(TOTALS)]
-    run(stages(field, store, rows, members, cols), totals, inner_ranges(rows))
+    strips = range(1, rows // QUAD + 1)
+    run(stages(field, shared, slope, store, rows, members, cols), totals, strips, inner_ranges(rows))
     for k, total in enumerate(totals):
         totals_ref[k] = total
 
 
 def outer_kernel(from_outer, from_inner, corner_outer, corner_inner, totals_ref, *refs):
-    sums, field, store = refs[12], refs[13], refs[14:25]
+    sums, field, shared, slope, store = refs[14], refs[15], refs[16], refs[17], refs[18:29]
     high, _, members, wide = field.shape
     rows, cols = high - 2 * DEPTH, wide - LANES
     tiles = cols // LANES
@@ -412,17 +434,19 @@
             )
         )
         for t, pair in enumerate(values):
-            for value, row in zip(pair, (above, below), strict=True):
-                for n in range(SHARED if plane == 3 else 1):
-                    field[row + n, plane, :, t * LANES : (t + 1) * LANES] = (
-                        pltpu.roll(value, members - 2 * n, 0) if n else value
-                    )
+            part = slice(t * LANES, (t + 1) * LANES)
+            for value, row, strip in zip(pair, (above, below), (0, rows // QUAD + 1), strict=True):
+                if plane == PLANES:
+                    shared[strip, :, part] = value
+                else:
+                    field[row, plane, :, part] = value
     inner = inner_ranges(rows)
     ranges = [
         [row for row in range(k, rows - k) if row not in inner[k + 4]] for k in range(-4, 1)
     ]
     totals = [totals_ref[k] for k in range(TOTALS)]
-    run(stages(field, store, rows, members, cols), totals, ranges)
+    strips = (0, rows // QUAD + 1)
+    run(stages(field, shared, slope, store, rows, members, cols), totals, strips, ranges)
     sub = sublane_iota((members, LANES))
     row = jnp.zeros((members, LANES), F32)
     for k, total in enumerate(totals):
@@ -482,11 +506,11 @@
     high = rows + 2 * DEPTH
     tiles, blocks = cols // LANES, rows // BLOCK
     tiled = pltpu.VMEM((tiles, blocks, members * parts * BLOCK, LANES), F32)
-    strip = vmem((rows // ROWS_PER_STRIP, members, LANES))
+    strip = vmem((rows // QUAD, members, LANES))
     edge = vmem((len(edge_items()) * tiles, members, LANES))
-    own, side_inner, side_outer = call(
+    own, own_shared, side_inner, side_outer = call(
         pack_kernel,
-        [vmem((rows, PLANES, members, cols)), strip, strip],
+        [vmem((rows, PLANES, members, cols)), vmem((rows // QUAD, members, cols)), strip, strip],
         ["hbm"] * 6,
         [
             tiled,
@@ -504,7 +528,7 @@
     side_inner = lax.ppermute(side_inner, "gy", inner)
     side_outer = lax.ppermute(side_outer, "gy", outer)
     inner, outer = row_swaps()
-    edge_outer, edge_inner = call(edge_kernel, [edge, edge], ["vmem"])(own)
+    edge_outer, edge_inner = call(edge_kernel, [edge, edge], ["vmem"] * 2)(own, own_shared)
     edge_outer = lax.ppermute(edge_outer, ("gx", "gy"), outer)
     edge_inner = lax.ppermute(edge_inner, ("gx", "gy"), inner)
 
@@ -514,18 +538,19 @@
     corner_inner = lax.ppermute(corner_inner, ("gx", "gy"), inner)
 
     one, two = vmem((high, members, wide)), vmem((high, 2, members, wide))
-    held = [vmem((high, PLANES, members, wide))] + [one] * 7 + [two] * 4
+    quads = vmem((rows // QUAD + 2, members, wide))
+    held = [vmem((high, PLANES, members, wide)), quads, quads] + [one] * 7 + [two] * 4
     *held_now, totals = call(
         inner_kernel,
         held + [vmem((TOTALS, members, cols))],
-        ["vmem"] * 3,
+        ["vmem"] * 4,
         flops=rows * members * wide * 30000,
-    )(own, side_inner, side_outer)
+    )(own, own_shared, side_inner, side_outer)
     sums, *held_now = call(
         outer_kernel,
         [vmem((devices, 1, LANES))] + held,
-        ["vmem"] * 17,
-        aliases={5 + k: 1 + k for k in range(12)},
+        ["vmem"] * 19,
+        aliases={5 + k: 1 + k for k in range(14)},
     )(edge_outer, edge_inner, corner_outer, corner_inner, totals, *held_now)
     shares = lax.all_to_all(sums, ("gx", "gy"), 0, 0, tiled=True)
     (out,) = call(

time: 26.9 us -> 26.6 us (0.989)
  Pallas kernels: 6.6 us -> 6.04 us
  blocking collectives: 10.6 us -> 10.9 us
    pallas_call x4, Pallas kernels: 5.38 us -> 4.81 us  [the longest x1 2.21 us: per_device(): call(inner_kernel, held + [vmem((TOTALS, members, cols))], ['vmem'] * 4,...]
    all_to_all x1, blocking collectives: 10.6 us -> 10.9 us  [per_device(): shares = lax.all_to_all(sums, ('gx', 'gy'), 0, 0, tiled=True)]
  transfers between devices with their start and end apart: 6 -> 6, of which waited for: 0 -> 0; matrix products, arithmetic and copies ran while one was open for 0% -> 0% of each run, Pallas kernels for 10% -> 9%
where the time goes in v5:
time: 26.6 us; the launch traced here: 26.4 us
  blocking collectives  10.9 us (41%)
  starting transfers between devices  9.36 us (35%)
  Pallas kernels  6.04 us (23%)
    all_to_all x1, blocking collectives, per_device(): shares = lax.all_to_all(sums, ('gx', 'gy'), 0, 0, tiled=True)  10.9 us
    ppermute x1, starting transfers between devices, per_device(): corner_inner = lax.ppermute(corner_inner, ('gx', 'gy'), inner)  3.03 us
    ppermute x1, starting transfers between devices, per_device(): edge_inner = lax.ppermute(edge_inner, ('gx', 'gy'), inner)  2.97 us
    ppermute x1, starting transfers between devices, per_device(): side_outer = lax.ppermute(side_outer, 'gy', outer)  2.64 us
    pallas_call x1, Pallas kernels, per_device(): call(inner_kernel, held + [vmem((TOTALS, members, cols))], ['vmem'] * 4,...  2.21 us
    pallas_call x1, Pallas kernels, per_device(): call(pack_kernel, [vmem((rows, PLANES, members, cols)), vmem((rows // QUA...  1.56 us
    pallas_call x1, Pallas kernels, per_device(): call(final_kernel, [jax.ShapeDtypeStruct((members * parts, rows, cols), F...  1.04 us
    pallas_call x1, Pallas kernels, per_device(): call(outer_kernel, [vmem((devices, 1, LANES))] + held, ['vmem'] * 19, ali...  1.01 us
  transfers between devices with their start and end apart: 6, of which 0 were waited for; matrix products, arithmetic and copies ran while one was open for 0% of the time, Pallas kernels for 9%

profile of v5, /device:TPU:0, one launch (start us, length us, event | category | flops | bytes accessed | tf_op | source)
XLA Modules:
  0.0 26.4 jit_solution(7335704195264572184)
XLA Ops:
  0.0 1.6 %shard_map.64 = (f32[32,3,8,256]{3,2,1,0:T(8,128)S(1)}, f32[8,8,256]{2,1,0:T(8,128)S(1)}, f32[8,8,128]{2,1,0:T(8,128)S(1)}, f32[8,8,128]{2,1,0:T(8,128)S(1)}) custom-call(f32[16,32,256]{2,1,0:T(8,128)} %bitcast.2, bf16[8,32,256]{2,1,0:T(8,128)(2,1)} %fric.1, f32[32,256]{1,0:T(8,128)} %thick.1, f32[32,256]{1,0:T(8,128)} %surf.1, s32[32,256]{1,0:T(8,128)} %ice.1, ...), custom_call_target="tpu_custom_call" | custom-call | tf_op jit(solution)/shard_map/pallas_call | solution.py:511
  1.6 0.5 %collective-permute-start.2 = (f32[8,8,128]{2,1,0:T(8,128)S(1)}, f32[8,8,128]{2,1,0:T(8,128)S(1)}, u32[]{:S(2)}, u32[]{:S(2)}) collective-permute-start(f32[8,8,128]{2,1,0:T(8,128)S(1)} %get-tuple-element.36), channel_id=1, source_target_pairs={{0,1},{1,0},{2,3},{3,2},{4,5},{5,4},{6,7},{7,6},{8,9},{9,8},{10,11... | collective-permute-start | bytes 98312 | tf_op jit(solution)/shard_map/ppermute | solution.py:528
  2.1 2.6 %collective-permute-start.3 = (f32[8,8,128]{2,1,0:T(8,128)S(1)}, f32[8,8,128]{2,1,0:T(8,128)S(1)}, u32[]{:S(2)}, u32[]{:S(2)}) collective-permute-start(f32[8,8,128]{2,1,0:T(8,128)S(1)} %get-tuple-element.37), channel_id=1, source_target_pairs={{0,3},{1,2},{2,1},{3,0},{4,7},{5,6},{6,5},{7,4},{8,11},{9,10},{10,... | collective-permute-start | bytes 98312 | tf_op jit(solution)/shard_map/ppermute | solution.py:529
  4.8 0.1 collective-permute-start
  4.9 3.0 %collective-permute-start.1 = (f32[28,8,128]{2,1,0:T(8,128)S(1)}, f32[28,8,128]{2,1,0:T(8,128)S(1)}, u32[]{:S(2)}, u32[]{:S(2)}) collective-permute-start(f32[28,8,128]{2,1,0:T(8,128)S(1)} %get-tuple-element.35), channel_id=1, source_target_pairs={{0,4},{1,5},{2,6},{3,7},{4,0},{5,1},{6,2},{7,3},{8,12},{9,13},{10,... | collective-permute-start | bytes 344072 | tf_op jit(solution)/shard_map/ppermute | solution.py:533
  7.9 0.0 collective-permute-done.2.from_inner
  7.9 0.0 collective-permute-done.3.from_outer
  7.9 0.2 shard_map.66
  8.1 0.1 collective-permute-start.4
  8.2 3.0 %collective-permute-start.5 = (f32[8,128]{1,0:T(8,128)S(1)}, f32[8,128]{1,0:T(8,128)S(1)}, u32[]{:S(2)}, u32[]{:S(2)}) collective-permute-start(f32[8,128]{1,0:T(8,128)S(1)} %get-tuple-element.39), channel_id=1, source_target_pairs={{0,4},{1,5},{2,6},{3,7},{4,0},{5,1},{6,2},{7,3},{8,12},{9,13},{10,... | collective-permute-start | bytes 12296 | tf_op jit(solution)/shard_map/ppermute | solution.py:538
  11.2 2.2 %shard_map.67 = (f32[42,3,8,384]{3,2,1,0:T(8,128)S(1)}, f32[10,8,384]{2,1,0:T(8,128)S(1)}, f32[10,8,384]{2,1,0:T(8,128)S(1)}, f32[42,8,384]{2,1,0:T(8,128)S(1)},...) custom-call(f32[32,3,8,256]{3,2,1,0:T(8,128)S(1)} %get-tuple-element, ...), custom_call_target="tpu_custom_call" | custom-call | flops 2949120000 | bytes 368640000 | tf_op jit(solution)/shard_map/pallas_call | solution.py:543
  13.4 0.0 collective-permute-done.4.corner_outer
  13.4 0.0 collective-permute-done.5.corner_inner
  13.4 0.0 collective-permute-done.from_outer
  13.4 0.0 collective-permute-done.1.from_inner
  13.4 1.0 %shard_map.68 = (f32[32,1,128]{2,1,0:T(1,128)S(1)}, f32[42,3,8,384]{3,2,1,0:T(8,128)S(1)}, f32[10,8,384]{2,1,0:T(8,128)S(1)}, f32[10,8,384]{2,1,0:T(8,128)S(1)},...) custom-call(f32[28,8,128]{2,1,0:T(8,128)S(1)} %collective-permute-do, ...), custom_call_target="tpu_custom_call", output_to_operand_aliasing={{1}: (5, {}), {2}: (6, {}), {3}: (7, {}), {4}: (8, {}), {5}... | custom-call | tf_op jit(solution)/shard_map/pallas_call | solution.py:549
  14.5 10.9 %all_to_all.5.parts = f32[32,1,128]{2,1,0:T(1,128)S(1)} all-to-all(f32[32,1,128]{2,1,0:T(1,128)S(1)} %get-tuple-element.55), channel_id=1, replica_groups=mesh['gx'=8,'gy'=4] {'gx','gy'}, dimensions={0} | all-to-all | bytes 32768 | tf_op jit(solution)/shard_map/all_to_all | solution.py:555
  25.4 1.0 %shard_map.69 = f32[16,32,256]{2,1,0:T(8,128)} custom-call(f32[32,1,128]{2,1,0:T(1,128)S(1)} %all_to_all.5.parts, f32[42,3,8,384]{3,2,1,0:T(8,128)S(1)} %get-tuple-element.56.field, f32[42,2,8,384]{3,2,1,0:T(8,128)S(1)} %get-tuple-element.57.along, f32[42,2,8,384]{3,2,1,0:T(8,128)S(1)} %get-tuple-element.58.across), custom_call_target="tpu_custom_call" | custom-call | tf_op jit(solution)/shard_map/pallas_call | solution.py:556
  (1 shorter events, 0.0 us)
Async XLA Ops:
  1.6 6.3 %collective-permute-start.2 = (f32[8,8,128]{2,1,0:T(8,128)S(1)}, f32[8,8,128]{2,1,0:T(8,128)S(1)}, u32[]{:S(2)}, u32[]{:S(2)}) collective-permute-start(f32[8,8,128]{2,1,0:T(8,128)S(1)} %get-tuple-element.36), channel_id=1, source_target_pairs={{0,1},{1,0},{2,3},{3,2},{4,5},{5,4},{6,7},{7,6},{8,9},{9,8},{10,11... | collective-permute-start | bytes 98312 | tf_op jit(solution)/shard_map/ppermute | solution.py:528
  2.1 5.8 %collective-permute-start.3 = (f32[8,8,128]{2,1,0:T(8,128)S(1)}, f32[8,8,128]{2,1,0:T(8,128)S(1)}, u32[]{:S(2)}, u32[]{:S(2)}) collective-permute-start(f32[8,8,128]{2,1,0:T(8,128)S(1)} %get-tuple-element.37), channel_id=1, source_target_pairs={{0,3},{1,2},{2,1},{3,0},{4,7},{5,6},{6,5},{7,4},{8,11},{9,10},{10,... | collective-permute-start | bytes 98312 | tf_op jit(solution)/shard_map/ppermute | solution.py:529
  4.8 8.7 %collective-permute-start = (f32[28,8,128]{2,1,0:T(8,128)S(1)}, f32[28,8,128]{2,1,0:T(8,128)S(1)}, u32[]{:S(2)}, u32[]{:S(2)}) collective-permute-start(f32[28,8,128]{2,1,0:T(8,128)S(1)} %get-tuple-element.34), channel_id=1, source_target_pairs={{0,1},{1,0},{2,3},{3,2},{4,8},{5,9},{6,10},{7,11},{8,4},{9,5},{10,... | collective-permute-start | bytes 344072 | tf_op jit(solution)/shard_map/ppermute | solution.py:532
  4.9 8.5 %collective-permute-start.1 = (f32[28,8,128]{2,1,0:T(8,128)S(1)}, f32[28,8,128]{2,1,0:T(8,128)S(1)}, u32[]{:S(2)}, u32[]{:S(2)}) collective-permute-start(f32[28,8,128]{2,1,0:T(8,128)S(1)} %get-tuple-element.35), channel_id=1, source_target_pairs={{0,4},{1,5},{2,6},{3,7},{4,0},{5,1},{6,2},{7,3},{8,12},{9,13},{10,... | collective-permute-start | bytes 344072 | tf_op jit(solution)/shard_map/ppermute | solution.py:533
  8.1 5.3 %collective-permute-start.4 = (f32[8,128]{1,0:T(8,128)S(1)}, f32[8,128]{1,0:T(8,128)S(1)}, u32[]{:S(2)}, u32[]{:S(2)}) collective-permute-start(f32[8,128]{1,0:T(8,128)S(1)} %get-tuple-element.38), channel_id=1, source_target_pairs={{0,1},{1,0},{2,3},{3,2},{4,8},{5,9},{6,10},{7,11},{8,4},{9,5},{10,... | collective-permute-start | bytes 12296 | tf_op jit(solution)/shard_map/ppermute | solution.py:537
  8.2 5.3 %collective-permute-start.5 = (f32[8,128]{1,0:T(8,128)S(1)}, f32[8,128]{1,0:T(8,128)S(1)}, u32[]{:S(2)}, u32[]{:S(2)}) collective-permute-start(f32[8,128]{1,0:T(8,128)S(1)} %get-tuple-element.39), channel_id=1, source_target_pairs={{0,4},{1,5},{2,6},{3,7},{4,0},{5,1},{6,2},{7,3},{8,12},{9,13},{10,... | collective-permute-start | bytes 12296 | tf_op jit(solution)/shard_map/ppermute | solution.py:538

commit v6 on v5

--- a/solution.py
+++ b/solution.py
@@ -10,6 +10,8 @@
 strain_floor = 0.1
 water_drag = 0.25
 flow_power = 1.0 / 3.0
+
+most_step = 1.0 + 2.5 * 2.25 * strain_floor**-flow_power / water_drag
 
 F32 = jnp.float32
 DEPTH = 5
@@ -405,41 +407,47 @@
         totals_ref[k] = total
 
 
-def outer_kernel(from_outer, from_inner, corner_outer, corner_inner, totals_ref, *refs):
+def land(received, valid, below, field, shared):
+    high, _, _, wide = field.shape
+    rows, tiles = high - 2 * DEPTH, wide // LANES - 1
+    for j, (plane, k) in enumerate(edge_items()):
+        above = DEPTH - rows + edge_row(plane, k, rows, False)
+        row = jnp.where(below, DEPTH + rows + edge_row(plane, k, rows, True), above)
+        strip = jnp.where(below, rows // QUAD + 1, 0)
+        for t in range(tiles):
+            part = slice(t * LANES, (t + 1) * LANES)
+            value = jnp.where(valid, received[j * tiles + t], 0.0)
+            if plane == PLANES:
+                shared[strip, :, part] = value
+            else:
+                field[row, plane, :, part] = value
+
+
+def land_kernel(from_inner, _, __, field, shared):
+    lower, has_inner, _ = neighbours("gx")
+    land(from_inner, has_inner, lower, field, shared)
+
+
+def outer_kernel(from_outer, corner_outer, corner_inner, totals_ref, *refs):
     sums, field, shared, slope, store = refs[14], refs[15], refs[16], refs[17], refs[18:29]
     high, _, members, wide = field.shape
     rows, cols = high - 2 * DEPTH, wide - LANES
-    tiles = cols // LANES
     lane = lane_iota((members, LANES))
     lower, has_inner, has_outer = neighbours("gx")
-
-    def both(inner, outer):
-        inner = jnp.where(has_inner, inner, 0.0)
-        outer = jnp.where(has_outer, outer, 0.0)
-        return either(lower, outer, inner), either(lower, inner, outer)
-
-    corners = both(corner_inner[...], corner_outer[...])
+    land(from_outer, has_outer, jnp.logical_not(lower), field, shared)
+    inner = jnp.where(has_inner, corner_inner[...], 0.0)
+    outer = jnp.where(has_outer, corner_outer[...], 0.0)
+    corners = (either(lower, outer, inner), either(lower, inner, outer))
     for j, (plane, k) in enumerate(edge_items()):
         above = DEPTH - rows + edge_row(plane, k, rows, False)
         below = DEPTH + rows + edge_row(plane, k, rows, True)
-        values = [both(from_inner[j * tiles + t], from_outer[j * tiles + t]) for t in range(tiles)]
-        values.append(
-            tuple(
-                jnp.where(
-                    (lane < CORNER) | (lane >= LANES - CORNER),
-                    pltpu.roll(corner, LANES - CORNER - 2 * CORNER * j, 1),
-                    0.0,
-                )
-                for corner in corners
-            )
-        )
-        for t, pair in enumerate(values):
-            part = slice(t * LANES, (t + 1) * LANES)
-            for value, row, strip in zip(pair, (above, below), (0, rows // QUAD + 1), strict=True):
-                if plane == PLANES:
-                    shared[strip, :, part] = value
-                else:
-                    field[row, plane, :, part] = value
+        for corner, row, strip in zip(corners, (above, below), (0, rows // QUAD + 1), strict=True):
+            value = pltpu.roll(corner, LANES - CORNER - 2 * CORNER * j, 1)
+            value = jnp.where((lane < CORNER) | (lane >= LANES - CORNER), value, 0.0)
+            if plane == PLANES:
+                shared[strip, :, cols:] = value
+            else:
+                field[row, plane, :, cols:] = value
     inner = inner_ranges(rows)
     ranges = [
         [row for row in range(k, rows - k) if row not in inner[k + 4]] for k in range(-4, 1)
@@ -472,6 +480,7 @@
     beta = (k2 - k1 * k1) * first * first
     curve = (k1 * k1 * scale - 2.0 * k1 * (k1 + k2) + k3) * first * first - beta * beta * scale
     second = jnp.where(curve > 0.0, beta / jnp.where(curve > 0.0, curve, 1.0), 0.0)
+    second = jnp.clip(second, 0.0, most_step)
     on_along = jnp.broadcast_to(first + second * (k1 * first + beta), (members, LANES))
     on_across = jnp.broadcast_to(second * first, (members, LANES))
     tiles = cols // LANES
@@ -544,14 +553,21 @@
         inner_kernel,
         held + [vmem((TOTALS, members, cols))],
         ["vmem"] * 4,
-        flops=rows * members * wide * 30000,
+        flops=rows * members * wide * 10000,
     )(own, own_shared, side_inner, side_outer)
+    held_now[:2] = call(
+        land_kernel,
+        held[:2],
+        ["vmem"] * 3,
+        flops=rows * members * wide * 10000,
+        aliases={1: 0, 2: 1},
+    )(edge_inner, *held_now[:2])
     sums, *held_now = call(
         outer_kernel,
         [vmem((devices, 1, LANES))] + held,
-        ["vmem"] * 19,
-        aliases={5 + k: 1 + k for k in range(14)},
-    )(edge_outer, edge_inner, corner_outer, corner_inner, totals, *held_now)
+        ["vmem"] * 18,
+        aliases={4 + k: 1 + k for k in range(14)},
+    )(edge_outer, corner_outer, corner_inner, totals, *held_now)
     shares = lax.all_to_all(sums, ("gx", "gy"), 0, 0, tiled=True)
     (out,) = call(
         final_kernel,

time: 26.6 us -> 26.4 us (level)
  starting transfers between devices: 9.36 us -> 8.17 us
  blocking collectives: 10.9 us -> 11.9 us
    ppermute x1, starting transfers between devices: 2.97 us -> 1.56 us  [per_device(): edge_inner = lax.ppermute(edge_inner, ('gx', 'gy'), inner)]
    all_to_all x1, blocking collectives: 10.9 us -> 11.9 us  [per_device(): shares = lax.all_to_all(sums, ('gx', 'gy'), 0, 0, tiled=True)]
    ppermute x1, starting transfers between devices: 0.07 us -> 0.5 us  [per_device(): corner_outer = lax.ppermute(corner_outer, ('gx', 'gy'), outer)]
    pallas_call x1 -> x2, Pallas kernels: 1.01 us -> 1.05 us  [the longest x1 1.02 us: per_device(): call(outer_kernel, [vmem((devices, 1, LANES))] + held, ['vmem'] * 18, ali...]
  transfers between devices with their start and end apart: 6 -> 6, of which waited for: 0 -> 1; matrix products, arithmetic and copies ran while one was open for 0% -> 0% of each run, Pallas kernels for 9% -> 9%
where the time goes in v6:
time: 26.4 us; the launch traced here: 26.3 us
  blocking collectives  11.9 us (45%)
  starting transfers between devices  8.17 us (31%)
  Pallas kernels  6.07 us (23%)
    all_to_all x1, blocking collectives, per_device(): shares = lax.all_to_all(sums, ('gx', 'gy'), 0, 0, tiled=True)  11.9 us
    ppermute x1, starting transfers between devices, per_device(): corner_inner = lax.ppermute(corner_inner, ('gx', 'gy'), inner)  2.95 us
    ppermute x1, starting transfers between devices, per_device(): side_outer = lax.ppermute(side_outer, 'gy', outer)  2.64 us
    pallas_call x1, Pallas kernels, per_device(): call(inner_kernel, held + [vmem((TOTALS, members, cols))], ['vmem'] * 4,...  2.2 us
    pallas_call x1, Pallas kernels, per_device(): call(pack_kernel, [vmem((rows, PLANES, members, cols)), vmem((rows // QUA...  1.56 us
    ppermute x1, starting transfers between devices, per_device(): edge_inner = lax.ppermute(edge_inner, ('gx', 'gy'), inner)  1.56 us
    pallas_call x1, Pallas kernels, per_device(): call(final_kernel, [jax.ShapeDtypeStruct((members * parts, rows, cols), F...  1.04 us
    pallas_call x1, Pallas kernels, per_device(): call(outer_kernel, [vmem((devices, 1, LANES))] + held, ['vmem'] * 18, ali...  1.02 us
  transfers between devices with their start and end apart: 6, of which 1 were waited for; matrix products, arithmetic and copies ran while one was open for 0% of the time, Pallas kernels for 9%

profile of v6, /device:TPU:0, one launch (start us, length us, event | category | flops | bytes accessed | tf_op | source)
XLA Modules:
  0.0 26.3 jit_solution(2445138729705851349)
XLA Ops:
  0.0 1.6 %shard_map.64 = (f32[32,3,8,256]{3,2,1,0:T(8,128)S(1)}, f32[8,8,256]{2,1,0:T(8,128)S(1)}, f32[8,8,128]{2,1,0:T(8,128)S(1)}, f32[8,8,128]{2,1,0:T(8,128)S(1)}) custom-call(f32[16,32,256]{2,1,0:T(8,128)} %bitcast.2, bf16[8,32,256]{2,1,0:T(8,128)(2,1)} %fric.1, f32[32,256]{1,0:T(8,128)} %thick.1, f32[32,256]{1,0:T(8,128)} %surf.1, s32[32,256]{1,0:T(8,128)} %ice.1, ...), custom_call_target="tpu_custom_call" | custom-call | tf_op jit(solution)/shard_map/pallas_call | solution.py:520
  1.6 0.5 %collective-permute-start.1 = (f32[8,8,128]{2,1,0:T(8,128)S(1)}, f32[8,8,128]{2,1,0:T(8,128)S(1)}, u32[]{:S(2)}, u32[]{:S(2)}) collective-permute-start(f32[8,8,128]{2,1,0:T(8,128)S(1)} %get-tuple-element.37), channel_id=1, source_target_pairs={{0,1},{1,0},{2,3},{3,2},{4,5},{5,4},{6,7},{7,6},{8,9},{9,8},{10,11... | collective-permute-start | bytes 98312 | tf_op jit(solution)/shard_map/ppermute | solution.py:537
  2.1 2.6 %collective-permute-start.2 = (f32[8,8,128]{2,1,0:T(8,128)S(1)}, f32[8,8,128]{2,1,0:T(8,128)S(1)}, u32[]{:S(2)}, u32[]{:S(2)}) collective-permute-start(f32[8,8,128]{2,1,0:T(8,128)S(1)} %get-tuple-element.38), channel_id=1, source_target_pairs={{0,3},{1,2},{2,1},{3,0},{4,7},{5,6},{6,5},{7,4},{8,11},{9,10},{10,... | collective-permute-start | bytes 98312 | tf_op jit(solution)/shard_map/ppermute | solution.py:538
  4.8 1.6 %collective-permute-start.5 = (f32[28,8,128]{2,1,0:T(8,128)S(1)}, f32[28,8,128]{2,1,0:T(8,128)S(1)}, u32[]{:S(2)}, u32[]{:S(2)}) collective-permute-start(f32[28,8,128]{2,1,0:T(8,128)S(1)} %get-tuple-element.42), channel_id=1, source_target_pairs={{0,4},{1,5},{2,6},{3,7},{4,0},{5,1},{6,2},{7,3},{8,12},{9,13},{10,... | collective-permute-start | bytes 344072 | tf_op jit(solution)/shard_map/ppermute | solution.py:542
  6.3 0.0 collective-permute-start
  6.3 0.0 collective-permute-done.1.from_inner
  6.3 0.1 collective-permute-done.2.from_outer
  6.4 0.2 shard_map.66
  6.6 0.5 %collective-permute-start.3 = (f32[8,128]{1,0:T(8,128)S(1)}, f32[8,128]{1,0:T(8,128)S(1)}, u32[]{:S(2)}, u32[]{:S(2)}) collective-permute-start(f32[8,128]{1,0:T(8,128)S(1)} %get-tuple-element.39), channel_id=1, source_target_pairs={{0,1},{1,0},{2,3},{3,2},{4,8},{5,9},{6,10},{7,11},{8,4},{9,5},{10,... | collective-permute-start | bytes 12296 | tf_op jit(solution)/shard_map/ppermute | solution.py:546
  7.1 2.9 %collective-permute-start.4 = (f32[8,128]{1,0:T(8,128)S(1)}, f32[8,128]{1,0:T(8,128)S(1)}, u32[]{:S(2)}, u32[]{:S(2)}) collective-permute-start(f32[8,128]{1,0:T(8,128)S(1)} %get-tuple-element.40), channel_id=1, source_target_pairs={{0,4},{1,5},{2,6},{3,7},{4,0},{5,1},{6,2},{7,3},{8,12},{9,13},{10,... | collective-permute-start | bytes 12296 | tf_op jit(solution)/shard_map/ppermute | solution.py:547
  10.0 2.2 %shard_map.67 = (f32[42,3,8,384]{3,2,1,0:T(8,128)S(1)}, f32[10,8,384]{2,1,0:T(8,128)S(1)}, f32[10,8,384]{2,1,0:T(8,128)S(1)}, f32[42,8,384]{2,1,0:T(8,128)S(1)},...) custom-call(f32[32,3,8,256]{3,2,1,0:T(8,128)S(1)} %get-tuple-element, ...), custom_call_target="tpu_custom_call" | custom-call | flops 983040000 | bytes 122880000 | tf_op jit(solution)/shard_map/pallas_call | solution.py:552
  12.3 0.0 collective-permute-done.5.from_inner
  12.3 0.0 collective-permute-done.3.corner_outer
  12.3 0.0 collective-permute-done.4.corner_inner
  12.3 0.0 collective-permute-done.from_outer
  12.3 1.0 %shard_map.69 = (f32[32,1,128]{2,1,0:T(1,128)S(1)}, f32[42,3,8,384]{3,2,1,0:T(8,128)S(1)}, f32[10,8,384]{2,1,0:T(8,128)S(1)}, f32[10,8,384]{2,1,0:T(8,128)S(1)},...) custom-call(f32[28,8,128]{2,1,0:T(8,128)S(1)} %collective-permute-do, ...), custom_call_target="tpu_custom_call", output_to_operand_aliasing={{1}: (4, {}), {2}: (5, {}), {3}: (6, {}), {4}: (7, {}), {5}... | custom-call | tf_op jit(solution)/shard_map/pallas_call | solution.py:565
  13.4 11.9 %all_to_all.5.parts = f32[32,1,128]{2,1,0:T(1,128)S(1)} all-to-all(f32[32,1,128]{2,1,0:T(1,128)S(1)} %get-tuple-element.59), channel_id=1, replica_groups=mesh['gx'=8,'gy'=4] {'gx','gy'}, dimensions={0} | all-to-all | bytes 32768 | tf_op jit(solution)/shard_map/all_to_all | solution.py:571
  25.2 1.0 %shard_map.70 = f32[16,32,256]{2,1,0:T(8,128)} custom-call(f32[32,1,128]{2,1,0:T(1,128)S(1)} %all_to_all.5.parts, f32[42,3,8,384]{3,2,1,0:T(8,128)S(1)} %get-tuple-element.60.field, f32[42,2,8,384]{3,2,1,0:T(8,128)S(1)} %get-tuple-element.61.along, f32[42,2,8,384]{3,2,1,0:T(8,128)S(1)} %get-tuple-element.62.across), custom_call_target="tpu_custom_call" | custom-call | tf_op jit(solution)/shard_map/pallas_call | solution.py:572
  (2 shorter events, 0.1 us)
Async XLA Ops:
  1.6 4.8 %collective-permute-start.1 = (f32[8,8,128]{2,1,0:T(8,128)S(1)}, f32[8,8,128]{2,1,0:T(8,128)S(1)}, u32[]{:S(2)}, u32[]{:S(2)}) collective-permute-start(f32[8,8,128]{2,1,0:T(8,128)S(1)} %get-tuple-element.37), channel_id=1, source_target_pairs={{0,1},{1,0},{2,3},{3,2},{4,5},{5,4},{6,7},{7,6},{8,9},{9,8},{10,11... | collective-permute-start | bytes 98312 | tf_op jit(solution)/shard_map/ppermute | solution.py:537
  2.1 4.3 %collective-permute-start.2 = (f32[8,8,128]{2,1,0:T(8,128)S(1)}, f32[8,8,128]{2,1,0:T(8,128)S(1)}, u32[]{:S(2)}, u32[]{:S(2)}) collective-permute-start(f32[8,8,128]{2,1,0:T(8,128)S(1)} %get-tuple-element.38), channel_id=1, source_target_pairs={{0,3},{1,2},{2,1},{3,0},{4,7},{5,6},{6,5},{7,4},{8,11},{9,10},{10,... | collective-permute-start | bytes 98312 | tf_op jit(solution)/shard_map/ppermute | solution.py:538
  4.8 7.5 %collective-permute-start.5 = (f32[28,8,128]{2,1,0:T(8,128)S(1)}, f32[28,8,128]{2,1,0:T(8,128)S(1)}, u32[]{:S(2)}, u32[]{:S(2)}) collective-permute-start(f32[28,8,128]{2,1,0:T(8,128)S(1)} %get-tuple-element.42), channel_id=1, source_target_pairs={{0,4},{1,5},{2,6},{3,7},{4,0},{5,1},{6,2},{7,3},{8,12},{9,13},{10,... | collective-permute-start | bytes 344072 | tf_op jit(solution)/shard_map/ppermute | solution.py:542
  6.3 6.0 %collective-permute-start = (f32[28,8,128]{2,1,0:T(8,128)S(1)}, f32[28,8,128]{2,1,0:T(8,128)S(1)}, u32[]{:S(2)}, u32[]{:S(2)}) collective-permute-start(f32[28,8,128]{2,1,0:T(8,128)S(1)} %get-tuple-element.36), channel_id=1, source_target_pairs={{0,1},{1,0},{2,3},{3,2},{4,8},{5,9},{6,10},{7,11},{8,4},{9,5},{10,... | collective-permute-start | bytes 344072 | tf_op jit(solution)/shard_map/ppermute | solution.py:541
  6.6 5.7 %collective-permute-start.3 = (f32[8,128]{1,0:T(8,128)S(1)}, f32[8,128]{1,0:T(8,128)S(1)}, u32[]{:S(2)}, u32[]{:S(2)}) collective-permute-start(f32[8,128]{1,0:T(8,128)S(1)} %get-tuple-element.39), channel_id=1, source_target_pairs={{0,1},{1,0},{2,3},{3,2},{4,8},{5,9},{6,10},{7,11},{8,4},{9,5},{10,... | collective-permute-start | bytes 12296 | tf_op jit(solution)/shard_map/ppermute | solution.py:546
  7.1 5.2 %collective-permute-start.4 = (f32[8,128]{1,0:T(8,128)S(1)}, f32[8,128]{1,0:T(8,128)S(1)}, u32[]{:S(2)}, u32[]{:S(2)}) collective-permute-start(f32[8,128]{1,0:T(8,128)S(1)} %get-tuple-element.40), channel_id=1, source_target_pairs={{0,4},{1,5},{2,6},{3,7},{4,0},{5,1},{6,2},{7,3},{8,12},{9,13},{10,... | collective-permute-start | bytes 12296 | tf_op jit(solution)/shard_map/ppermute | solution.py:547

commit v7 on v6

--- a/solution.py
+++ b/solution.py
@@ -161,9 +161,9 @@
                 shared = jnp.where(sub == 2 * step, thin[at], jnp.where(sub == 2 * step + 1, top[at], shared))
                 rough = friction32[t, pl.ds(row, members, stride=rows), :]
                 drag = grounded[at] * rough + water_drag * icef[at]
-                own[row, 2, :, part] = drag
+                own[row + DEPTH, 2, :, part] = drag
                 place(strip, step * PLANES + 2, t, drag)
-            own_shared[strip, :, part] = shared
+            own_shared[strip + 1, :, part] = shared
             place(strip, ITEMS - 1, t, shared)
     for copy in sum(large, []):
         copy.wait()
@@ -175,7 +175,7 @@
                 icef = near[b, t][0][at : at + 1, :]
                 for plane in range(2):
                     value = vel_in[t, b, pl.ds(plane * BLOCK + at, members, stride=2 * BLOCK), :] * icef
-                    own[row, plane, :, t * LANES : (t + 1) * LANES] = value
+                    own[row + DEPTH, plane, :, t * LANES : (t + 1) * LANES] = value
                     place(strip, step * PLANES + plane, t, value)
             if step == QUAD - 1:
                 heads, tails = strips[strip]
@@ -184,14 +184,14 @@
 
 
 def edge_kernel(own, own_shared, edge_outer, edge_inner):
-    rows, _, _, cols = own.shape
-    tiles = cols // LANES
+    high, _, _, wide = own.shape
+    rows, tiles = high - 2 * DEPTH, wide // LANES - 1
     first, _, _ = neighbours("gx")
 
     def tile(up, plane, k, part):
         if plane == PLANES:
-            return own_shared[0 if up else rows // QUAD - 1, :, part]
-        return own[edge_row(plane, k, rows, up), plane, :, part]
+            return own_shared[1 if up else rows // QUAD, :, part]
+        return own[edge_row(plane, k, rows, up) + DEPTH, plane, :, part]
 
     for j, (plane, k) in enumerate(edge_items()):
         for t in range(tiles):
@@ -227,18 +227,20 @@
     strips = side_strips(from_inner, from_outer)
     first, _, _ = neighbours("gx")
 
-    def item(up, plane, k):
+    def item(up, plane, k, target):
         strip, step = divmod(edge_row(plane, k, rows, up), QUAD)
         left, right = strips(strip)
-        return unpacked(left, right, ITEMS - 1 if plane == PLANES else step * PLANES + plane, lane)
+        place = SIDE * (ITEMS - 1 if plane == PLANES else step * PLANES + plane)
+        left = pltpu.roll(left, (target - place - SIDE + CORNER) % LANES, 1)
+        right = pltpu.roll(right, (target - place + CORNER) % LANES, 1)
+        return jnp.where(lane % (2 * CORNER) < CORNER, left, right)
 
     top = jnp.zeros((members, LANES), F32)
     bottom = jnp.zeros((members, LANES), F32)
     for j, (plane, k) in enumerate(edge_items()):
         here = lane // (2 * CORNER) == j
-        shift = CORNER + 2 * CORNER * j
-        top = jnp.where(here, pltpu.roll(item(True, plane, k), shift, 1), top)
-        bottom = jnp.where(here, pltpu.roll(item(False, plane, k), shift, 1), bottom)
+        top = jnp.where(here, item(True, plane, k, 2 * CORNER * j), top)
+        bottom = jnp.where(here, item(False, plane, k, 2 * CORNER * j), bottom)
     to_inner[...] = either(first, bottom, top)
     to_outer[...] = either(first, top, bottom)
 
@@ -386,19 +388,18 @@
     return [range(k, rows - k) for k in range(1, 6)]
 
 
-def inner_kernel(own, own_shared, from_inner, from_outer, field, shared, slope, *rest):
+def inner_kernel(from_inner, from_outer, _, __, field, shared, slope, *rest):
     store, totals_ref = rest[:11], rest[11]
-    rows, _, members, cols = own.shape
+    high, _, members, wide = field.shape
+    rows, cols = high - 2 * DEPTH, wide - LANES
     lane = lane_iota((members, LANES))
     strips = side_strips(from_inner, from_outer)
     for strip in range(rows // QUAD):
         left, right = strips(strip)
-        shared[strip + 1, :, :cols] = own_shared[strip]
         shared[strip + 1, :, cols:] = unpacked(left, right, ITEMS - 1, lane)
         for step in range(QUAD):
             row = strip * QUAD + step
             for plane in range(PLANES):
-                field[row + DEPTH, plane, :, :cols] = own[row, plane]
                 field[row + DEPTH, plane, :, cols:] = unpacked(left, right, step * PLANES + plane, lane)
     totals = [jnp.zeros((members, cols), F32) for _ in range(TOTALS)]
     strips = range(1, rows // QUAD + 1)
@@ -516,10 +517,11 @@
     tiles, blocks = cols // LANES, rows // BLOCK
     tiled = pltpu.VMEM((tiles, blocks, members * parts * BLOCK, LANES), F32)
     strip = vmem((rows // QUAD, members, LANES))
+    quads = vmem((rows // QUAD + 2, members, wide))
     edge = vmem((len(edge_items()) * tiles, members, LANES))
     own, own_shared, side_inner, side_outer = call(
         pack_kernel,
-        [vmem((rows, PLANES, members, cols)), vmem((rows // QUAD, members, cols)), strip, strip],
+        [vmem((high, PLANES, members, wide)), quads, strip, strip],
         ["hbm"] * 6,
         [
             tiled,
@@ -547,14 +549,14 @@
     corner_inner = lax.ppermute(corner_inner, ("gx", "gy"), inner)
 
     one, two = vmem((high, members, wide)), vmem((high, 2, members, wide))
-    quads = vmem((rows // QUAD + 2, members, wide))
     held = [vmem((high, PLANES, members, wide)), quads, quads] + [one] * 7 + [two] * 4
     *held_now, totals = call(
         inner_kernel,
         held + [vmem((TOTALS, members, cols))],
         ["vmem"] * 4,
         flops=rows * members * wide * 10000,
-    )(own, own_shared, side_inner, side_outer)
+        aliases={2: 0, 3: 1},
+    )(side_inner, side_outer, own, own_shared)
     held_now[:2] = call(
         land_kernel,
         held[:2],

time: 26.4 us -> 26.3 us (level)
  no operation moved by 1% of the time
where the time goes in v7:
time: 26.3 us; the launch traced here: 26.2 us
  blocking collectives  11.9 us (45%)
  starting transfers between devices  8.17 us (31%)
  Pallas kernels  5.97 us (23%)
    all_to_all x1, blocking collectives, per_device(): shares = lax.all_to_all(sums, ('gx', 'gy'), 0, 0, tiled=True)  11.9 us
    ppermute x1, starting transfers between devices, per_device(): corner_inner = lax.ppermute(corner_inner, ('gx', 'gy'), inner)  2.95 us
    ppermute x1, starting transfers between devices, per_device(): side_outer = lax.ppermute(side_outer, 'gy', outer)  2.64 us
    pallas_call x1, Pallas kernels, per_device(): call(inner_kernel, held + [vmem((TOTALS, members, cols))], ['vmem'] * 4,...  2.21 us
    pallas_call x1, Pallas kernels, per_device(): call(pack_kernel, [vmem((high, PLANES, members, wide)), quads, strip, str...  1.56 us
    ppermute x1, starting transfers between devices, per_device(): edge_inner = lax.ppermute(edge_inner, ('gx', 'gy'), inner)  1.56 us
    pallas_call x1, Pallas kernels, per_device(): call(final_kernel, [jax.ShapeDtypeStruct((members * parts, rows, cols), F...  1.02 us
    pallas_call x1, Pallas kernels, per_device(): call(outer_kernel, [vmem((devices, 1, LANES))] + held, ['vmem'] * 18, ali...  1.01 us
  transfers between devices with their start and end apart: 6, of which 1 were waited for; matrix products, arithmetic and copies ran while one was open for 0% of the time, Pallas kernels for 9%

profile of v7, /device:TPU:0, one launch (start us, length us, event | category | flops | bytes accessed | tf_op | source)
XLA Modules:
  0.0 26.2 jit_solution(2077243974760101466)
XLA Ops:
  0.0 1.6 %shard_map.64 = (f32[42,3,8,384]{3,2,1,0:T(8,128)S(1)}, f32[10,8,384]{2,1,0:T(8,128)S(1)}, f32[8,8,128]{2,1,0:T(8,128)S(1)}, f32[8,8,128]{2,1,0:T(8,128)S(1)}) custom-call(f32[16,32,256]{2,1,0:T(8,128)} %bitcast.2, bf16[8,32,256]{2,1,0:T(8,128)(2,1)} %fric.1, f32[32,256]{1,0:T(8,128)} %thick.1, f32[32,256]{1,0:T(8,128)} %surf.1, s32[32,256]{1,0:T(8,128)} %ice.1, ...), custom_call_target="tpu_custom_call" | custom-call | tf_op jit(solution)/shard_map/pallas_call | solution.py:522
  1.6 0.5 %collective-permute-start.1 = (f32[8,8,128]{2,1,0:T(8,128)S(1)}, f32[8,8,128]{2,1,0:T(8,128)S(1)}, u32[]{:S(2)}, u32[]{:S(2)}) collective-permute-start(f32[8,8,128]{2,1,0:T(8,128)S(1)} %get-tuple-element.37), channel_id=1, source_target_pairs={{0,1},{1,0},{2,3},{3,2},{4,5},{5,4},{6,7},{7,6},{8,9},{9,8},{10,11... | collective-permute-start | bytes 98312 | tf_op jit(solution)/shard_map/ppermute | solution.py:539
  2.1 2.6 %collective-permute-start.2 = (f32[8,8,128]{2,1,0:T(8,128)S(1)}, f32[8,8,128]{2,1,0:T(8,128)S(1)}, u32[]{:S(2)}, u32[]{:S(2)}) collective-permute-start(f32[8,8,128]{2,1,0:T(8,128)S(1)} %get-tuple-element.38), channel_id=1, source_target_pairs={{0,3},{1,2},{2,1},{3,0},{4,7},{5,6},{6,5},{7,4},{8,11},{9,10},{10,... | collective-permute-start | bytes 98312 | tf_op jit(solution)/shard_map/ppermute | solution.py:540
  4.8 1.6 %collective-permute-start.5 = (f32[28,8,128]{2,1,0:T(8,128)S(1)}, f32[28,8,128]{2,1,0:T(8,128)S(1)}, u32[]{:S(2)}, u32[]{:S(2)}) collective-permute-start(f32[28,8,128]{2,1,0:T(8,128)S(1)} %get-tuple-element.42), channel_id=1, source_target_pairs={{0,4},{1,5},{2,6},{3,7},{4,0},{5,1},{6,2},{7,3},{8,12},{9,13},{10,... | collective-permute-start | bytes 344072 | tf_op jit(solution)/shard_map/ppermute | solution.py:544
  6.3 0.0 collective-permute-start
  6.3 0.0 collective-permute-done.1.from_inner
  6.3 0.1 collective-permute-done.2.from_outer
  6.4 0.1 shard_map.66
  6.5 0.5 %collective-permute-start.3 = (f32[8,128]{1,0:T(8,128)S(1)}, f32[8,128]{1,0:T(8,128)S(1)}, u32[]{:S(2)}, u32[]{:S(2)}) collective-permute-start(f32[8,128]{1,0:T(8,128)S(1)} %get-tuple-element.39), channel_id=1, source_target_pairs={{0,1},{1,0},{2,3},{3,2},{4,8},{5,9},{6,10},{7,11},{8,4},{9,5},{10,... | collective-permute-start | bytes 12296 | tf_op jit(solution)/shard_map/ppermute | solution.py:548
  7.0 2.9 %collective-permute-start.4 = (f32[8,128]{1,0:T(8,128)S(1)}, f32[8,128]{1,0:T(8,128)S(1)}, u32[]{:S(2)}, u32[]{:S(2)}) collective-permute-start(f32[8,128]{1,0:T(8,128)S(1)} %get-tuple-element.40), channel_id=1, source_target_pairs={{0,4},{1,5},{2,6},{3,7},{4,0},{5,1},{6,2},{7,3},{8,12},{9,13},{10,... | collective-permute-start | bytes 12296 | tf_op jit(solution)/shard_map/ppermute | solution.py:549
  10.0 2.2 %shard_map.67 = (f32[42,3,8,384]{3,2,1,0:T(8,128)S(1)}, f32[10,8,384]{2,1,0:T(8,128)S(1)}, f32[10,8,384]{2,1,0:T(8,128)S(1)}, f32[42,8,384]{2,1,0:T(8,128)S(1)},...) custom-call(f32[8,8,128]{2,1,0:T(8,128)S(1)} %collective-permute-don, ...), custom_call_target="tpu_custom_call", output_to_operand_aliasing={{0}: (2, {}), {1}: (3, {})} | custom-call | flops 983040000 | bytes 122880000 | tf_op jit(solution)/shard_map/pallas_call | solution.py:553
  12.2 0.0 collective-permute-done.5.from_inner
  12.2 0.0 collective-permute-done.3.corner_outer
  12.2 0.0 collective-permute-done.4.corner_inner
  12.3 0.0 collective-permute-done.from_outer
  12.3 1.0 %shard_map.69 = (f32[32,1,128]{2,1,0:T(1,128)S(1)}, f32[42,3,8,384]{3,2,1,0:T(8,128)S(1)}, f32[10,8,384]{2,1,0:T(8,128)S(1)}, f32[10,8,384]{2,1,0:T(8,128)S(1)},...) custom-call(f32[28,8,128]{2,1,0:T(8,128)S(1)} %collective-permute-do, ...), custom_call_target="tpu_custom_call", output_to_operand_aliasing={{1}: (4, {}), {2}: (5, {}), {3}: (6, {}), {4}: (7, {}), {5}... | custom-call | tf_op jit(solution)/shard_map/pallas_call | solution.py:567
  13.3 11.9 %all_to_all.5.parts = f32[32,1,128]{2,1,0:T(1,128)S(1)} all-to-all(f32[32,1,128]{2,1,0:T(1,128)S(1)} %get-tuple-element.59), channel_id=1, replica_groups=mesh['gx'=8,'gy'=4] {'gx','gy'}, dimensions={0} | all-to-all | bytes 32768 | tf_op jit(solution)/shard_map/all_to_all | solution.py:573
  25.1 1.0 %shard_map.70 = f32[16,32,256]{2,1,0:T(8,128)} custom-call(f32[32,1,128]{2,1,0:T(1,128)S(1)} %all_to_all.5.parts, f32[42,3,8,384]{3,2,1,0:T(8,128)S(1)} %get-tuple-element.60.field, f32[42,2,8,384]{3,2,1,0:T(8,128)S(1)} %get-tuple-element.61.along, f32[42,2,8,384]{3,2,1,0:T(8,128)S(1)} %get-tuple-element.62.across), custom_call_target="tpu_custom_call" | custom-call | tf_op jit(solution)/shard_map/pallas_call | solution.py:574
  (2 shorter events, 0.1 us)
Async XLA Ops:
  1.6 4.8 %collective-permute-start.1 = (f32[8,8,128]{2,1,0:T(8,128)S(1)}, f32[8,8,128]{2,1,0:T(8,128)S(1)}, u32[]{:S(2)}, u32[]{:S(2)}) collective-permute-start(f32[8,8,128]{2,1,0:T(8,128)S(1)} %get-tuple-element.37), channel_id=1, source_target_pairs={{0,1},{1,0},{2,3},{3,2},{4,5},{5,4},{6,7},{7,6},{8,9},{9,8},{10,11... | collective-permute-start | bytes 98312 | tf_op jit(solution)/shard_map/ppermute | solution.py:539
  2.1 4.3 %collective-permute-start.2 = (f32[8,8,128]{2,1,0:T(8,128)S(1)}, f32[8,8,128]{2,1,0:T(8,128)S(1)}, u32[]{:S(2)}, u32[]{:S(2)}) collective-permute-start(f32[8,8,128]{2,1,0:T(8,128)S(1)} %get-tuple-element.38), channel_id=1, source_target_pairs={{0,3},{1,2},{2,1},{3,0},{4,7},{5,6},{6,5},{7,4},{8,11},{9,10},{10,... | collective-permute-start | bytes 98312 | tf_op jit(solution)/shard_map/ppermute | solution.py:540
  4.8 7.4 %collective-permute-start.5 = (f32[28,8,128]{2,1,0:T(8,128)S(1)}, f32[28,8,128]{2,1,0:T(8,128)S(1)}, u32[]{:S(2)}, u32[]{:S(2)}) collective-permute-start(f32[28,8,128]{2,1,0:T(8,128)S(1)} %get-tuple-element.42), channel_id=1, source_target_pairs={{0,4},{1,5},{2,6},{3,7},{4,0},{5,1},{6,2},{7,3},{8,12},{9,13},{10,... | collective-permute-start | bytes 344072 | tf_op jit(solution)/shard_map/ppermute | solution.py:544
  6.3 5.9 %collective-permute-start = (f32[28,8,128]{2,1,0:T(8,128)S(1)}, f32[28,8,128]{2,1,0:T(8,128)S(1)}, u32[]{:S(2)}, u32[]{:S(2)}) collective-permute-start(f32[28,8,128]{2,1,0:T(8,128)S(1)} %get-tuple-element.36), channel_id=1, source_target_pairs={{0,1},{1,0},{2,3},{3,2},{4,8},{5,9},{6,10},{7,11},{8,4},{9,5},{10,... | collective-permute-start | bytes 344072 | tf_op jit(solution)/shard_map/ppermute | solution.py:543
  6.5 5.7 %collective-permute-start.3 = (f32[8,128]{1,0:T(8,128)S(1)}, f32[8,128]{1,0:T(8,128)S(1)}, u32[]{:S(2)}, u32[]{:S(2)}) collective-permute-start(f32[8,128]{1,0:T(8,128)S(1)} %get-tuple-element.39), channel_id=1, source_target_pairs={{0,1},{1,0},{2,3},{3,2},{4,8},{5,9},{6,10},{7,11},{8,4},{9,5},{10,... | collective-permute-start | bytes 12296 | tf_op jit(solution)/shard_map/ppermute | solution.py:548
  7.0 5.2 %collective-permute-start.4 = (f32[8,128]{1,0:T(8,128)S(1)}, f32[8,128]{1,0:T(8,128)S(1)}, u32[]{:S(2)}, u32[]{:S(2)}) collective-permute-start(f32[8,128]{1,0:T(8,128)S(1)} %get-tuple-element.40), channel_id=1, source_target_pairs={{0,4},{1,5},{2,6},{3,7},{4,0},{5,1},{6,2},{7,3},{8,12},{9,13},{10,... | collective-permute-start | bytes 12296 | tf_op jit(solution)/shard_map/ppermute | solution.py:549

commit v8 on v7

--- a/solution.py
+++ b/solution.py
@@ -10,6 +10,7 @@
 strain_floor = 0.1
 water_drag = 0.25
 flow_power = 1.0 / 3.0
+viscosity_factor = 0.5 * 4.0**flow_power
 
 most_step = 1.0 + 2.5 * 2.25 * strain_floor**-flow_power / water_drag
 
@@ -138,7 +139,7 @@
         for t in range(tiles):
             at = (slice(b * BLOCK, (b + 1) * BLOCK), slice(t * LANES, (t + 1) * LANES))
             icef = ice_in[at].astype(F32)
-            near[b, t] = (icef, icef * ground_in[at].astype(F32), icef * thick_in[at], surf_in[at])
+            near[b, t] = (icef, icef * ground_in[at].astype(F32), (viscosity_factor * icef) * thick_in[at], surf_in[at])
     strips = [[jnp.zeros((members, LANES), F32)] * 2 for _ in range(rows // QUAD)]
 
     def place(strip, item, t, value):
@@ -293,11 +294,13 @@
             (after(u) - before(u)) + (ref[row + 1, 1] - ref[row - 1, 1]),
         )
 
-    def stress(x, y, z, row, strain_u, strain_v, strain_c, nu):
-        half = 0.5 * nu
-        x[row + DEPTH] = half * (2.0 * strain_u + strain_v)
-        y[row + DEPTH] = half * (strain_u + 2.0 * strain_v)
-        z[row + DEPTH] = half * (0.5 * strain_c)
+    def leans(strain_u, strain_v, strain_c):
+        return strain_u + 0.5 * strain_v, strain_v + 0.5 * strain_u, 0.25 * strain_c
+
+    def stress(x, y, z, row, nu, p, q, c):
+        x[row + DEPTH] = nu * p
+        y[row + DEPTH] = nu * q
+        z[row + DEPTH] = nu * c
 
     def divergence(x, y, z, row):
         row = row + DEPTH
@@ -309,10 +312,11 @@
 
     def viscosity(row):
         su, sv, sc = strains(field, row)
-        square = 0.25 * (su * su + sv * sv + su * sv + 0.25 * (sc * sc)) + strain_floor
-        nu = (0.5 * spread(shared, row, 0)) * jnp.exp(-flow_power * jnp.log(square))
+        p, q, c = leans(su, sv, sc)
+        square = (su * p + sv * q + sc * c) + 4.0 * strain_floor
+        nu = spread(shared, row, 0) * jnp.exp(-flow_power * jnp.log(square))
         visc[row + DEPTH] = nu
-        stress(sx, sy, sz, row, su, sv, sc, nu)
+        stress(sx, sy, sz, row, nu, p, q, c)
 
     def reciprocal(value):
         guess = pltpu.reciprocal(value, approx=True)
@@ -323,7 +327,7 @@
         at = row + DEPTH
         drag = field[at, 2]
         on = drag > 0.0
-        half = 0.5 * spread(shared, row, 0)
+        half = (0.5 / viscosity_factor) * spread(shared, row, 0)
         force_u = half * (spread(shared, row - 1, 1) - spread(shared, row + 1, 1))
         force_v = half * spread(slope, row, 1)
         res_u = force_u - (drag * field[at, 0] - jnp.where(on, div_u, 0.0))
@@ -342,7 +346,7 @@
 
     def direction(row):
         su, sv, sc = strains(along, row)
-        stress(tx, ty, tz, row, su, sv, sc, visc[row + DEPTH])
+        stress(tx, ty, tz, row, visc[row + DEPTH], *leans(su, sv, sc))
 
     def image(row, totals):
         div_u, div_v = divergence(tx, ty, tz, row)
@@ -366,7 +370,7 @@
         su, sv, sc = strains(across, row)
         at = row + DEPTH
         u, v = across[at, 0], across[at, 1]
-        power = field[at, 2] * (u * u + v * v) + visc[at] * (su * su + su * sv + sv * sv + 0.25 * (sc * sc))
+        power = field[at, 2] * (u * u + v * v) + visc[at] * (su * (su + sv) + sv * sv + 0.25 * (sc * sc))
         totals[3] += power[:, :cols]
 
     return incline, viscosity, residual, direction, image, energy

time: 26.3 us -> 26.3 us (level)
  no operation moved by 1% of the time
where the time goes in v8:
time: 26.3 us; the launch traced here: 26.1 us
  blocking collectives  11.9 us (45%)
  starting transfers between devices  8.17 us (31%)
  Pallas kernels  5.91 us (22%)
    all_to_all x1, blocking collectives, per_device(): shares = lax.all_to_all(sums, ('gx', 'gy'), 0, 0, tiled=True)  11.9 us
    ppermute x1, starting transfers between devices, per_device(): corner_inner = lax.ppermute(corner_inner, ('gx', 'gy'), inner)  2.95 us
    ppermute x1, starting transfers between devices, per_device(): side_outer = lax.ppermute(side_outer, 'gy', outer)  2.64 us
    pallas_call x1, Pallas kernels, per_device(): call(inner_kernel, held + [vmem((TOTALS, members, cols))], ['vmem'] * 4,...  2.16 us
    pallas_call x1, Pallas kernels, per_device(): call(pack_kernel, [vmem((high, PLANES, members, wide)), quads, strip, str...  1.56 us
    ppermute x1, starting transfers between devices, per_device(): edge_inner = lax.ppermute(edge_inner, ('gx', 'gy'), inner)  1.56 us
    pallas_call x1, Pallas kernels, per_device(): call(final_kernel, [jax.ShapeDtypeStruct((members * parts, rows, cols), F...  1.02 us
    pallas_call x1, Pallas kernels, per_device(): call(outer_kernel, [vmem((devices, 1, LANES))] + held, ['vmem'] * 18, ali...  1.01 us
  transfers between devices with their start and end apart: 6, of which 1 were waited for; matrix products, arithmetic and copies ran while one was open for 0% of the time, Pallas kernels for 9%

profile of v8, /device:TPU:0, one launch (start us, length us, event | category | flops | bytes accessed | tf_op | source)
XLA Modules:
  0.0 26.1 jit_solution(4176837114082622070)
XLA Ops:
  0.0 1.6 %shard_map.64 = (f32[42,3,8,384]{3,2,1,0:T(8,128)S(1)}, f32[10,8,384]{2,1,0:T(8,128)S(1)}, f32[8,8,128]{2,1,0:T(8,128)S(1)}, f32[8,8,128]{2,1,0:T(8,128)S(1)}) custom-call(f32[16,32,256]{2,1,0:T(8,128)} %bitcast.2, bf16[8,32,256]{2,1,0:T(8,128)(2,1)} %fric.1, f32[32,256]{1,0:T(8,128)} %thick.1, f32[32,256]{1,0:T(8,128)} %surf.1, s32[32,256]{1,0:T(8,128)} %ice.1, ...), custom_call_target="tpu_custom_call" | custom-call | tf_op jit(solution)/shard_map/pallas_call | solution.py:526
  1.6 0.5 %collective-permute-start.1 = (f32[8,8,128]{2,1,0:T(8,128)S(1)}, f32[8,8,128]{2,1,0:T(8,128)S(1)}, u32[]{:S(2)}, u32[]{:S(2)}) collective-permute-start(f32[8,8,128]{2,1,0:T(8,128)S(1)} %get-tuple-element.37), channel_id=1, source_target_pairs={{0,1},{1,0},{2,3},{3,2},{4,5},{5,4},{6,7},{7,6},{8,9},{9,8},{10,11... | collective-permute-start | bytes 98312 | tf_op jit(solution)/shard_map/ppermute | solution.py:543
  2.1 2.6 %collective-permute-start.2 = (f32[8,8,128]{2,1,0:T(8,128)S(1)}, f32[8,8,128]{2,1,0:T(8,128)S(1)}, u32[]{:S(2)}, u32[]{:S(2)}) collective-permute-start(f32[8,8,128]{2,1,0:T(8,128)S(1)} %get-tuple-element.38), channel_id=1, source_target_pairs={{0,3},{1,2},{2,1},{3,0},{4,7},{5,6},{6,5},{7,4},{8,11},{9,10},{10,... | collective-permute-start | bytes 98312 | tf_op jit(solution)/shard_map/ppermute | solution.py:544
  4.8 1.6 %collective-permute-start.5 = (f32[28,8,128]{2,1,0:T(8,128)S(1)}, f32[28,8,128]{2,1,0:T(8,128)S(1)}, u32[]{:S(2)}, u32[]{:S(2)}) collective-permute-start(f32[28,8,128]{2,1,0:T(8,128)S(1)} %get-tuple-element.42), channel_id=1, source_target_pairs={{0,4},{1,5},{2,6},{3,7},{4,0},{5,1},{6,2},{7,3},{8,12},{9,13},{10,... | collective-permute-start | bytes 344072 | tf_op jit(solution)/shard_map/ppermute | solution.py:548
  6.3 0.0 collective-permute-start
  6.3 0.0 collective-permute-done.1.from_inner
  6.3 0.1 collective-permute-done.2.from_outer
  6.4 0.1 shard_map.66
  6.5 0.5 %collective-permute-start.3 = (f32[8,128]{1,0:T(8,128)S(1)}, f32[8,128]{1,0:T(8,128)S(1)}, u32[]{:S(2)}, u32[]{:S(2)}) collective-permute-start(f32[8,128]{1,0:T(8,128)S(1)} %get-tuple-element.39), channel_id=1, source_target_pairs={{0,1},{1,0},{2,3},{3,2},{4,8},{5,9},{6,10},{7,11},{8,4},{9,5},{10,... | collective-permute-start | bytes 12296 | tf_op jit(solution)/shard_map/ppermute | solution.py:552
  7.0 2.9 %collective-permute-start.4 = (f32[8,128]{1,0:T(8,128)S(1)}, f32[8,128]{1,0:T(8,128)S(1)}, u32[]{:S(2)}, u32[]{:S(2)}) collective-permute-start(f32[8,128]{1,0:T(8,128)S(1)} %get-tuple-element.40), channel_id=1, source_target_pairs={{0,4},{1,5},{2,6},{3,7},{4,0},{5,1},{6,2},{7,3},{8,12},{9,13},{10,... | collective-permute-start | bytes 12296 | tf_op jit(solution)/shard_map/ppermute | solution.py:553
  10.0 2.2 %shard_map.67 = (f32[42,3,8,384]{3,2,1,0:T(8,128)S(1)}, f32[10,8,384]{2,1,0:T(8,128)S(1)}, f32[10,8,384]{2,1,0:T(8,128)S(1)}, f32[42,8,384]{2,1,0:T(8,128)S(1)},...) custom-call(f32[8,8,128]{2,1,0:T(8,128)S(1)} %collective-permute-don, ...), custom_call_target="tpu_custom_call", output_to_operand_aliasing={{0}: (2, {}), {1}: (3, {})} | custom-call | flops 983040000 | bytes 122880000 | tf_op jit(solution)/shard_map/pallas_call | solution.py:557
  12.1 0.0 collective-permute-done.5.from_inner
  12.2 0.0 collective-permute-done.3.corner_outer
  12.2 0.0 collective-permute-done.4.corner_inner
  12.2 0.0 collective-permute-done.from_outer
  12.2 1.0 %shard_map.69 = (f32[32,1,128]{2,1,0:T(1,128)S(1)}, f32[42,3,8,384]{3,2,1,0:T(8,128)S(1)}, f32[10,8,384]{2,1,0:T(8,128)S(1)}, f32[10,8,384]{2,1,0:T(8,128)S(1)},...) custom-call(f32[28,8,128]{2,1,0:T(8,128)S(1)} %collective-permute-do, ...), custom_call_target="tpu_custom_call", output_to_operand_aliasing={{1}: (4, {}), {2}: (5, {}), {3}: (6, {}), {4}: (7, {}), {5}... | custom-call | tf_op jit(solution)/shard_map/pallas_call | solution.py:571
  13.2 11.9 %all_to_all.5.parts = f32[32,1,128]{2,1,0:T(1,128)S(1)} all-to-all(f32[32,1,128]{2,1,0:T(1,128)S(1)} %get-tuple-element.59), channel_id=1, replica_groups=mesh['gx'=8,'gy'=4] {'gx','gy'}, dimensions={0} | all-to-all | bytes 32768 | tf_op jit(solution)/shard_map/all_to_all | solution.py:577
  25.1 1.0 %shard_map.70 = f32[16,32,256]{2,1,0:T(8,128)} custom-call(f32[32,1,128]{2,1,0:T(1,128)S(1)} %all_to_all.5.parts, f32[42,3,8,384]{3,2,1,0:T(8,128)S(1)} %get-tuple-element.60.field, f32[42,2,8,384]{3,2,1,0:T(8,128)S(1)} %get-tuple-element.61.along, f32[42,2,8,384]{3,2,1,0:T(8,128)S(1)} %get-tuple-element.62.across), custom_call_target="tpu_custom_call" | custom-call | tf_op jit(solution)/shard_map/pallas_call | solution.py:578
  (2 shorter events, 0.1 us)
Async XLA Ops:
  1.6 4.8 %collective-permute-start.1 = (f32[8,8,128]{2,1,0:T(8,128)S(1)}, f32[8,8,128]{2,1,0:T(8,128)S(1)}, u32[]{:S(2)}, u32[]{:S(2)}) collective-permute-start(f32[8,8,128]{2,1,0:T(8,128)S(1)} %get-tuple-element.37), channel_id=1, source_target_pairs={{0,1},{1,0},{2,3},{3,2},{4,5},{5,4},{6,7},{7,6},{8,9},{9,8},{10,11... | collective-permute-start | bytes 98312 | tf_op jit(solution)/shard_map/ppermute | solution.py:543
  2.1 4.3 %collective-permute-start.2 = (f32[8,8,128]{2,1,0:T(8,128)S(1)}, f32[8,8,128]{2,1,0:T(8,128)S(1)}, u32[]{:S(2)}, u32[]{:S(2)}) collective-permute-start(f32[8,8,128]{2,1,0:T(8,128)S(1)} %get-tuple-element.38), channel_id=1, source_target_pairs={{0,3},{1,2},{2,1},{3,0},{4,7},{5,6},{6,5},{7,4},{8,11},{9,10},{10,... | collective-permute-start | bytes 98312 | tf_op jit(solution)/shard_map/ppermute | solution.py:544
  4.8 7.4 %collective-permute-start.5 = (f32[28,8,128]{2,1,0:T(8,128)S(1)}, f32[28,8,128]{2,1,0:T(8,128)S(1)}, u32[]{:S(2)}, u32[]{:S(2)}) collective-permute-start(f32[28,8,128]{2,1,0:T(8,128)S(1)} %get-tuple-element.42), channel_id=1, source_target_pairs={{0,4},{1,5},{2,6},{3,7},{4,0},{5,1},{6,2},{7,3},{8,12},{9,13},{10,... | collective-permute-start | bytes 344072 | tf_op jit(solution)/shard_map/ppermute | solution.py:548
  6.3 5.9 %collective-permute-start = (f32[28,8,128]{2,1,0:T(8,128)S(1)}, f32[28,8,128]{2,1,0:T(8,128)S(1)}, u32[]{:S(2)}, u32[]{:S(2)}) collective-permute-start(f32[28,8,128]{2,1,0:T(8,128)S(1)} %get-tuple-element.36), channel_id=1, source_target_pairs={{0,1},{1,0},{2,3},{3,2},{4,8},{5,9},{6,10},{7,11},{8,4},{9,5},{10,... | collective-permute-start | bytes 344072 | tf_op jit(solution)/shard_map/ppermute | solution.py:547
  6.5 5.7 %collective-permute-start.3 = (f32[8,128]{1,0:T(8,128)S(1)}, f32[8,128]{1,0:T(8,128)S(1)}, u32[]{:S(2)}, u32[]{:S(2)}) collective-permute-start(f32[8,128]{1,0:T(8,128)S(1)} %get-tuple-element.39), channel_id=1, source_target_pairs={{0,1},{1,0},{2,3},{3,2},{4,8},{5,9},{6,10},{7,11},{8,4},{9,5},{10,... | collective-permute-start | bytes 12296 | tf_op jit(solution)/shard_map/ppermute | solution.py:552
  7.0 5.2 %collective-permute-start.4 = (f32[8,128]{1,0:T(8,128)S(1)}, f32[8,128]{1,0:T(8,128)S(1)}, u32[]{:S(2)}, u32[]{:S(2)}) collective-permute-start(f32[8,128]{1,0:T(8,128)S(1)} %get-tuple-element.40), channel_id=1, source_target_pairs={{0,4},{1,5},{2,6},{3,7},{4,0},{5,1},{6,2},{7,3},{8,12},{9,13},{10,... | collective-permute-start | bytes 12296 | tf_op jit(solution)/shard_map/ppermute | solution.py:553

commit v9 on v8

--- a/solution.py
+++ b/solution.py
@@ -297,9 +297,10 @@
     def leans(strain_u, strain_v, strain_c):
         return strain_u + 0.5 * strain_v, strain_v + 0.5 * strain_u, 0.25 * strain_c
 
-    def stress(x, y, z, row, nu, p, q, c):
+    def stress(x, y, z, row, nu, p, q, c, reach):
         x[row + DEPTH] = nu * p
-        y[row + DEPTH] = nu * q
+        if -reach < row < rows - 1 + reach:
+            y[row + DEPTH] = nu * q
         z[row + DEPTH] = nu * c
 
     def divergence(x, y, z, row):
@@ -316,7 +317,7 @@
         square = (su * p + sv * q + sc * c) + 4.0 * strain_floor
         nu = spread(shared, row, 0) * jnp.exp(-flow_power * jnp.log(square))
         visc[row + DEPTH] = nu
-        stress(sx, sy, sz, row, nu, p, q, c)
+        stress(sx, sy, sz, row, nu, p, q, c, DEPTH - 1)
 
     def reciprocal(value):
         guess = pltpu.reciprocal(value, approx=True)
@@ -346,7 +347,7 @@
 
     def direction(row):
         su, sv, sc = strains(along, row)
-        stress(tx, ty, tz, row, visc[row + DEPTH], *leans(su, sv, sc))
+        stress(tx, ty, tz, row, visc[row + DEPTH], *leans(su, sv, sc), DEPTH - 3)
 
     def image(row, totals):
         div_u, div_v = divergence(tx, ty, tz, row)

time: 26.3 us -> 26.3 us (level)
  no operation moved by 1% of the time
where the time goes in v9:
time: 26.3 us; the launch traced here: 26.1 us
  blocking collectives  11.9 us (45%)
  starting transfers between devices  8.17 us (31%)
  Pallas kernels  5.91 us (22%)
    all_to_all x1, blocking collectives, per_device(): shares = lax.all_to_all(sums, ('gx', 'gy'), 0, 0, tiled=True)  11.9 us
    ppermute x1, starting transfers between devices, per_device(): corner_inner = lax.ppermute(corner_inner, ('gx', 'gy'), inner)  2.95 us
    ppermute x1, starting transfers between devices, per_device(): side_outer = lax.ppermute(side_outer, 'gy', outer)  2.64 us
    pallas_call x1, Pallas kernels, per_device(): call(inner_kernel, held + [vmem((TOTALS, members, cols))], ['vmem'] * 4,...  2.16 us
    pallas_call x1, Pallas kernels, per_device(): call(pack_kernel, [vmem((high, PLANES, members, wide)), quads, strip, str...  1.56 us
    ppermute x1, starting transfers between devices, per_device(): edge_inner = lax.ppermute(edge_inner, ('gx', 'gy'), inner)  1.56 us
    pallas_call x1, Pallas kernels, per_device(): call(final_kernel, [jax.ShapeDtypeStruct((members * parts, rows, cols), F...  1.02 us
    pallas_call x1, Pallas kernels, per_device(): call(outer_kernel, [vmem((devices, 1, LANES))] + held, ['vmem'] * 18, ali...  1.01 us
  transfers between devices with their start and end apart: 6, of which 1 were waited for; matrix products, arithmetic and copies ran while one was open for 0% of the time, Pallas kernels for 9%

profile of v9, /device:TPU:0, one launch (start us, length us, event | category | flops | bytes accessed | tf_op | source)
XLA Modules:
  0.0 26.1 jit_solution(3047829275905223575)
XLA Ops:
  0.0 1.6 %shard_map.64 = (f32[42,3,8,384]{3,2,1,0:T(8,128)S(1)}, f32[10,8,384]{2,1,0:T(8,128)S(1)}, f32[8,8,128]{2,1,0:T(8,128)S(1)}, f32[8,8,128]{2,1,0:T(8,128)S(1)}) custom-call(f32[16,32,256]{2,1,0:T(8,128)} %bitcast.2, bf16[8,32,256]{2,1,0:T(8,128)(2,1)} %fric.1, f32[32,256]{1,0:T(8,128)} %thick.1, f32[32,256]{1,0:T(8,128)} %surf.1, s32[32,256]{1,0:T(8,128)} %ice.1, ...), custom_call_target="tpu_custom_call" | custom-call | tf_op jit(solution)/shard_map/pallas_call | solution.py:527
  1.6 0.5 %collective-permute-start.1 = (f32[8,8,128]{2,1,0:T(8,128)S(1)}, f32[8,8,128]{2,1,0:T(8,128)S(1)}, u32[]{:S(2)}, u32[]{:S(2)}) collective-permute-start(f32[8,8,128]{2,1,0:T(8,128)S(1)} %get-tuple-element.37), channel_id=1, source_target_pairs={{0,1},{1,0},{2,3},{3,2},{4,5},{5,4},{6,7},{7,6},{8,9},{9,8},{10,11... | collective-permute-start | bytes 98312 | tf_op jit(solution)/shard_map/ppermute | solution.py:544
  2.1 2.6 %collective-permute-start.2 = (f32[8,8,128]{2,1,0:T(8,128)S(1)}, f32[8,8,128]{2,1,0:T(8,128)S(1)}, u32[]{:S(2)}, u32[]{:S(2)}) collective-permute-start(f32[8,8,128]{2,1,0:T(8,128)S(1)} %get-tuple-element.38), channel_id=1, source_target_pairs={{0,3},{1,2},{2,1},{3,0},{4,7},{5,6},{6,5},{7,4},{8,11},{9,10},{10,... | collective-permute-start | bytes 98312 | tf_op jit(solution)/shard_map/ppermute | solution.py:545
  4.8 1.6 %collective-permute-start.5 = (f32[28,8,128]{2,1,0:T(8,128)S(1)}, f32[28,8,128]{2,1,0:T(8,128)S(1)}, u32[]{:S(2)}, u32[]{:S(2)}) collective-permute-start(f32[28,8,128]{2,1,0:T(8,128)S(1)} %get-tuple-element.42), channel_id=1, source_target_pairs={{0,4},{1,5},{2,6},{3,7},{4,0},{5,1},{6,2},{7,3},{8,12},{9,13},{10,... | collective-permute-start | bytes 344072 | tf_op jit(solution)/shard_map/ppermute | solution.py:549
  6.3 0.0 collective-permute-start
  6.3 0.0 collective-permute-done.1.from_inner
  6.3 0.1 collective-permute-done.2.from_outer
  6.4 0.1 shard_map.66
  6.5 0.5 %collective-permute-start.3 = (f32[8,128]{1,0:T(8,128)S(1)}, f32[8,128]{1,0:T(8,128)S(1)}, u32[]{:S(2)}, u32[]{:S(2)}) collective-permute-start(f32[8,128]{1,0:T(8,128)S(1)} %get-tuple-element.39), channel_id=1, source_target_pairs={{0,1},{1,0},{2,3},{3,2},{4,8},{5,9},{6,10},{7,11},{8,4},{9,5},{10,... | collective-permute-start | bytes 12296 | tf_op jit(solution)/shard_map/ppermute | solution.py:553
  7.0 2.9 %collective-permute-start.4 = (f32[8,128]{1,0:T(8,128)S(1)}, f32[8,128]{1,0:T(8,128)S(1)}, u32[]{:S(2)}, u32[]{:S(2)}) collective-permute-start(f32[8,128]{1,0:T(8,128)S(1)} %get-tuple-element.40), channel_id=1, source_target_pairs={{0,4},{1,5},{2,6},{3,7},{4,0},{5,1},{6,2},{7,3},{8,12},{9,13},{10,... | collective-permute-start | bytes 12296 | tf_op jit(solution)/shard_map/ppermute | solution.py:554
  10.0 2.2 %shard_map.67 = (f32[42,3,8,384]{3,2,1,0:T(8,128)S(1)}, f32[10,8,384]{2,1,0:T(8,128)S(1)}, f32[10,8,384]{2,1,0:T(8,128)S(1)}, f32[42,8,384]{2,1,0:T(8,128)S(1)},...) custom-call(f32[8,8,128]{2,1,0:T(8,128)S(1)} %collective-permute-don, ...), custom_call_target="tpu_custom_call", output_to_operand_aliasing={{0}: (2, {}), {1}: (3, {})} | custom-call | flops 983040000 | bytes 122880000 | tf_op jit(solution)/shard_map/pallas_call | solution.py:558
  12.1 0.0 collective-permute-done.5.from_inner
  12.2 0.0 collective-permute-done.3.corner_outer
  12.2 0.0 collective-permute-done.4.corner_inner
  12.2 0.0 collective-permute-done.from_outer
  12.2 1.0 %shard_map.69 = (f32[32,1,128]{2,1,0:T(1,128)S(1)}, f32[42,3,8,384]{3,2,1,0:T(8,128)S(1)}, f32[10,8,384]{2,1,0:T(8,128)S(1)}, f32[10,8,384]{2,1,0:T(8,128)S(1)},...) custom-call(f32[28,8,128]{2,1,0:T(8,128)S(1)} %collective-permute-do, ...), custom_call_target="tpu_custom_call", output_to_operand_aliasing={{1}: (4, {}), {2}: (5, {}), {3}: (6, {}), {4}: (7, {}), {5}... | custom-call | tf_op jit(solution)/shard_map/pallas_call | solution.py:572
  13.2 11.9 %all_to_all.5.parts = f32[32,1,128]{2,1,0:T(1,128)S(1)} all-to-all(f32[32,1,128]{2,1,0:T(1,128)S(1)} %get-tuple-element.59), channel_id=1, replica_groups=mesh['gx'=8,'gy'=4] {'gx','gy'}, dimensions={0} | all-to-all | bytes 32768 | tf_op jit(solution)/shard_map/all_to_all | solution.py:578
  25.1 1.0 %shard_map.70 = f32[16,32,256]{2,1,0:T(8,128)} custom-call(f32[32,1,128]{2,1,0:T(1,128)S(1)} %all_to_all.5.parts, f32[42,3,8,384]{3,2,1,0:T(8,128)S(1)} %get-tuple-element.60.field, f32[42,2,8,384]{3,2,1,0:T(8,128)S(1)} %get-tuple-element.61.along, f32[42,2,8,384]{3,2,1,0:T(8,128)S(1)} %get-tuple-element.62.across), custom_call_target="tpu_custom_call" | custom-call | tf_op jit(solution)/shard_map/pallas_call | solution.py:579
  (2 shorter events, 0.1 us)
Async XLA Ops:
  1.6 4.8 %collective-permute-start.1 = (f32[8,8,128]{2,1,0:T(8,128)S(1)}, f32[8,8,128]{2,1,0:T(8,128)S(1)}, u32[]{:S(2)}, u32[]{:S(2)}) collective-permute-start(f32[8,8,128]{2,1,0:T(8,128)S(1)} %get-tuple-element.37), channel_id=1, source_target_pairs={{0,1},{1,0},{2,3},{3,2},{4,5},{5,4},{6,7},{7,6},{8,9},{9,8},{10,11... | collective-permute-start | bytes 98312 | tf_op jit(solution)/shard_map/ppermute | solution.py:544
  2.1 4.3 %collective-permute-start.2 = (f32[8,8,128]{2,1,0:T(8,128)S(1)}, f32[8,8,128]{2,1,0:T(8,128)S(1)}, u32[]{:S(2)}, u32[]{:S(2)}) collective-permute-start(f32[8,8,128]{2,1,0:T(8,128)S(1)} %get-tuple-element.38), channel_id=1, source_target_pairs={{0,3},{1,2},{2,1},{3,0},{4,7},{5,6},{6,5},{7,4},{8,11},{9,10},{10,... | collective-permute-start | bytes 98312 | tf_op jit(solution)/shard_map/ppermute | solution.py:545
  4.8 7.4 %collective-permute-start.5 = (f32[28,8,128]{2,1,0:T(8,128)S(1)}, f32[28,8,128]{2,1,0:T(8,128)S(1)}, u32[]{:S(2)}, u32[]{:S(2)}) collective-permute-start(f32[28,8,128]{2,1,0:T(8,128)S(1)} %get-tuple-element.42), channel_id=1, source_target_pairs={{0,4},{1,5},{2,6},{3,7},{4,0},{5,1},{6,2},{7,3},{8,12},{9,13},{10,... | collective-permute-start | bytes 344072 | tf_op jit(solution)/shard_map/ppermute | solution.py:549
  6.3 5.9 %collective-permute-start = (f32[28,8,128]{2,1,0:T(8,128)S(1)}, f32[28,8,128]{2,1,0:T(8,128)S(1)}, u32[]{:S(2)}, u32[]{:S(2)}) collective-permute-start(f32[28,8,128]{2,1,0:T(8,128)S(1)} %get-tuple-element.36), channel_id=1, source_target_pairs={{0,1},{1,0},{2,3},{3,2},{4,8},{5,9},{6,10},{7,11},{8,4},{9,5},{10,... | collective-permute-start | bytes 344072 | tf_op jit(solution)/shard_map/ppermute | solution.py:548
  6.5 5.7 %collective-permute-start.3 = (f32[8,128]{1,0:T(8,128)S(1)}, f32[8,128]{1,0:T(8,128)S(1)}, u32[]{:S(2)}, u32[]{:S(2)}) collective-permute-start(f32[8,128]{1,0:T(8,128)S(1)} %get-tuple-element.39), channel_id=1, source_target_pairs={{0,1},{1,0},{2,3},{3,2},{4,8},{5,9},{6,10},{7,11},{8,4},{9,5},{10,... | collective-permute-start | bytes 12296 | tf_op jit(solution)/shard_map/ppermute | solution.py:553
  7.0 5.2 %collective-permute-start.4 = (f32[8,128]{1,0:T(8,128)S(1)}, f32[8,128]{1,0:T(8,128)S(1)}, u32[]{:S(2)}, u32[]{:S(2)}) collective-permute-start(f32[8,128]{1,0:T(8,128)S(1)} %get-tuple-element.40), channel_id=1, source_target_pairs={{0,4},{1,5},{2,6},{3,7},{4,0},{5,1},{6,2},{7,3},{8,12},{9,13},{10,... | collective-permute-start | bytes 12296 | tf_op jit(solution)/shard_map/ppermute | solution.py:554
